TPU v7x, 512 devices: a whole 4x4x16 slice. The times are simulated.
512 devices in a mesh: feat: 128 (over x_hi, z, y), tok: 4 (over x_lo, core).
Axes of the slice: x: 4 (x_hi: 2, x_lo: 2; x = x_hi * 2 + x_lo), y: 4, z: 16, core: 2. Of those that a mesh axis runs over, the one named last changes fastest.
Arguments:
- layer_inputs: bfloat16 [3, 256, 4096], P(None, 'feat', 'tok'), may hold values from -6 to 6
- targets: bfloat16 [3, 256, 4096], P(None, 'feat', 'tok'), may hold values from -6 to 6
- winners: int32 [3, 256, 64], replicated, may hold values from 0 to 16383, all different within a row
- encoder_weight: bfloat16 [3, 4096, 16384], P(None, 'tok', 'feat'), may hold values from -0.09375 to 0.09375
- encoder_bias: float32 [3, 16384], P(None, 'feat'), may hold values from -3 to 3
- decoder_weight: bfloat16 [6, 16384, 4096], P(None, 'feat', 'tok'), may hold values from -0.75 to 0.75
- decoder_bias: float32 [3, 4096], P(None, 'tok'), may hold values from -3 to 3
Outputs:
- recon: bfloat16 [3, 256, 4096], P(None, 'feat', 'tok')
- encoder_grad: bfloat16 [3, 4096, 16384], P(None, 'tok', 'feat')
- encoder_bias_grad: float32 [3, 16384], P(None, 'feat')
- decoder_grad: bfloat16 [6, 16384, 4096], P(None, 'feat', 'tok')
- decoder_bias_grad: float32 [3, 4096], P(None, 'tok')
Inputs may be any that keep to these rules, and one draw needn't show every extreme that they name: For each layer and token the 64 winners are distinct; every feature number is a winner somewhere.
All inputs are finite; a program needn't handle non-finite values.
Results may differ from a plain program's by a relative error of at most 0.0062.
Values may be sent and summed in bfloat16 or wider, within the bound.
No kernel may reach another device: no remote copies, remote signals or barrier semaphores. Data moves between devices by JAX's collectives and lax.ppermute only.
A program may use at most 64 MiB of HBM per device.

v0:
```python
import jax
import jax.numpy as jnp
from jax import lax
from jax.sharding import PartitionSpec as P


def pair_number(source, target_layer, layers):
    return sum((layers - before for before in range(source))) + target_layer - source


def body(
    layer_inputs, targets, winners, encoder_weight, encoder_bias, decoder_weight, decoder_bias
):
    layers = layer_inputs.shape[0]
    width_here = encoder_weight.shape[2]
    picks = winners.shape[2]
    gathered = lax.all_gather(layer_inputs, "feat", axis=1, tiled=True)
    partial_pre = jnp.einsum(
        "ltd,ldf->ltf", gathered, encoder_weight, preferred_element_type=jnp.float32
    )
    pre_acts = lax.psum(partial_pre, "tok") + encoder_bias[:, None, :]
    feature_ids = lax.axis_index("feat") * width_here + jnp.arange(width_here, dtype=jnp.int32)
    chosen = jnp.zeros(pre_acts.shape, jnp.bool_)
    for offset in range(0, picks, 8):
        matches = winners[:, :, offset : offset + 8, None] == feature_ids
        chosen = jnp.logical_or(chosen, jnp.any(matches, axis=2))
    activation = jnp.where(chosen, pre_acts, 0.0).astype(jnp.bfloat16)
    decoded = []
    for target_layer in range(layers):
        partial_sum = None
        for source in range(target_layer + 1):
            product = jnp.dot(
                activation[source],
                decoder_weight[pair_number(source, target_layer, layers)],
                preferred_element_type=jnp.float32,
            )
            partial_sum = product if partial_sum is None else partial_sum + product
        decoded.append(partial_sum)
    decoded = jnp.stack(decoded)
    summed = (
        lax.psum_scatter(decoded, "feat", scatter_dimension=1, tiled=True)
        + decoder_bias[:, None, :]
    )
    recon = summed.astype(jnp.bfloat16)
    errors_home = (summed - targets.astype(jnp.float32)).astype(jnp.bfloat16)
    errors_all = lax.all_gather(errors_home, "feat", axis=1, tiled=True)
    partial_grad = []
    decoder_grads = [None] * decoder_weight.shape[0]
    for source in range(layers):
        grad_act = None
        for target_layer in range(source, layers):
            pair_slot = pair_number(source, target_layer, layers)
            product = lax.dot_general(
                errors_all[target_layer],
                decoder_weight[pair_slot],
                (((1,), (1,)), ((), ())),
                preferred_element_type=jnp.float32,
            )
            grad_act = product if grad_act is None else grad_act + product
            decoder_grads[pair_slot] = lax.dot_general(
                activation[source],
                errors_all[target_layer],
                (((0,), (0,)), ((), ())),
                preferred_element_type=jnp.float32,
            ).astype(jnp.bfloat16)
        partial_grad.append(grad_act)
    grad_act_all = lax.psum(jnp.stack(partial_grad), "tok")
    grad_pre = jnp.where(chosen, grad_act_all, 0.0).astype(jnp.bfloat16)
    encoder_grad = jnp.einsum(
        "ltd,ltf->ldf", gathered, grad_pre, preferred_element_type=jnp.float32
    ).astype(jnp.bfloat16)
    encoder_bias_grad = jnp.sum(grad_pre.astype(jnp.float32), axis=1)
    decoder_bias_grad = jnp.sum(errors_all.astype(jnp.float32), axis=1)
    return (recon, encoder_grad, encoder_bias_grad, jnp.stack(decoder_grads), decoder_bias_grad)


def solution(mesh):
    in_specs = (
        P(None, "feat", "tok"),
        P(None, "feat", "tok"),
        P(),
        P(None, "tok", "feat"),
        P(None, "feat"),
        P(None, "feat", "tok"),
        P(None, "tok"),
    )
    out_specs = (
        P(None, "feat", "tok"),
        P(None, "tok", "feat"),
        P(None, "feat"),
        P(None, "feat", "tok"),
        P(None, "tok"),
    )
    return jax.shard_map(body, mesh=mesh, in_specs=in_specs, out_specs=out_specs, check_vma=False)
```

profile of v0, /device:TPU:1, one launch (start us, length us, event | category | flops | bytes accessed | tf_op | source)
XLA Modules:
  0.0 1922.9 jit_solution(1679910102688351173)
XLA Ops:
  7.2 1.4 copy.61
  8.7 0.9 fusion.51
  9.9 0.9 copy.57
  10.9 0.9 copy.56
  11.8 0.9 copy.55
  12.7 0.9 copy.54
  13.6 0.9 copy.60
  14.5 0.9 copy.59
  15.4 207.0 %all-gather.3.cloned.1.call-done = bf16[3,256,1024]{2,0,1:T(4,128)(2,1)} async-done(((bf16[3,2,1024]{2,0,1:T(4,128)(2,1)}), bf16[3,256,1024]{2,0,1:T(4,128)(2,1)}) %all-gather.3.cloned.1.call-update) | async-done | bytes 1572880 | tf_op jit(solution)/shard_map/all_gather | solution.py:17
  222.4 3.4 fusion.18
  225.9 11.5 compare_reduce_fusion.6
  237.5 44.9 %all-reduce.5.cloned.1.call-done = f32[3,256,128]{2,1,0:T(8,128)} async-done(((f32[3,256,128]{2,1,0:T(8,128)}), f32[3,256,128]{2,1,0:T(8,128)}) %all-reduce.5.cloned.1.call-update) | async-done | bytes 393232 | tf_op jit(solution)/shard_map/psum | solution.py:21
  282.4 1.5 select_convert_fusion.1
  285.6 1.9 pad_maximum_fusion
  287.7 1.3 dynamic-slice
  289.6 1295.9 %all-reduce.7.cloned.1.call-done = f32[3,256,1024]{2,1,0:T(8,128)} async-done(((f32[3,256,1024]{2,1,0:T(8,128)}), f32[3,256,1024]{2,1,0:T(8,128)}) %all-reduce.7.cloned.1.call-update) | async-done | bytes 3145744
  1585.5 1.5 subtract_convert_fusion
  1587.0 0.6 copy.63
  1587.7 286.4 %all-gather.5.cloned.1.call-done = bf16[3,256,1024]{2,0,1:T(4,128)(2,1)} async-done(((bf16[3,2,1024]{2,0,1:T(4,128)(2,1)}), bf16[3,256,1024]{2,0,1:T(4,128)(2,1)}) %all-gather.5.cloned.1.call-update) | async-done | bytes 1572880 | tf_op jit(solution)/shard_map/all_gather | solution.py:46
  1874.0 5.9 fusion.50
  1880.3 1.0 fusion.4
  1881.3 0.4 copy_bitcast_fusion
  1883.2 22.2 %all-reduce.8 = bf16[3,256,128]{2,1,0:T(8,128)(2,1)S(1)} all-reduce(f32[3,256,128]{2,1,0:T(8,128)S(1)} %pad_maximum_fusion.1), channel_id=1, replica_groups=mesh['feat'=128,'tok'=4] {'tok'}, use_global_device_ids=true, to_apply=%region_10.11 | all-reduce | flops 98304 | bytes 589824 | tf_op jit(solution)/shard_map/psum | solution.py:67
  1905.5 0.7 convert_reduce_fusion.1
  1906.1 2.7 fusion.2
  1908.9 1.2 copy.69
  1910.0 1.0 fusion.6
  1911.0 1.0 fusion.8
  1912.0 1.0 fusion.10
  1912.9 1.0 fusion.12
  1913.9 1.0 fusion.14
  1914.8 1.5 convert_reduce_fusion
  (40 shorter events, 4.1 us)
Async XLA Ops:
  7.2 215.3 %copy-start = (bf16[3,1024,128]{2,1,0:T(8,128)(2,1)S(1)}, bf16[3,1024,128]{2,1,0:T(8,128)(2,1)}, u32[]{:S(2)}) copy-start(bf16[3,1024,128]{2,1,0:T(8,128)(2,1)} %param.10) | copy-start | bytes 2359300
  7.2 215.2 %all-gather.3.cloned.1.call-start = ((), (), s32[]{:S(2)}) async-start(), calls=%async_computation | async-start | bytes 2113536 | tf_op jit(solution)/shard_map/all_gather | solution.py:17
  8.6 273.8 %all-reduce.5.cloned.1.call-start = ((), (), s32[]{:S(2)}) async-start(), calls=%async_computation.1 | async-start | bytes 786432 | tf_op jit(solution)/shard_map/psum | solution.py:21
  225.8 56.5 %copy-start.7 = (f32[3,128]{1,0:T(4,128)S(1)}, f32[3,128]{1,0:T(4,128)}, u32[]{:S(2)}) copy-start(f32[3,128]{1,0:T(4,128)} %param.11) | copy-start | bytes 4612
  225.9 1359.7 %all-reduce.7.cloned.1.call-start = ((), (), s32[]{:S(2)}) async-start(), calls=%async_computation.3 | async-start | bytes 6291456
  225.9 58.0 %copy-start.2 = (bf16[6,128,1024]{2,1,0:T(8,128)(2,1)S(1)}, bf16[6,128,1024]{2,1,0:T(8,128)(2,1)}, u32[]{:S(2)}) copy-start(bf16[6,128,1024]{2,1,0:T(8,128)(2,1)} %param.12) | copy-start | bytes 4718596
  283.9 1596.4 %copy-start.3 = (bf16[3,256,128]{2,1,0:T(8,128)(2,1)}, bf16[3,256,128]{2,1,0:T(8,128)(2,1)S(1)}, u32[]{:S(2)}) copy-start(bf16[3,256,128]{2,1,0:T(8,128)(2,1)S(1)} %get-tuple-element.33) | copy-start | bytes 589828
  287.6 1297.9 %copy-start.5 = (f32[3,1024]{1,0:T(4,128)S(1)}, f32[3,1024]{1,0:T(4,128)}, u32[]{:S(2)}) copy-start(f32[3,1024]{1,0:T(4,128)} %param.13) | copy-start | bytes 36868
  287.6 1297.9 %copy-start.6 = (bf16[3,2,1024]{2,1,0:T(2,128)(2,1)S(1)}, bf16[3,2,1024]{2,1,0:T(2,128)(2,1)}, u32[]{:S(2)}) copy-start(bf16[3,2,1024]{2,1,0:T(2,128)(2,1)} %param.8) | copy-start | bytes 36868
  287.6 1586.4 %all-gather.5.cloned.1.call-start = ((), (), s32[]{:S(2)}) async-start(), calls=%async_computation.2 | async-start | bytes 2113536 | tf_op jit(solution)/shard_map/all_gather | solution.py:46
  1906.1 3.9 copy-start.4
  1911.0 3.8 copy-start.1
Sparse Core Ops, SparseCore 0:
  13.2 209.1 all-gather.2
  226.0 56.3 all-reduce.4
  287.7 1297.7 all-reduce.6
  1590.6 283.4 all-gather.4
where the time goes:
time: 1920 us
  waiting for transfers between devices  1830 us (95%)
  blocking collectives  22.2 us (1%)
    unnamed x5, waiting for transfers between devices  1300 us
    all_gather x1, waiting for transfers between devices, body(): errors_all = lax.all_gather(errors_home, 'feat', axis=1, tiled=True)  286 us
    all_gather x1, waiting for transfers between devices, body(): gathered = lax.all_gather(layer_inputs, 'feat', axis=1, tiled=True)  207 us
    psum x1, waiting for transfers between devices, body(): pre_acts = lax.psum(partial_pre, 'tok') + encoder_bias[:, None, :]  44.9 us
  transfers between devices with their start and end apart: 4, of which 4 were waited for; matrix products, arithmetic and copies ran while one was open for 1% of the time, Pallas kernels for 0%

commit v1 on v0

v1 whole, which is shorter than its diff:
```python
import jax
import jax.numpy as jnp
from jax import lax
from jax.sharding import Mesh, PartitionSpec as P

FEAT = ("xh", "z", "y")
TOK = ("xl", "core")
PLANE = ("xh", "y")
XH, Z, Y, XL, CORE = 2, 16, 4, 2, 2
bf16, f32 = jnp.bfloat16, jnp.float32


def pair_number(source, target_layer, layers):
    return sum((layers - before for before in range(source))) + target_layer - source


def swap(x, axis):
    return lax.ppermute(x, axis, [(0, 1), (1, 0)])


def gather_tokens(home):
    layers, rows, width = home.shape
    along_z = lax.all_to_all(
        jnp.broadcast_to(home[None], (Z, layers, rows, width)), "z", 0, 0
    )
    block = along_z.transpose(1, 0, 2, 3).reshape(1, layers, Z * rows, width)
    return lax.all_to_all(
        jnp.broadcast_to(block, (XH * Y,) + block.shape[1:]), PLANE, 0, 0
    )


def scatter_tokens(partial):
    planes, layers, rows, width = partial.shape
    got = lax.all_to_all(partial.astype(bf16), PLANE, 0, 0)
    summed = jnp.sum(got.astype(f32), axis=0).astype(bf16)
    blocks = summed.reshape(layers, Z, rows // Z, width).transpose(1, 0, 2, 3)
    got = lax.all_to_all(blocks, "z", 0, 0)
    return jnp.sum(got.astype(f32), axis=0)


def sum_tok(partial):
    both = partial + swap(partial, "core")
    mine = both.astype(bf16)
    return mine.astype(f32) + swap(mine, "xl").astype(f32)


def body(
    layer_inputs, targets, winners, encoder_weight, encoder_bias, decoder_weight, decoder_bias
):
    layers = layer_inputs.shape[0]
    width_here = encoder_weight.shape[2]
    picks = winners.shape[2]
    tokens = winners.shape[1]
    model = encoder_weight.shape[1]

    gathered = gather_tokens(layer_inputs)
    x = [gathered[:, l].reshape(tokens, model) for l in range(layers)]

    order = winners.reshape(layers, XH, Z, Y, 2, picks).transpose(0, 1, 3, 2, 4, 5)
    order = order.reshape(layers, tokens, picks)
    feature_ids = lax.axis_index(FEAT) * width_here + jnp.arange(width_here, dtype=jnp.int32)
    chosen = jnp.zeros((layers, tokens, width_here), jnp.bool_)
    for offset in range(0, picks, 8):
        matches = order[:, :, offset : offset + 8, None] == feature_ids
        chosen = jnp.logical_or(chosen, jnp.any(matches, axis=2))

    partial_pre = jnp.stack(
        [jnp.dot(x[l], encoder_weight[l], preferred_element_type=f32) for l in range(layers)]
    )
    pre_acts = sum_tok(partial_pre) + encoder_bias[:, None, :]
    activation = jnp.where(chosen, pre_acts, 0.0).astype(bf16)
    decoded = []
    for target_layer in range(layers):
        partial_sum = None
        for source in range(target_layer + 1):
            product = jnp.dot(
                activation[source],
                decoder_weight[pair_number(source, target_layer, layers)],
                preferred_element_type=f32,
            )
            partial_sum = product if partial_sum is None else partial_sum + product
        decoded.append(partial_sum.astype(bf16).reshape(XH * Y, tokens // (XH * Y), model))
    summed = scatter_tokens(jnp.stack(decoded, axis=1)) + decoder_bias[:, None, :]
    recon = summed.astype(bf16)
    errors_home = (summed - targets.astype(f32)).astype(bf16)
    errors_got = gather_tokens(errors_home)
    errors_all = [errors_got[:, l].reshape(tokens, model) for l in range(layers)]
    partial_grad = []
    decoder_grads = [None] * decoder_weight.shape[0]
    for source in range(layers):
        grad_act = None
        for target_layer in range(source, layers):
            pair_slot = pair_number(source, target_layer, layers)
            product = lax.dot_general(
                errors_all[target_layer],
                decoder_weight[pair_slot],
                (((1,), (1,)), ((), ())),
                preferred_element_type=f32,
            )
            grad_act = product if grad_act is None else grad_act + product
            decoder_grads[pair_slot] = lax.dot_general(
                activation[source],
                errors_all[target_layer],
                (((0,), (0,)), ((), ())),
                preferred_element_type=f32,
            ).astype(bf16)
        partial_grad.append(grad_act)
    grad_act_all = sum_tok(jnp.stack(partial_grad))
    grad_pre = jnp.where(chosen, grad_act_all, 0.0).astype(bf16)
    encoder_grad = jnp.stack(
        [
            lax.dot_general(
                x[l], grad_pre[l], (((0,), (0,)), ((), ())), preferred_element_type=f32
            ).astype(bf16)
            for l in range(layers)
        ]
    )
    encoder_bias_grad = jnp.sum(grad_pre.astype(f32), axis=1)
    decoder_bias_grad = jnp.sum(errors_got.astype(f32), axis=(0, 2))
    return (recon, encoder_grad, encoder_bias_grad, jnp.stack(decoder_grads), decoder_bias_grad)


def solution(mesh):
    fine = Mesh(mesh.devices.reshape(XH, Z, Y, XL, CORE), FEAT + TOK)
    in_specs = (
        P(None, FEAT, TOK),
        P(None, FEAT, TOK),
        P(),
        P(None, TOK, FEAT),
        P(None, FEAT),
        P(None, FEAT, TOK),
        P(None, TOK),
    )
    out_specs = (
        P(None, FEAT, TOK),
        P(None, TOK, FEAT),
        P(None, FEAT),
        P(None, FEAT, TOK),
        P(None, TOK),
    )
    return jax.shard_map(body, mesh=fine, in_specs=in_specs, out_specs=out_specs, check_vma=False)
```

time: 1920 us -> 196 us (0.10)
  waiting for transfers between devices: 1830 us -> 20.1 us
  blocking collectives: 22.2 us -> 113 us
  starting transfers between devices: 0.16 us -> 29.5 us
    unnamed x5 -> x0, waiting for transfers between devices: 1300 us -> none
    all_gather x2 -> x0, waiting for transfers between devices: 493 us -> none  [the longest x1 286 us: body(): errors_all = lax.all_gather(errors_home, 'feat', axis=1, tiled=True)]
    all_to_all x0 -> x5, blocking collectives: none -> 113 us  [the longest x2 47.4 us: gather_tokens(): lax.all_to_all(jnp.broadcast_to(home[None], (Z, layers, rows, width)), 'z...]
    psum x1 -> x0, waiting for transfers between devices: 44.9 us -> none  [body(): pre_acts = lax.psum(partial_pre, 'tok') + encoder_bias[:, None, :]]
    ppermute x0 -> x4, starting transfers between devices: none -> 22.7 us  [swap(): return lax.ppermute(x, axis, [(0, 1), (1, 0)])]
    psum x1 -> x0, blocking collectives: 22.2 us -> none  [body(): grad_act_all = lax.psum(jnp.stack(partial_grad), 'tok')]
  transfers between devices with their start and end apart: 4 -> 5, of which waited for: 4 -> 3; matrix products, arithmetic and copies ran while one was open for 1% -> 8% of each run, Pallas kernels for 0% -> 0%
where the time goes in v1:
time: 196 us
  blocking collectives  113 us (58%)
  starting transfers between devices  29.5 us (15%)
  waiting for transfers between devices  20.1 us (10%)
  other arithmetic  14.3 us (7%)
  matrix products  10.9 us (6%)
  local copies, waits for them, and re-layouts  6.37 us (3%)
    all_to_all x2, blocking collectives, gather_tokens(): lax.all_to_all(jnp.broadcast_to(home[None], (Z, layers, rows, width)), 'z...  47.4 us
    all_to_all x1, blocking collectives, scatter_tokens(): got = lax.all_to_all(partial.astype(bf16), PLANE, 0, 0)  25.5 us
    ppermute x4, starting transfers between devices, swap(): return lax.ppermute(x, axis, [(0, 1), (1, 0)])  22.7 us
    all_to_all x1, blocking collectives, scatter_tokens(): got = lax.all_to_all(blocks, 'z', 0, 0)  21 us
    all_to_all x1, blocking collectives, gather_tokens(): lax.all_to_all(jnp.broadcast_to(block, (XH * Y,) + block.shape[1:]), PLAN...  19.6 us
    all_to_all x1, waiting for transfers between devices, gather_tokens(): lax.all_to_all(jnp.broadcast_to(block, (XH * Y,) + block.shape[1:]), PLAN...  15 us
    reduce_or x1, other arithmetic, body(): chosen = jnp.logical_or(chosen, jnp.any(matches, axis=2))  9.5 us
    all_to_all x1, starting transfers between devices, gather_tokens(): lax.all_to_all(jnp.broadcast_to(block, (XH * Y,) + block.shape[1:]), PLAN...  6.78 us
  transfers between devices with their start and end apart: 5, of which 3 were waited for; matrix products, arithmetic and copies ran while one was open for 8% of the time, Pallas kernels for 0%

profile of v1, /device:TPU:1, one launch (start us, length us, event | category | flops | bytes accessed | tf_op | source)
XLA Modules:
  0.0 195.6 jit_solution(5449175856061842752)
XLA Ops:
  0.6 0.8 broadcast_in_dim.16
  1.4 28.1 %all_to_all.30 = bf16[16,3,2,1024]{3,2,1,0:T(2,128)(2,1)S(1)} all-to-all(bf16[16,3,2,1024]{3,2,1,0:T(2,128)(2,1)S(1)} %broadcast_in_dim.16), channel_id=1, replica_groups=mesh['xh'=2,'z'=16,'y'=4,'xl'=2,'core'=2] {'z'}, dimensions={0} | all-to-all | bytes 393216 | tf_op jit(solution)/shard_map/all_to_all | solution.py:23
  29.8 1.3 broadcast_in_dim.18
  31.1 6.8 %all-to-all-start.1 = ((bf16[8,3,32,1024]{3,2,1,0:T(8,128)(2,1)}), bf16[8,3,32,1024]{3,2,1,0:T(8,128)(2,1)S(1)}, u32[]{:S(2)}, u32[]{:S(2)}) async-start(bf16[8,3,32,1024]{3,2,1,0:T(8,128)(2,1)} %broadcast_in_dim.18), calls=%async_computation.1 | async-start | bytes 3145728 | tf_op jit(solution)/shard_map/all_to_all | solution.py:27
  38.3 15.0 %all-to-all-done.1 = bf16[8,3,32,1024]{3,2,1,0:T(8,128)(2,1)S(1)} async-done(((bf16[8,3,32,1024]{3,2,1,0:T(8,128)(2,1)}), bf16[8,3,32,1024]{3,2,1,0:T(8,128)(2,1)S(1)}, u32[]{:S(2)}, u32[]{:S(2)}) %all-to-all-start.1) | async-done | bytes 1572896 | tf_op jit(solution)/shard_map/all_to_all | solution.py:27
  54.6 8.5 %collective-permute-start = (f32[3,256,128]{2,1,0:T(8,128)S(1)}, f32[3,256,128]{2,1,0:T(8,128)S(1)}, u32[]{:S(2)}, u32[]{:S(2)}) collective-permute-start(f32[3,256,128]{2,1,0:T(8,128)S(1)} %pad_maximum_fusion.2), channel_id=1, source_target_pairs={{0,1},{1,0},{2,3},{3,2},{4,5},{5,4},{6,7},{7,6},{8,9},{9,8},{10,11... | collective-permute-start | bytes 1179656 | tf_op jit(solution)/shard_map/ppermute | solution.py:18
  63.1 0.8 fusion.55
  63.9 0.5 collective-permute-done
  64.5 2.6 %collective-permute-start.1 = (bf16[3,256,128]{2,1,0:T(8,128)(2,1)S(1)}, bf16[3,256,128]{2,1,0:T(8,128)(2,1)S(1)}, u32[]{:S(2)}, u32[]{:S(2)}) collective-permute-start(bf16[3,256,128]{2,1,0:T(8,128)(2,1)S(1)} %add_convert_fusion.1), channel_id=1, source_target_pairs={{0,2},{2,0},{1,3},{3,1},{4,6},{6,4},{5,7},{7,5},{8,10},{10,8},{9,1... | collective-permute-start | bytes 589832 | tf_op jit(solution)/shard_map/ppermute | solution.py:18
  67.1 9.5 %compare_reduce_fusion.6 = (pred[3,256,128]{2,1,0:T(8,128)(4,1)S(1)}, pred[3,256,128]{2,1,0:T(8,128)(4,1)S(1)}, pred[3,256,128]{2,1,0:T(8,128)(4,1)S(1)}, pred[3...) fusion(s32[3,256,8]{2,1,0:T(8,128)S(1)} %get-tuple-element.55, ...), kind=kLoop, calls=%fused_computation.7 | loop fusion | flops 11796480 | bytes 983552 | tf_op jit(solution)/shard_map/reduce_or | solution.py:65
  76.6 1.0 select_convert_fusion.1
  77.6 0.4 copy-done
  80.0 25.5 %all_to_all.31 = bf16[8,3,32,1024]{3,2,1,0:T(8,128)(2,1)S(1)} all-to-all(bf16[8,3,32,1024]{3,2,1,0:T(8,128)(2,1)S(1)} %pad_maximum_fusion), channel_id=1, replica_groups=mesh['xh'=2,'z'=16,'y'=4,'xl'=2,'core'=2] {'xh','y'}, dimensions={0} | all-to-all | bytes 3145728 | tf_op jit(solution)/shard_map/all_to_all | solution.py:34
  106.0 21.0 %all_to_all.32 = bf16[16,3,2,1024]{3,2,1,0:T(2,128)(2,1)S(1)} all-to-all(bf16[16,3,2,1024]{3,2,1,0:T(2,128)(2,1)S(1)} %copy.39), channel_id=1, replica_groups=mesh['xh'=2,'z'=16,'y'=4,'xl'=2,'core'=2] {'z'}, dimensions={0} | all-to-all | bytes 393216 | tf_op jit(solution)/shard_map/all_to_all | solution.py:37
  127.1 1.3 subtract_convert_fusion
  128.5 19.3 %all_to_all.33 = bf16[16,3,2,1024]{3,2,1,0:T(2,128)(2,1)S(1)} all-to-all(bf16[16,3,2,1024]{3,2,1,0:T(2,128)(2,1)S(1)} %broadcast_in_dim.20), channel_id=1, replica_groups=mesh['xh'=2,'z'=16,'y'=4,'xl'=2,'core'=2] {'z'}, dimensions={0} | all-to-all | bytes 393216 | tf_op jit(solution)/shard_map/all_to_all | solution.py:23
  148.2 19.6 %all_to_all.34 = bf16[8,3,32,1024]{3,2,1,0:T(8,128)(2,1)S(1)} all-to-all(bf16[8,3,32,1024]{3,2,1,0:T(8,128)(2,1)S(1)} %broadcast_in_dim.22), channel_id=1, replica_groups=mesh['xh'=2,'z'=16,'y'=4,'xl'=2,'core'=2] {'xh','y'}, dimensions={0} | all-to-all | bytes 3145728 | tf_op jit(solution)/shard_map/all_to_all | solution.py:27
  168.0 0.3 fusion.32
  168.3 1.0 fusion.6
  169.3 0.3 convolution_bitcast_fusion
  169.6 0.3 fusion.26
  170.9 9.6 %collective-permute-start.2 = (f32[3,256,128]{2,1,0:T(8,128)S(1)}, f32[3,256,128]{2,1,0:T(8,128)S(1)}, u32[]{:S(2)}, u32[]{:S(2)}) collective-permute-start(f32[3,256,128]{2,1,0:T(8,128)S(1)} %pad_maximum_fusion.3), channel_id=1, source_target_pairs={{0,1},{1,0},{2,3},{3,2},{4,5},{5,4},{6,7},{7,6},{8,9},{9,8},{10,11... | collective-permute-start | bytes 1179656 | tf_op jit(solution)/shard_map/ppermute | solution.py:18
  180.5 1.0 fusion.8
  181.5 1.0 fusion.10
  182.4 1.0 fusion.12
  183.4 1.0 fusion.14
  184.4 2.0 collective-permute-start.3
  186.4 1.0 fusion.16
  187.3 0.9 convert_reduce_fusion
  188.3 4.6 %collective-permute-done.3 = bf16[3,256,128]{2,1,0:T(8,128)(2,1)S(1)} collective-permute-done((bf16[3,256,128]{2,1,0:T(8,128)(2,1)S(1)}, bf16[3,256,128]{2,1,0:T(8,128)(2,1)S(1)}, u32[]{:S(2)}, u32[]{:S(2)}) %collective-permute-start.3) | collective-permute-done | bytes 196640 | tf_op jit(solution)/shard_map/ppermute | solution.py:18
  192.8 0.7 convert_reduce_fusion.1
  194.4 1.2 copy.41
  (61 shorter events, 6.9 us)
Async XLA Ops:
  31.1 6.8 %copy-start.9 = (s32[3,256,64]{1,2,0:T(8,128)S(1)}, s32[3,256,64]{1,2,0:T(8,128)}, u32[]{:S(2)}) copy-start(s32[3,256,64]{1,2,0:T(8,128)} %param.9) | copy-start | bytes 589828
  31.1 22.2 %all-to-all-start.1 = ((bf16[8,3,32,1024]{3,2,1,0:T(8,128)(2,1)}), bf16[8,3,32,1024]{3,2,1,0:T(8,128)(2,1)S(1)}, u32[]{:S(2)}, u32[]{:S(2)}) async-start(bf16[8,3,32,1024]{3,2,1,0:T(8,128)(2,1)} %broadcast_in_dim.18), calls=%async_computation.1 | async-start | bytes 3145728 | tf_op jit(solution)/shard_map/all_to_all | solution.py:27
  38.3 15.2 %copy-start.7 = (bf16[3,1024,128]{2,1,0:T(8,128)(2,1)S(1)}, bf16[3,1024,128]{2,1,0:T(8,128)(2,1)}, u32[]{:S(2)}) copy-start(bf16[3,1024,128]{2,1,0:T(8,128)(2,1)} %param.10) | copy-start | bytes 2359300
  53.4 1.0 copy-start.1
  53.4 1.0 copy-start.3
  53.4 1.1 copy-start.5
  54.6 9.9 %collective-permute-start = (f32[3,256,128]{2,1,0:T(8,128)S(1)}, f32[3,256,128]{2,1,0:T(8,128)S(1)}, u32[]{:S(2)}, u32[]{:S(2)}) collective-permute-start(f32[3,256,128]{2,1,0:T(8,128)S(1)} %pad_maximum_fusion.2), channel_id=1, source_target_pairs={{0,1},{1,0},{2,3},{3,2},{4,5},{5,4},{6,7},{7,6},{8,9},{9,8},{10,11... | collective-permute-start | bytes 1179656 | tf_op jit(solution)/shard_map/ppermute | solution.py:18
  64.5 12.1 %collective-permute-start.1 = (bf16[3,256,128]{2,1,0:T(8,128)(2,1)S(1)}, bf16[3,256,128]{2,1,0:T(8,128)(2,1)S(1)}, u32[]{:S(2)}, u32[]{:S(2)}) collective-permute-start(bf16[3,256,128]{2,1,0:T(8,128)(2,1)S(1)} %add_convert_fusion.1), channel_id=1, source_target_pairs={{0,2},{2,0},{1,3},{3,1},{4,6},{6,4},{5,7},{7,5},{8,10},{10,8},{9,1... | collective-permute-start | bytes 589832 | tf_op jit(solution)/shard_map/ppermute | solution.py:18
  67.1 9.5 %copy-start.11 = (f32[3,128]{1,0:T(4,128)S(1)}, f32[3,128]{1,0:T(4,128)}, u32[]{:S(2)}) copy-start(f32[3,128]{1,0:T(4,128)} %param.11) | copy-start | bytes 4612
  76.6 1.4 copy-start
  105.4 21.6 %copy-start.10 = (f32[3,1024]{1,0:T(4,128)S(1)}, f32[3,1024]{1,0:T(4,128)}, u32[]{:S(2)}) copy-start(f32[3,1024]{1,0:T(4,128)} %param.13) | copy-start | bytes 36868
  170.9 13.5 %collective-permute-start.2 = (f32[3,256,128]{2,1,0:T(8,128)S(1)}, f32[3,256,128]{2,1,0:T(8,128)S(1)}, u32[]{:S(2)}, u32[]{:S(2)}) collective-permute-start(f32[3,256,128]{2,1,0:T(8,128)S(1)} %pad_maximum_fusion.3), channel_id=1, source_target_pairs={{0,1},{1,0},{2,3},{3,2},{4,5},{5,4},{6,7},{7,6},{8,9},{9,8},{10,11... | collective-permute-start | bytes 1179656 | tf_op jit(solution)/shard_map/ppermute | solution.py:18
  184.4 8.5 %copy-start.8 = (pred[3,256,128]{2,1,0:T(8,128)(4,1)S(1)}, pred[3,256,128]{2,1,0:T(8,128)(4,1)}, u32[]{:S(2)}) copy-start(pred[3,256,128]{2,1,0:T(8,128)(4,1)} %get-tuple-element.41) | copy-start | bytes 294916
  184.4 8.4 %collective-permute-start.3 = (bf16[3,256,128]{2,1,0:T(8,128)(2,1)S(1)}, bf16[3,256,128]{2,1,0:T(8,128)(2,1)S(1)}, u32[]{:S(2)}, u32[]{:S(2)}) collective-permute-start(bf16[3,256,128]{2,1,0:T(8,128)(2,1)S(1)} %add_convert_fusion), channel_id=1, source_target_pairs={{0,2},{2,0},{1,3},{3,1},{4,6},{6,4},{5,7},{7,5},{8,10},{10,8},{9,1... | collective-permute-start | bytes 589832 | tf_op jit(solution)/shard_map/ppermute | solution.py:18
  187.3 6.2 %copy-start.6 = (bf16[8,1,32,1024]{3,2,1,0:T(8,128)(2,1)S(1)}, bf16[8,1,32,1024]{3,2,1,0:T(8,128)(2,1)}, u32[]{:S(2)}) copy-start(bf16[8,1,32,1024]{3,2,1,0:T(8,128)(2,1)} %copy-done.5) | copy-start | bytes 1572868
  187.3 6.4 %copy-start.4 = (bf16[8,1,32,1024]{3,2,1,0:T(8,128)(2,1)S(1)}, bf16[8,1,32,1024]{3,2,1,0:T(8,128)(2,1)}, u32[]{:S(2)}) copy-start(bf16[8,1,32,1024]{3,2,1,0:T(8,128)(2,1)} %copy-done.3) | copy-start | bytes 1572868
  188.3 5.8 %copy-start.2 = (bf16[8,1,32,1024]{3,2,1,0:T(8,128)(2,1)S(1)}, bf16[8,1,32,1024]{3,2,1,0:T(8,128)(2,1)}, u32[]{:S(2)}) copy-start(bf16[8,1,32,1024]{3,2,1,0:T(8,128)(2,1)} %copy-done.1) | copy-start | bytes 1572868

commit v2 on v1

--- a/solution.py
+++ b/solution.py
@@ -18,11 +18,13 @@
     return lax.ppermute(x, axis, [(0, 1), (1, 0)])
 
 
-def gather_tokens(home):
+def gather_z(home):
     layers, rows, width = home.shape
-    along_z = lax.all_to_all(
-        jnp.broadcast_to(home[None], (Z, layers, rows, width)), "z", 0, 0
-    )
+    return lax.all_to_all(jnp.broadcast_to(home[None], (Z, layers, rows, width)), "z", 0, 0)
+
+
+def gather_plane(along_z):
+    _, layers, rows, width = along_z.shape
     block = along_z.transpose(1, 0, 2, 3).reshape(1, layers, Z * rows, width)
     return lax.all_to_all(
         jnp.broadcast_to(block, (XH * Y,) + block.shape[1:]), PLANE, 0, 0
@@ -53,7 +55,8 @@
     tokens = winners.shape[1]
     model = encoder_weight.shape[1]
 
-    gathered = gather_tokens(layer_inputs)
+    along_z, winners = lax.optimization_barrier((gather_z(layer_inputs), winners))
+    gathered = gather_plane(along_z)
     x = [gathered[:, l].reshape(tokens, model) for l in range(layers)]
 
     order = winners.reshape(layers, XH, Z, Y, 2, picks).transpose(0, 1, 3, 2, 4, 5)
@@ -67,6 +70,7 @@
     partial_pre = jnp.stack(
         [jnp.dot(x[l], encoder_weight[l], preferred_element_type=f32) for l in range(layers)]
     )
+    partial_pre, chosen = lax.optimization_barrier((partial_pre, chosen))
     pre_acts = sum_tok(partial_pre) + encoder_bias[:, None, :]
     activation = jnp.where(chosen, pre_acts, 0.0).astype(bf16)
     decoded = []
@@ -83,29 +87,35 @@
     summed = scatter_tokens(jnp.stack(decoded, axis=1)) + decoder_bias[:, None, :]
     recon = summed.astype(bf16)
     errors_home = (summed - targets.astype(f32)).astype(bf16)
-    errors_got = gather_tokens(errors_home)
+    errors_got = gather_plane(gather_z(errors_home))
     errors_all = [errors_got[:, l].reshape(tokens, model) for l in range(layers)]
     partial_grad = []
-    decoder_grads = [None] * decoder_weight.shape[0]
     for source in range(layers):
         grad_act = None
         for target_layer in range(source, layers):
-            pair_slot = pair_number(source, target_layer, layers)
             product = lax.dot_general(
                 errors_all[target_layer],
-                decoder_weight[pair_slot],
+                decoder_weight[pair_number(source, target_layer, layers)],
                 (((1,), (1,)), ((), ())),
                 preferred_element_type=f32,
             )
             grad_act = product if grad_act is None else grad_act + product
-            decoder_grads[pair_slot] = lax.dot_general(
-                activation[source],
-                errors_all[target_layer],
-                (((0,), (0,)), ((), ())),
-                preferred_element_type=f32,
-            ).astype(bf16)
         partial_grad.append(grad_act)
-    grad_act_all = sum_tok(jnp.stack(partial_grad))
+    partial_grad = jnp.stack(partial_grad)
+    both, errors_got = lax.optimization_barrier((swap(partial_grad, "core"), errors_got))
+    both = (partial_grad + both).astype(bf16)
+    errors_all = [errors_got[:, l].reshape(tokens, model) for l in range(layers)]
+    decoder_grads = [
+        lax.dot_general(
+            activation[source],
+            errors_all[target_layer],
+            (((0,), (0,)), ((), ())),
+            preferred_element_type=f32,
+        ).astype(bf16)
+        for source in range(layers)
+        for target_layer in range(source, layers)
+    ]
+    grad_act_all = both.astype(f32) + swap(both, "xl").astype(f32)
     grad_pre = jnp.where(chosen, grad_act_all, 0.0).astype(bf16)
     encoder_grad = jnp.stack(
         [

time: 196 us -> 191 us (0.974)
  blocking collectives: 113 us -> 84.8 us
  starting transfers between devices: 29.5 us -> 45.4 us
  waiting for transfers between devices: 20.1 us -> 28.7 us
  matrix products: 10.9 us -> 8.04 us
    all_to_all x3 -> x2, blocking collectives: 66.9 us -> 39.5 us  [the longest x1 21.3 us: gather_plane(): lax.all_to_all(jnp.broadcast_to(block, (XH * Y,) + block.shape[1:]), PLAN...]
    all_to_all x1 -> x2, starting transfers between devices: 6.78 us -> 22.4 us  [the longest x1 15.7 us: gather_z(): lax.all_to_all(jnp.broadcast_to(home[None], (Z, layers, rows, width)), 'z...]
    ppermute x4, waiting for transfers between devices: 5.1 us -> 11.3 us  [swap(): return lax.ppermute(x, axis, [(0, 1), (1, 0)])]
    dot_general x6, matrix products: 5.77 us -> 1.51 us  [body(): lax.dot_general(activation[source], errors_all[target_layer], (((0,), (0,...]
    all_to_all x1 -> x2, waiting for transfers between devices: 15 us -> 17.4 us  [the longest x1 12.5 us: gather_z(): lax.all_to_all(jnp.broadcast_to(home[None], (Z, layers, rows, width)), 'z...]
  transfers between devices with their start and end apart: 5 -> 6, of which waited for: 3 -> 6; matrix products, arithmetic and copies ran while one was open for 8% -> 7% of each run, Pallas kernels for 0% -> 0%
where the time goes in v2:
time: 191 us; the launch traced here: 190 us
  blocking collectives  84.8 us (44%)
  starting transfers between devices  45.4 us (24%)
  waiting for transfers between devices  28.7 us (15%)
  other arithmetic  14.5 us (8%)
  matrix products  8.04 us (4%)
  local copies, waits for them, and re-layouts  7.31 us (4%)
    all_to_all x1, blocking collectives, scatter_tokens(): got = lax.all_to_all(partial.astype(bf16), PLANE, 0, 0)  24.4 us
    ppermute x4, starting transfers between devices, swap(): return lax.ppermute(x, axis, [(0, 1), (1, 0)])  23 us
    all_to_all x1, blocking collectives, gather_plane(): lax.all_to_all(jnp.broadcast_to(block, (XH * Y,) + block.shape[1:]), PLAN...  21.3 us
    all_to_all x1, blocking collectives, scatter_tokens(): got = lax.all_to_all(blocks, 'z', 0, 0)  20.9 us
    all_to_all x1, blocking collectives, gather_z(): lax.all_to_all(jnp.broadcast_to(home[None], (Z, layers, rows, width)), 'z...  18.2 us
    all_to_all x1, starting transfers between devices, gather_z(): lax.all_to_all(jnp.broadcast_to(home[None], (Z, layers, rows, width)), 'z...  15.7 us
    all_to_all x1, waiting for transfers between devices, gather_z(): lax.all_to_all(jnp.broadcast_to(home[None], (Z, layers, rows, width)), 'z...  12.5 us
    ppermute x4, waiting for transfers between devices, swap(): return lax.ppermute(x, axis, [(0, 1), (1, 0)])  11.3 us
  transfers between devices with their start and end apart: 6, of which 6 were waited for; matrix products, arithmetic and copies ran while one was open for 7% of the time, Pallas kernels for 0%

profile of v2, /device:TPU:1, one launch (start us, length us, event | category | flops | bytes accessed | tf_op | source)
XLA Modules:
  0.0 189.9 jit_solution(12395695393592526645)
XLA Ops:
  0.6 1.5 broadcast_in_dim.16
  2.1 15.7 %all-to-all-start = ((bf16[16,3,2,1024]{3,2,1,0:T(2,128)(2,1)}), bf16[16,3,2,1024]{3,2,1,0:T(2,128)(2,1)S(1)}, u32[]{:S(2)}, u32[]{:S(2)}) async-start(bf16[16,3,2,1024]{3,2,1,0:T(2,128)(2,1)} %broadcast_in_dim.16), calls=%async_computation | async-start | bytes 393216 | tf_op jit(solution)/shard_map/all_to_all | solution.py:23
  17.9 12.5 %all-to-all-done = bf16[16,3,2,1024]{3,2,1,0:T(2,128)(2,1)S(1)} async-done(((bf16[16,3,2,1024]{3,2,1,0:T(2,128)(2,1)}), bf16[16,3,2,1024]{3,2,1,0:T(2,128)(2,1)S(1)}, u32[]{:S(2)}, u32[]{:S(2)}) %all-to-all-start) | async-done | bytes 196640 | tf_op jit(solution)/shard_map/all_to_all | solution.py:23
  30.6 1.1 copy.30
  31.9 1.3 broadcast_in_dim.18
  33.3 6.7 %all-to-all-start.1 = ((bf16[8,3,32,1024]{3,2,1,0:T(8,128)(2,1)}), bf16[8,3,32,1024]{3,2,1,0:T(8,128)(2,1)S(1)}, u32[]{:S(2)}, u32[]{:S(2)}) async-start(bf16[8,3,32,1024]{3,2,1,0:T(8,128)(2,1)} %broadcast_in_dim.18), calls=%async_computation.1 | async-start | bytes 3145728 | tf_op jit(solution)/shard_map/all_to_all | solution.py:29
  39.9 0.8 fusion.56
  40.7 9.5 %compare_reduce_fusion.6 = (pred[3,256,128]{2,1,0:T(8,128)(4,1)S(1)}, pred[3,256,128]{2,1,0:T(8,128)(4,1)S(1)}, pred[3,256,128]{2,1,0:T(8,128)(4,1)S(1)}, pred[3...) fusion(s32[3,256,8]{2,1,0:T(8,128)S(1)} %get-tuple-element.43, ...), kind=kLoop, calls=%fused_computation.7 | loop fusion | flops 11796480 | bytes 983552 | tf_op jit(solution)/shard_map/reduce_or | solution.py:68
  50.5 4.8 %all-to-all-done.1 = bf16[8,3,32,1024]{3,2,1,0:T(8,128)(2,1)S(1)} async-done(((bf16[8,3,32,1024]{3,2,1,0:T(8,128)(2,1)}), bf16[8,3,32,1024]{3,2,1,0:T(8,128)(2,1)S(1)}, u32[]{:S(2)}, u32[]{:S(2)}) %all-to-all-start.1) | async-done | bytes 1572896 | tf_op jit(solution)/shard_map/all_to_all | solution.py:29
  56.1 1.4 convolution_bitcast_fusion.2
  57.5 8.5 %collective-permute-start = (f32[3,256,128]{2,1,0:T(8,128)S(1)}, f32[3,256,128]{2,1,0:T(8,128)S(1)}, u32[]{:S(2)}, u32[]{:S(2)}) collective-permute-start(f32[3,256,128]{2,1,0:T(8,128)S(1)} %pad_maximum_fusion.2), channel_id=1, source_target_pairs={{0,1},{1,0},{2,3},{3,2},{4,5},{5,4},{6,7},{7,6},{8,9},{9,8},{10,11... | collective-permute-start | bytes 1179656 | tf_op jit(solution)/shard_map/ppermute | solution.py:18
  66.1 1.3 collective-permute-done
  67.5 2.6 %collective-permute-start.1 = (bf16[3,256,128]{2,1,0:T(8,128)(2,1)S(1)}, bf16[3,256,128]{2,1,0:T(8,128)(2,1)S(1)}, u32[]{:S(2)}, u32[]{:S(2)}) collective-permute-start(bf16[3,256,128]{2,1,0:T(8,128)(2,1)S(1)} %add_convert_fusion.1), channel_id=1, source_target_pairs={{0,2},{2,0},{1,3},{3,1},{4,6},{6,4},{5,7},{7,5},{8,10},{10,8},{9,1... | collective-permute-start | bytes 589832 | tf_op jit(solution)/shard_map/ppermute | solution.py:18
  70.1 5.4 %collective-permute-done.1 = bf16[3,256,128]{2,1,0:T(8,128)(2,1)S(1)} collective-permute-done((bf16[3,256,128]{2,1,0:T(8,128)(2,1)S(1)}, bf16[3,256,128]{2,1,0:T(8,128)(2,1)S(1)}, u32[]{:S(2)}, u32[]{:S(2)}) %collective-permute-start.1) | collective-permute-done | bytes 196640 | tf_op jit(solution)/shard_map/ppermute | solution.py:18
  77.5 24.4 %all_to_all.30 = bf16[8,3,32,1024]{3,2,1,0:T(8,128)(2,1)S(1)} all-to-all(bf16[8,3,32,1024]{3,2,1,0:T(8,128)(2,1)S(1)} %pad_maximum_fusion), channel_id=1, replica_groups=mesh['xh'=2,'z'=16,'y'=4,'xl'=2,'core'=2] {'xh','y'}, dimensions={0} | all-to-all | bytes 3145728 | tf_op jit(solution)/shard_map/all_to_all | solution.py:36
  101.9 1.0 reduce_sum.39
  102.9 1.0 reshape.41
  104.1 20.9 %all_to_all.31 = bf16[16,3,2,1024]{3,2,1,0:T(2,128)(2,1)S(1)} all-to-all(bf16[16,3,2,1024]{3,2,1,0:T(2,128)(2,1)S(1)} %copy.35), channel_id=1, replica_groups=mesh['xh'=2,'z'=16,'y'=4,'xl'=2,'core'=2] {'z'}, dimensions={0} | all-to-all | bytes 393216 | tf_op jit(solution)/shard_map/all_to_all | solution.py:39
  125.2 0.6 subtract_convert_fusion
  125.9 18.2 %all_to_all.32 = bf16[16,3,2,1024]{3,2,1,0:T(2,128)(2,1)S(1)} all-to-all(bf16[16,3,2,1024]{3,2,1,0:T(2,128)(2,1)S(1)} %broadcast_in_dim.20), channel_id=1, replica_groups=mesh['xh'=2,'z'=16,'y'=4,'xl'=2,'core'=2] {'z'}, dimensions={0} | all-to-all | bytes 393216 | tf_op jit(solution)/shard_map/all_to_all | solution.py:23
  144.5 21.3 %all_to_all.33 = bf16[8,3,32,1024]{3,2,1,0:T(8,128)(2,1)S(1)} all-to-all(bf16[8,3,32,1024]{3,2,1,0:T(8,128)(2,1)S(1)} %broadcast_in_dim.22), channel_id=1, replica_groups=mesh['xh'=2,'z'=16,'y'=4,'xl'=2,'core'=2] {'xh','y'}, dimensions={0} | all-to-all | bytes 3145728 | tf_op jit(solution)/shard_map/all_to_all | solution.py:29
  166.0 0.3 fusion.32
  167.9 9.6 %collective-permute-start.2 = (f32[3,256,128]{2,1,0:T(8,128)S(1)}, f32[3,256,128]{2,1,0:T(8,128)S(1)}, u32[]{:S(2)}, u32[]{:S(2)}) collective-permute-start(f32[3,256,128]{2,1,0:T(8,128)S(1)} %pad_maximum_fusion.3), channel_id=1, source_target_pairs={{0,1},{1,0},{2,3},{3,2},{4,5},{5,4},{6,7},{7,6},{8,9},{9,8},{10,11... | collective-permute-start | bytes 1179656 | tf_op jit(solution)/shard_map/ppermute | solution.py:18
  177.5 1.3 collective-permute-done.2
  179.1 2.2 %collective-permute-start.3 = (bf16[3,256,128]{2,1,0:T(8,128)(2,1)S(1)}, bf16[3,256,128]{2,1,0:T(8,128)(2,1)S(1)}, u32[]{:S(2)}, u32[]{:S(2)}) collective-permute-start(bf16[3,256,128]{2,1,0:T(8,128)(2,1)S(1)} %add_convert_fusion), channel_id=1, source_target_pairs={{0,2},{2,0},{1,3},{3,1},{4,6},{6,4},{5,7},{7,5},{8,10},{10,8},{9,1... | collective-permute-start | bytes 589832 | tf_op jit(solution)/shard_map/ppermute | solution.py:18
  182.9 0.9 convert_reduce_fusion
  183.9 3.3 %collective-permute-done.3 = bf16[3,256,128]{2,1,0:T(8,128)(2,1)S(1)} collective-permute-done((bf16[3,256,128]{2,1,0:T(8,128)(2,1)S(1)}, bf16[3,256,128]{2,1,0:T(8,128)(2,1)S(1)}, u32[]{:S(2)}, u32[]{:S(2)}) %collective-permute-start.3) | collective-permute-done | bytes 196640 | tf_op jit(solution)/shard_map/ppermute | solution.py:18
  187.1 0.7 convert_reduce_fusion.1
  187.8 0.4 fusion.4
  188.2 0.4 fusion.3
  188.6 0.4 fusion.2
  188.9 1.0 pad_maximum_fusion.1
  (63 shorter events, 7.7 us)
Async XLA Ops:
  2.1 28.3 %all-to-all-start = ((bf16[16,3,2,1024]{3,2,1,0:T(2,128)(2,1)}), bf16[16,3,2,1024]{3,2,1,0:T(2,128)(2,1)S(1)}, u32[]{:S(2)}, u32[]{:S(2)}) async-start(bf16[16,3,2,1024]{3,2,1,0:T(2,128)(2,1)} %broadcast_in_dim.16), calls=%async_computation | async-start | bytes 393216 | tf_op jit(solution)/shard_map/all_to_all | solution.py:23
  33.3 22.0 %all-to-all-start.1 = ((bf16[8,3,32,1024]{3,2,1,0:T(8,128)(2,1)}), bf16[8,3,32,1024]{3,2,1,0:T(8,128)(2,1)S(1)}, u32[]{:S(2)}, u32[]{:S(2)}) async-start(bf16[8,3,32,1024]{3,2,1,0:T(8,128)(2,1)} %broadcast_in_dim.18), calls=%async_computation.1 | async-start | bytes 3145728 | tf_op jit(solution)/shard_map/all_to_all | solution.py:29
  50.5 5.0 %copy-start.7 = (bf16[3,1024,128]{2,1,0:T(8,128)(2,1)S(1)}, bf16[3,1024,128]{2,1,0:T(8,128)(2,1)}, u32[]{:S(2)}) copy-start(bf16[3,1024,128]{2,1,0:T(8,128)(2,1)} %param.10) | copy-start | bytes 2359300
  55.5 2.1 %copy-start.1 = (bf16[8,1,32,1024]{3,2,1,0:T(8,128)(2,1)}, bf16[8,1,32,1024]{3,2,1,0:T(8,128)(2,1)S(1)}, u32[]{:S(2)}) copy-start(bf16[8,1,32,1024]{3,2,1,0:T(8,128)(2,1)S(1)} %get-tuple-element.33) | copy-start | bytes 1572868
  55.5 2.1 %copy-start.3 = (bf16[8,1,32,1024]{3,2,1,0:T(8,128)(2,1)}, bf16[8,1,32,1024]{3,2,1,0:T(8,128)(2,1)S(1)}, u32[]{:S(2)}) copy-start(bf16[8,1,32,1024]{3,2,1,0:T(8,128)(2,1)S(1)} %get-tuple-element.35) | copy-start | bytes 1572868
  55.5 2.1 %copy-start.5 = (bf16[8,1,32,1024]{3,2,1,0:T(8,128)(2,1)}, bf16[8,1,32,1024]{3,2,1,0:T(8,128)(2,1)S(1)}, u32[]{:S(2)}) copy-start(bf16[8,1,32,1024]{3,2,1,0:T(8,128)(2,1)S(1)} %get-tuple-element.34) | copy-start | bytes 1572868
  56.1 19.4 %copy-start.11 = (f32[3,128]{1,0:T(4,128)S(1)}, f32[3,128]{1,0:T(4,128)}, u32[]{:S(2)}) copy-start(f32[3,128]{1,0:T(4,128)} %param.11) | copy-start | bytes 4612
  56.1 19.5 %copy-start = (bf16[6,128,1024]{2,1,0:T(8,128)(2,1)S(1)}, bf16[6,128,1024]{2,1,0:T(8,128)(2,1)}, u32[]{:S(2)}) copy-start(bf16[6,128,1024]{2,1,0:T(8,128)(2,1)} %param.12) | copy-start | bytes 4718596
  57.5 9.9 %collective-permute-start = (f32[3,256,128]{2,1,0:T(8,128)S(1)}, f32[3,256,128]{2,1,0:T(8,128)S(1)}, u32[]{:S(2)}, u32[]{:S(2)}) collective-permute-start(f32[3,256,128]{2,1,0:T(8,128)S(1)} %pad_maximum_fusion.2), channel_id=1, source_target_pairs={{0,1},{1,0},{2,3},{3,2},{4,5},{5,4},{6,7},{7,6},{8,9},{9,8},{10,11... | collective-permute-start | bytes 1179656 | tf_op jit(solution)/shard_map/ppermute | solution.py:18
  67.5 8.0 %collective-permute-start.1 = (bf16[3,256,128]{2,1,0:T(8,128)(2,1)S(1)}, bf16[3,256,128]{2,1,0:T(8,128)(2,1)S(1)}, u32[]{:S(2)}, u32[]{:S(2)}) collective-permute-start(bf16[3,256,128]{2,1,0:T(8,128)(2,1)S(1)} %add_convert_fusion.1), channel_id=1, source_target_pairs={{0,2},{2,0},{1,3},{3,1},{4,6},{6,4},{5,7},{7,5},{8,10},{10,8},{9,1... | collective-permute-start | bytes 589832 | tf_op jit(solution)/shard_map/ppermute | solution.py:18
  101.9 23.2 %copy-start.9 = (f32[3,1024]{1,0:T(4,128)S(1)}, f32[3,1024]{1,0:T(4,128)}, u32[]{:S(2)}) copy-start(f32[3,1024]{1,0:T(4,128)} %param.13) | copy-start | bytes 36868
  101.9 23.2 %copy-start.10 = (bf16[3,2,1024]{2,1,0:T(2,128)(2,1)S(1)}, bf16[3,2,1024]{2,1,0:T(2,128)(2,1)}, u32[]{:S(2)}) copy-start(bf16[3,2,1024]{2,1,0:T(2,128)(2,1)} %param.8) | copy-start | bytes 36868
  167.9 11.0 %collective-permute-start.2 = (f32[3,256,128]{2,1,0:T(8,128)S(1)}, f32[3,256,128]{2,1,0:T(8,128)S(1)}, u32[]{:S(2)}, u32[]{:S(2)}) collective-permute-start(f32[3,256,128]{2,1,0:T(8,128)S(1)} %pad_maximum_fusion.3), channel_id=1, source_target_pairs={{0,1},{1,0},{2,3},{3,2},{4,5},{5,4},{6,7},{7,6},{8,9},{9,8},{10,11... | collective-permute-start | bytes 1179656 | tf_op jit(solution)/shard_map/ppermute | solution.py:18
  179.1 8.0 %collective-permute-start.3 = (bf16[3,256,128]{2,1,0:T(8,128)(2,1)S(1)}, bf16[3,256,128]{2,1,0:T(8,128)(2,1)S(1)}, u32[]{:S(2)}, u32[]{:S(2)}) collective-permute-start(bf16[3,256,128]{2,1,0:T(8,128)(2,1)S(1)} %add_convert_fusion), channel_id=1, source_target_pairs={{0,2},{2,0},{1,3},{3,1},{4,6},{6,4},{5,7},{7,5},{8,10},{10,8},{9,1... | collective-permute-start | bytes 589832 | tf_op jit(solution)/shard_map/ppermute | solution.py:18
  182.9 5.3 %copy-start.8 = (bf16[6,128,1024]{2,1,0:T(8,128)(2,1)}, bf16[6,128,1024]{2,1,0:T(8,128)(2,1)S(1)}, u32[]{:S(2)}) copy-start(bf16[6,128,1024]{2,1,0:T(8,128)(2,1)S(1)} %fusion.16) | copy-start | bytes 4718596
  182.9 4.9 %copy-start.6 = (bf16[8,1,32,1024]{3,2,1,0:T(8,128)(2,1)S(1)}, bf16[8,1,32,1024]{3,2,1,0:T(8,128)(2,1)}, u32[]{:S(2)}) copy-start(bf16[8,1,32,1024]{3,2,1,0:T(8,128)(2,1)} %copy-done.5) | copy-start | bytes 1572868
  182.9 5.3 %copy-start.4 = (bf16[8,1,32,1024]{3,2,1,0:T(8,128)(2,1)S(1)}, bf16[8,1,32,1024]{3,2,1,0:T(8,128)(2,1)}, u32[]{:S(2)}) copy-start(bf16[8,1,32,1024]{3,2,1,0:T(8,128)(2,1)} %copy-done.3) | copy-start | bytes 1572868
  183.9 4.7 %copy-start.2 = (bf16[8,1,32,1024]{3,2,1,0:T(8,128)(2,1)S(1)}, bf16[8,1,32,1024]{3,2,1,0:T(8,128)(2,1)}, u32[]{:S(2)}) copy-start(bf16[8,1,32,1024]{3,2,1,0:T(8,128)(2,1)} %copy-done.1) | copy-start | bytes 1572868

commit v3 on v2

--- a/solution.py
+++ b/solution.py
@@ -31,10 +31,13 @@
     )
 
 
-def scatter_tokens(partial):
-    planes, layers, rows, width = partial.shape
-    got = lax.all_to_all(partial.astype(bf16), PLANE, 0, 0)
-    summed = jnp.sum(got.astype(f32), axis=0).astype(bf16)
+def scatter_plane(partial):
+    got = lax.all_to_all(partial, PLANE, 0, 0)
+    return jnp.sum(got.astype(f32), axis=0).astype(bf16)
+
+
+def scatter_z(summed):
+    layers, rows, width = summed.shape
     blocks = summed.reshape(layers, Z, rows // Z, width).transpose(1, 0, 2, 3)
     got = lax.all_to_all(blocks, "z", 0, 0)
     return jnp.sum(got.astype(f32), axis=0)
@@ -55,9 +58,12 @@
     tokens = winners.shape[1]
     model = encoder_weight.shape[1]
 
-    along_z, winners = lax.optimization_barrier((gather_z(layer_inputs), winners))
-    gathered = gather_plane(along_z)
-    x = [gathered[:, l].reshape(tokens, model) for l in range(layers)]
+    early = layers - 1
+    along_z = gather_z(layer_inputs)
+    gathered = [gather_plane(along_z[:, :early]), gather_plane(along_z[:, early:])]
+    x = [
+        g[:, l].reshape(tokens, model) for g in gathered for l in range(g.shape[1])
+    ]
 
     order = winners.reshape(layers, XH, Z, Y, 2, picks).transpose(0, 1, 3, 2, 4, 5)
     order = order.reshape(layers, tokens, picks)
@@ -67,24 +73,47 @@
         matches = order[:, :, offset : offset + 8, None] == feature_ids
         chosen = jnp.logical_or(chosen, jnp.any(matches, axis=2))
 
-    partial_pre = jnp.stack(
-        [jnp.dot(x[l], encoder_weight[l], preferred_element_type=f32) for l in range(layers)]
-    )
-    partial_pre, chosen = lax.optimization_barrier((partial_pre, chosen))
-    pre_acts = sum_tok(partial_pre) + encoder_bias[:, None, :]
-    activation = jnp.where(chosen, pre_acts, 0.0).astype(bf16)
-    decoded = []
-    for target_layer in range(layers):
+    def encode(first, last):
+        return jnp.stack(
+            [
+                jnp.dot(x[l], encoder_weight[l], preferred_element_type=f32)
+                for l in range(first, last)
+            ]
+        )
+
+    def act(pre_acts, first, last):
+        pre_acts = pre_acts + encoder_bias[first:last, None, :]
+        return jnp.where(chosen[first:last], pre_acts, 0.0).astype(bf16)
+
+    def decode(target_layer, sources):
         partial_sum = None
-        for source in range(target_layer + 1):
+        for source in sources:
             product = jnp.dot(
                 activation[source],
                 decoder_weight[pair_number(source, target_layer, layers)],
                 preferred_element_type=f32,
             )
             partial_sum = product if partial_sum is None else partial_sum + product
-        decoded.append(partial_sum.astype(bf16).reshape(XH * Y, tokens // (XH * Y), model))
-    summed = scatter_tokens(jnp.stack(decoded, axis=1)) + decoder_bias[:, None, :]
+        return partial_sum
+
+    def by_plane(totals):
+        return jnp.stack(
+            [t.astype(bf16).reshape(XH * Y, tokens // (XH * Y), model) for t in totals], axis=1
+        )
+
+    partial_pre, chosen = lax.optimization_barrier((encode(0, early), chosen))
+    pre_acts, x[early] = lax.optimization_barrier((sum_tok(partial_pre), x[early]))
+    activation = list(act(pre_acts, 0, early))
+    sent = by_plane([decode(u, range(u + 1)) for u in range(early)])
+    sent, partial_pre, begun = lax.optimization_barrier(
+        (sent, encode(early, layers), decode(early, range(early)))
+    )
+    summed_early = scatter_plane(sent)
+    activation += list(act(sum_tok(partial_pre), early, layers))
+    sent = by_plane([begun + decode(early, [early])])
+    sent, summed_early = lax.optimization_barrier((sent, summed_early))
+    summed = scatter_z(jnp.concatenate([summed_early, scatter_plane(sent)]))
+    summed = summed + decoder_bias[:, None, :]
     recon = summed.astype(bf16)
     errors_home = (summed - targets.astype(f32)).astype(bf16)
     errors_got = gather_plane(gather_z(errors_home))

time: 191 us -> 215 us (1.13)
  blocking collectives: 84.8 us -> 55.4 us
  starting transfers between devices: 45.4 us -> 70.3 us
  other arithmetic: 14.5 us -> 24 us
  matrix products: 8.04 us -> 16.8 us
  local copies, waits for them, and re-layouts: 7.31 us -> 15.5 us
  waiting for transfers between devices: 28.7 us -> 31 us
    all_to_all x2 -> x1, blocking collectives: 45.3 us -> 18.8 us  [scatter_z(): got = lax.all_to_all(blocks, 'z', 0, 0)]
    all_to_all x0 -> x2, starting transfers between devices: none -> 14.3 us  [scatter_plane(): got = lax.all_to_all(partial, PLANE, 0, 0)]
    all_to_all x0 -> x2, waiting for transfers between devices: none -> 7.23 us  [scatter_plane(): got = lax.all_to_all(partial, PLANE, 0, 0)]
    all_to_all x1 -> x2, starting transfers between devices: 6.65 us -> 12.3 us  [gather_plane(): lax.all_to_all(jnp.broadcast_to(block, (XH * Y,) + block.shape[1:]), PLAN...]
    ppermute x4 -> x6, starting transfers between devices: 23 us -> 28 us  [swap(): return lax.ppermute(x, axis, [(0, 1), (1, 0)])]
    dot_general x9, matrix products: 3.63 us -> 8.42 us  [the longest x6 4.69 us: decode(): jnp.dot(activation[source], decoder_weight[pair_number(source, target_lay...]
    all_to_all x1 -> x2, waiting for transfers between devices: 4.84 us -> 0.2 us  [gather_plane(): lax.all_to_all(jnp.broadcast_to(block, (XH * Y,) + block.shape[1:]), PLAN...]
    dot_general x6, matrix products: 1.51 us -> 5.77 us  [body(): lax.dot_general(activation[source], errors_all[target_layer], (((0,), (0,...]
  transfers between devices with their start and end apart: 6 -> 11, of which waited for: 6 -> 7; matrix products, arithmetic and copies ran while one was open for 7% -> 13% of each run, Pallas kernels for 0% -> 0%
where the time goes in v3:
time: 215 us; the launch traced here: 214 us
  starting transfers between devices  70.3 us (33%)
  blocking collectives  55.4 us (26%)
  waiting for transfers between devices  31 us (14%)
  other arithmetic  24 us (11%)
  matrix products  16.8 us (8%)
  local copies, waits for them, and re-layouts  15.5 us (7%)
    ppermute x6, starting transfers between devices, swap(): return lax.ppermute(x, axis, [(0, 1), (1, 0)])  28 us
    all_to_all x1, blocking collectives, scatter_z(): got = lax.all_to_all(blocks, 'z', 0, 0)  18.8 us
    all_to_all x1, blocking collectives, gather_plane(): lax.all_to_all(jnp.broadcast_to(block, (XH * Y,) + block.shape[1:]), PLAN...  18.5 us
    all_to_all x1, blocking collectives, gather_z(): lax.all_to_all(jnp.broadcast_to(home[None], (Z, layers, rows, width)), 'z...  18 us
    all_to_all x1, starting transfers between devices, gather_z(): lax.all_to_all(jnp.broadcast_to(home[None], (Z, layers, rows, width)), 'z...  15.7 us
    all_to_all x2, starting transfers between devices, scatter_plane(): got = lax.all_to_all(partial, PLANE, 0, 0)  14.3 us
    ppermute x6, waiting for transfers between devices, swap(): return lax.ppermute(x, axis, [(0, 1), (1, 0)])  14.1 us
    all_to_all x2, starting transfers between devices, gather_plane(): lax.all_to_all(jnp.broadcast_to(block, (XH * Y,) + block.shape[1:]), PLAN...  12.3 us
  transfers between devices with their start and end apart: 11, of which 7 were waited for; matrix products, arithmetic and copies ran while one was open for 13% of the time, Pallas kernels for 0%

profile of v3, /device:TPU:1, one launch (start us, length us, event | category | flops | bytes accessed | tf_op | source)
XLA Modules:
  0.0 214.1 jit_solution(4806236879309727016)
XLA Ops:
  0.6 1.5 broadcast_in_dim.25
  2.1 15.7 %all-to-all-start = ((bf16[16,3,2,1024]{3,2,1,0:T(2,128)(2,1)}), bf16[16,3,2,1024]{3,2,1,0:T(2,128)(2,1)S(1)}, u32[]{:S(2)}, u32[]{:S(2)}) async-start(bf16[16,3,2,1024]{3,2,1,0:T(2,128)(2,1)} %broadcast_in_dim.25), calls=%async_computation | async-start | bytes 393216 | tf_op jit(solution)/shard_map/all_to_all | solution.py:23
  19.2 1.8 fusion.59
  21.0 9.5 %all-to-all-done = bf16[16,3,2,1024]{3,2,1,0:T(2,128)(2,1)S(1)} async-done(((bf16[16,3,2,1024]{3,2,1,0:T(2,128)(2,1)}), bf16[16,3,2,1024]{3,2,1,0:T(2,128)(2,1)S(1)}, u32[]{:S(2)}, u32[]{:S(2)}) %all-to-all-start) | async-done | bytes 196640 | tf_op jit(solution)/shard_map/all_to_all | solution.py:23
  31.8 6.7 %all-to-all-start.1 = ((bf16[8,2,32,1024]{3,2,1,0:T(8,128)(2,1)}), bf16[8,2,32,1024]{3,2,1,0:T(8,128)(2,1)S(1)}, u32[]{:S(2)}, u32[]{:S(2)}) async-start(bf16[8,2,32,1024]{3,2,1,0:T(8,128)(2,1)} %broadcast_in_dim.27), calls=%async_computation.1 | async-start | bytes 2097152 | tf_op jit(solution)/shard_map/all_to_all | solution.py:29
  38.4 10.5 %compare_reduce_fusion.6 = (pred[3,256,128]{2,1,0:T(8,128)(4,1)S(1)}, pred[3,256,128]{2,1,0:T(8,128)(4,1)S(1)}, pred[3,256,128]{2,1,0:T(8,128)(4,1)S(1)}, pred[3...) fusion(s32[3,256,8]{2,1,0:T(8,128)} %get-tuple-element.92, ...), kind=kLoop, calls=%fused_computation.7 | loop fusion | flops 11796480 | bytes 983552 | tf_op jit(solution)/shard_map/reduce_or | solution.py:74
  49.5 1.3 convolution_bitcast_fusion.2
  52.7 8.2 %collective-permute-start = (f32[2,256,128]{2,1,0:T(8,128)}, f32[2,256,128]{2,1,0:T(8,128)}, u32[]{:S(2)}, u32[]{:S(2)}) collective-permute-start(f32[2,256,128]{2,1,0:T(8,128)} %pad_maximum_fusion.3), channel_id=1, source_target_pairs={{0,1},{1,0},{2,3},{3,2},{4,5},{5,4},{6,7},{7,6},{8,9},{9,8},{10,11... | collective-permute-start | bytes 786440 | tf_op jit(solution)/shard_map/ppermute | solution.py:18
  61.8 5.7 %all-to-all-start.2 = ((bf16[8,1,32,1024]{3,2,1,0:T(8,128)(2,1)}), bf16[8,1,32,1024]{3,2,1,0:T(8,128)(2,1)S(1)}, u32[]{:S(2)}, u32[]{:S(2)}) async-start(bf16[8,1,32,1024]{3,2,1,0:T(8,128)(2,1)} %broadcast_in_dim.30), calls=%async_computation.2 | async-start | bytes 1048576 | tf_op jit(solution)/shard_map/all_to_all | solution.py:29
  68.5 2.2 %collective-permute-start.1 = (bf16[2,256,128]{2,1,0:T(8,128)(2,1)S(1)}, bf16[2,256,128]{2,1,0:T(8,128)(2,1)S(1)}, u32[]{:S(2)}, u32[]{:S(2)}) collective-permute-start(bf16[2,256,128]{2,1,0:T(8,128)(2,1)S(1)} %add_convert_fusion.1), channel_id=1, source_target_pairs={{0,2},{2,0},{1,3},{3,1},{4,6},{6,4},{5,7},{7,5},{8,10},{10,8},{9,1... | collective-permute-start | bytes 393224 | tf_op jit(solution)/shard_map/ppermute | solution.py:18
  70.8 6.5 %collective-permute-done.1 = bf16[2,256,128]{2,1,0:T(8,128)(2,1)S(1)} collective-permute-done((bf16[2,256,128]{2,1,0:T(8,128)(2,1)S(1)}, bf16[2,256,128]{2,1,0:T(8,128)(2,1)S(1)}, u32[]{:S(2)}, u32[]{:S(2)}) %collective-permute-start.1) | collective-permute-done | bytes 131104 | tf_op jit(solution)/shard_map/ppermute | solution.py:18
  79.9 1.2 convolution_bitcast_fusion.1
  81.4 1.3 convolution_add_fusion.1
  83.8 7.1 %all-to-all-start.3 = ((bf16[8,2,32,1024]{3,2,1,0:T(8,128)(2,1)}), bf16[8,2,32,1024]{3,2,1,0:T(8,128)(2,1)}, u32[]{:S(2)}, u32[]{:S(2)}) async-start(bf16[8,2,32,1024]{3,2,1,0:T(8,128)(2,1)} %pad_maximum_fusion), calls=%async_computation.3 | async-start | bytes 2097152 | tf_op jit(solution)/shard_map/all_to_all | solution.py:35
  90.9 3.3 %collective-permute-start.2 = (f32[1,256,128]{2,1,0:T(8,128)S(1)}, f32[1,256,128]{2,1,0:T(8,128)S(1)}, u32[]{:S(2)}, u32[]{:S(2)}) collective-permute-start(f32[1,256,128]{2,1,0:T(8,128)S(1)} %convolution_bitcast_fusion.1), channel_id=1, source_target_pairs={{0,1},{1,0},{2,3},{3,2},{4,5},{5,4},{6,7},{7,6},{8,9},{9,8},{10,11... | collective-permute-start | bytes 393224 | tf_op jit(solution)/shard_map/ppermute | solution.py:18
  96.1 1.9 collective-permute-start.3
  98.0 5.3 %collective-permute-done.3 = bf16[1,256,128]{2,1,0:T(8,128)(2,1)S(1)} collective-permute-done((bf16[1,256,128]{2,1,0:T(8,128)(2,1)S(1)}, bf16[1,256,128]{2,1,0:T(8,128)(2,1)S(1)}, u32[]{:S(2)}, u32[]{:S(2)}) %collective-permute-start.3) | collective-permute-done | bytes 65568 | tf_op jit(solution)/shard_map/ppermute | solution.py:18
  103.4 2.3 %fusion.1 = bf16[256,1024]{1,0:T(8,128)(2,1)} fusion(f32[256,1024]{1,0:T(8,128)} %convolution_add_fusion.1, bf16[6,128,1024]{2,1,0:T(8,128)(2,1)S(1)} %copy-done, bf16[1,256,128]{2,1,0:T(8,128)(2,1)S(1)} %collective-permute-done.3, bf16[1,256,128]{2,1,0:T(8,128)(2,1)S(1)} %add_convert_fusion.2, pred[3,256,128]{2,1,0:T(32,128)(4,1)S(1)} %or_or_fusion, ...), kind=kOutput, calls=%fused_computation.13 | convolution fusion | flops 67829760 | bytes 1999360 | tf_op jit(solution)/shard_map/dot_general | solution.py:91
  105.7 2.1 reduce_sum.51
  107.8 7.2 %all-to-all-start.4 = ((bf16[8,1,32,1024]{3,2,1,0:T(8,128)(2,1)}), bf16[8,1,32,1024]{3,2,1,0:T(8,128)(2,1)}, u32[]{:S(2)}, u32[]{:S(2)}) async-start(bf16[8,1,32,1024]{3,2,1,0:T(8,128)(2,1)} %bitcast.177), calls=%async_computation.4 | async-start | bytes 1048576 | tf_op jit(solution)/shard_map/all_to_all | solution.py:35
  115.0 1.7 copy.78
  116.8 7.2 %all-to-all-done.4 = bf16[8,1,32,1024]{3,2,1,0:T(8,128)(2,1)} async-done(((bf16[8,1,32,1024]{3,2,1,0:T(8,128)(2,1)}), bf16[8,1,32,1024]{3,2,1,0:T(8,128)(2,1)}, u32[]{:S(2)}, u32[]{:S(2)}) %all-to-all-start.4) | async-done | bytes 524320 | tf_op jit(solution)/shard_map/all_to_all | solution.py:35
  124.0 1.8 reduce_sum.52
  125.7 1.5 concatenate.11
  127.3 1.2 maximum_bitcast_fusion
  128.7 18.8 %all_to_all.40 = bf16[16,3,2,1024]{3,2,1,0:T(2,128)(2,1)S(1)} all-to-all(bf16[16,3,2,1024]{3,2,1,0:T(2,128)(2,1)S(1)} %copy.81), channel_id=1, replica_groups=mesh['xh'=2,'z'=16,'y'=4,'xl'=2,'core'=2] {'z'}, dimensions={0} | all-to-all | bytes 393216 | tf_op jit(solution)/shard_map/all_to_all | solution.py:42
  148.4 18.0 %all_to_all.41 = bf16[16,3,2,1024]{3,2,1,0:T(2,128)(2,1)S(1)} all-to-all(bf16[16,3,2,1024]{3,2,1,0:T(2,128)(2,1)S(1)} %broadcast_in_dim.34), channel_id=1, replica_groups=mesh['xh'=2,'z'=16,'y'=4,'xl'=2,'core'=2] {'z'}, dimensions={0} | all-to-all | bytes 393216 | tf_op jit(solution)/shard_map/all_to_all | solution.py:23
  167.3 1.7 broadcast_in_dim.35
  170.1 18.5 %all_to_all.42 = bf16[8,3,32,1024]{3,2,1,0:T(8,128)(2,1)S(1)} all-to-all(bf16[8,3,32,1024]{3,2,1,0:T(8,128)(2,1)S(1)} %broadcast_in_dim.36), channel_id=1, replica_groups=mesh['xh'=2,'z'=16,'y'=4,'xl'=2,'core'=2] {'xh','y'}, dimensions={0} | all-to-all | bytes 3145728 | tf_op jit(solution)/shard_map/all_to_all | solution.py:29
  190.7 10.4 %collective-permute-start.4 = (f32[3,256,128]{2,1,0:T(8,128)S(1)}, f32[3,256,128]{2,1,0:T(8,128)S(1)}, u32[]{:S(2)}, u32[]{:S(2)}) collective-permute-start(f32[3,256,128]{2,1,0:T(8,128)S(1)} %pad_maximum_fusion.2), channel_id=1, source_target_pairs={{0,1},{1,0},{2,3},{3,2},{4,5},{5,4},{6,7},{7,6},{8,9},{9,8},{10,11... | collective-permute-start | bytes 1179656 | tf_op jit(solution)/shard_map/ppermute | solution.py:18
  201.1 1.3 collective-permute-done.4
  202.6 2.0 collective-permute-start.5
  (76 shorter events, 27.6 us)
Async XLA Ops:
  2.1 28.3 %all-to-all-start = ((bf16[16,3,2,1024]{3,2,1,0:T(2,128)(2,1)}), bf16[16,3,2,1024]{3,2,1,0:T(2,128)(2,1)S(1)}, u32[]{:S(2)}, u32[]{:S(2)}) async-start(bf16[16,3,2,1024]{3,2,1,0:T(2,128)(2,1)} %broadcast_in_dim.25), calls=%async_computation | async-start | bytes 393216 | tf_op jit(solution)/shard_map/all_to_all | solution.py:23
  30.4 1.4 copy-start.2
  30.7 7.8 %copy-start.1 = (s32[3,256,8]{2,1,0:T(8,128)S(1)}, s32[3,256,8]{2,1,0:T(8,128)}, u32[]{:S(2)}) copy-start(s32[3,256,8]{2,1,0:T(8,128)} %get-tuple-element.90) | copy-start | bytes 73732
  31.8 17.6 %all-to-all-start.1 = ((bf16[8,2,32,1024]{3,2,1,0:T(8,128)(2,1)}), bf16[8,2,32,1024]{3,2,1,0:T(8,128)(2,1)S(1)}, u32[]{:S(2)}, u32[]{:S(2)}) async-start(bf16[8,2,32,1024]{3,2,1,0:T(8,128)(2,1)} %broadcast_in_dim.27), calls=%async_computation.1 | async-start | bytes 2097152 | tf_op jit(solution)/shard_map/all_to_all | solution.py:29
  49.4 11.5 %slice-start = ((bf16[16,3,2,1024]{3,2,1,0:T(2,128)(2,1)}), bf16[16,1,2,1024]{3,2,1,0:T(2,128)(2,1)S(1)}, s32[]{:S(2)}) async-start(bf16[16,3,2,1024]{3,2,1,0:T(2,128)(2,1)} %copy-done.2), calls=%async_computation.8 | async-start | bytes 131072 | tf_op jit(solution)/shard_map/slice | solution.py:63
  52.7 25.3 %slice-start.1 = ((f32[3,128]{1,0:T(4,128)}), f32[2,128]{1,0:T(2,128)S(1)}, s32[]{:S(2)}) async-start(f32[3,128]{1,0:T(4,128)} %param.11), calls=%async_computation.9 | async-start | bytes 2048 | tf_op jit(solution)/shard_map/slice | solution.py:85
  52.7 14.8 %collective-permute-start = (f32[2,256,128]{2,1,0:T(8,128)}, f32[2,256,128]{2,1,0:T(8,128)}, u32[]{:S(2)}, u32[]{:S(2)}) collective-permute-start(f32[2,256,128]{2,1,0:T(8,128)} %pad_maximum_fusion.3), channel_id=1, source_target_pairs={{0,1},{1,0},{2,3},{3,2},{4,5},{5,4},{6,7},{7,6},{8,9},{9,8},{10,11... | collective-permute-start | bytes 786440 | tf_op jit(solution)/shard_map/ppermute | solution.py:18
  60.9 18.1 %copy-start = (bf16[6,128,1024]{2,1,0:T(8,128)(2,1)S(1)}, bf16[6,128,1024]{2,1,0:T(8,128)(2,1)}, u32[]{:S(2)}) copy-start(bf16[6,128,1024]{2,1,0:T(8,128)(2,1)} %param.12) | copy-start | bytes 4718596
  61.8 16.2 %all-to-all-start.2 = ((bf16[8,1,32,1024]{3,2,1,0:T(8,128)(2,1)}), bf16[8,1,32,1024]{3,2,1,0:T(8,128)(2,1)S(1)}, u32[]{:S(2)}, u32[]{:S(2)}) async-start(bf16[8,1,32,1024]{3,2,1,0:T(8,128)(2,1)} %broadcast_in_dim.30), calls=%async_computation.2 | async-start | bytes 1048576 | tf_op jit(solution)/shard_map/all_to_all | solution.py:29
  68.5 8.7 %collective-permute-start.1 = (bf16[2,256,128]{2,1,0:T(8,128)(2,1)S(1)}, bf16[2,256,128]{2,1,0:T(8,128)(2,1)S(1)}, u32[]{:S(2)}, u32[]{:S(2)}) collective-permute-start(bf16[2,256,128]{2,1,0:T(8,128)(2,1)S(1)} %add_convert_fusion.1), channel_id=1, source_target_pairs={{0,2},{2,0},{1,3},{3,1},{4,6},{6,4},{5,7},{7,5},{8,10},{10,8},{9,1... | collective-permute-start | bytes 393224 | tf_op jit(solution)/shard_map/ppermute | solution.py:18
  81.1 9.8 %copy-start.3 = (f32[1,256,128]{2,1,0:T(8,128)}, f32[1,256,128]{2,1,0:T(8,128)S(1)}, u32[]{:S(2)}) copy-start(f32[1,256,128]{2,1,0:T(8,128)S(1)} %convolution_bitcast_fusion.1) | copy-start | bytes 393220
  83.8 14.2 %copy-start.6 = (f32[3,128]{1,0:T(4,128)S(1)}, f32[3,128]{1,0:T(4,128)}, u32[]{:S(2)}) copy-start(f32[3,128]{1,0:T(4,128)} %param.11) | copy-start | bytes 4612
  83.8 21.9 %all-to-all-start.3 = ((bf16[8,2,32,1024]{3,2,1,0:T(8,128)(2,1)}), bf16[8,2,32,1024]{3,2,1,0:T(8,128)(2,1)}, u32[]{:S(2)}, u32[]{:S(2)}) async-start(bf16[8,2,32,1024]{3,2,1,0:T(8,128)(2,1)} %pad_maximum_fusion), calls=%async_computation.3 | async-start | bytes 2097152 | tf_op jit(solution)/shard_map/all_to_all | solution.py:35
  90.9 4.3 %collective-permute-start.2 = (f32[1,256,128]{2,1,0:T(8,128)S(1)}, f32[1,256,128]{2,1,0:T(8,128)S(1)}, u32[]{:S(2)}, u32[]{:S(2)}) collective-permute-start(f32[1,256,128]{2,1,0:T(8,128)S(1)} %convolution_bitcast_fusion.1), channel_id=1, source_target_pairs={{0,1},{1,0},{2,3},{3,2},{4,5},{5,4},{6,7},{7,6},{8,9},{9,8},{10,11... | collective-permute-start | bytes 393224 | tf_op jit(solution)/shard_map/ppermute | solution.py:18
  96.1 7.3 %collective-permute-start.3 = (bf16[1,256,128]{2,1,0:T(8,128)(2,1)S(1)}, bf16[1,256,128]{2,1,0:T(8,128)(2,1)S(1)}, u32[]{:S(2)}, u32[]{:S(2)}) collective-permute-start(bf16[1,256,128]{2,1,0:T(8,128)(2,1)S(1)} %add_convert_fusion.2), channel_id=1, source_target_pairs={{0,2},{2,0},{1,3},{3,1},{4,6},{6,4},{5,7},{7,5},{8,10},{10,8},{9,1... | collective-permute-start | bytes 196616 | tf_op jit(solution)/shard_map/ppermute | solution.py:18
  107.8 16.2 %all-to-all-start.4 = ((bf16[8,1,32,1024]{3,2,1,0:T(8,128)(2,1)}), bf16[8,1,32,1024]{3,2,1,0:T(8,128)(2,1)}, u32[]{:S(2)}, u32[]{:S(2)}) async-start(bf16[8,1,32,1024]{3,2,1,0:T(8,128)(2,1)} %bitcast.177), calls=%async_computation.4 | async-start | bytes 1048576 | tf_op jit(solution)/shard_map/all_to_all | solution.py:35
  115.0 32.6 %copy-start.4 = (f32[3,1024]{1,0:T(4,128)S(1)}, f32[3,1024]{1,0:T(4,128)}, u32[]{:S(2)}) copy-start(f32[3,1024]{1,0:T(4,128)} %param.13) | copy-start | bytes 36868
  115.0 32.6 %copy-start.5 = (bf16[3,2,1024]{2,1,0:T(2,128)(2,1)S(1)}, bf16[3,2,1024]{2,1,0:T(2,128)(2,1)}, u32[]{:S(2)}) copy-start(bf16[3,2,1024]{2,1,0:T(2,128)(2,1)} %param.8) | copy-start | bytes 36868
  190.7 11.7 %collective-permute-start.4 = (f32[3,256,128]{2,1,0:T(8,128)S(1)}, f32[3,256,128]{2,1,0:T(8,128)S(1)}, u32[]{:S(2)}, u32[]{:S(2)}) collective-permute-start(f32[3,256,128]{2,1,0:T(8,128)S(1)} %pad_maximum_fusion.2), channel_id=1, source_target_pairs={{0,1},{1,0},{2,3},{3,2},{4,5},{5,4},{6,7},{7,6},{8,9},{9,8},{10,11... | collective-permute-start | bytes 1179656 | tf_op jit(solution)/shard_map/ppermute | solution.py:18
  202.6 8.7 %collective-permute-start.5 = (bf16[3,256,128]{2,1,0:T(8,128)(2,1)S(1)}, bf16[3,256,128]{2,1,0:T(8,128)(2,1)S(1)}, u32[]{:S(2)}, u32[]{:S(2)}) collective-permute-start(bf16[3,256,128]{2,1,0:T(8,128)(2,1)S(1)} %add_convert_fusion), channel_id=1, source_target_pairs={{0,2},{2,0},{1,3},{3,1},{4,6},{6,4},{5,7},{7,5},{8,10},{10,8},{9,1... | collective-permute-start | bytes 589832 | tf_op jit(solution)/shard_map/ppermute | solution.py:18

commit v4 on v2

v4 whole, which is shorter than its diff:
```python
import jax
import jax.numpy as jnp
from jax import lax
from jax.experimental import pallas as pl
from jax.experimental.pallas import tpu as pltpu
from jax.sharding import Mesh, PartitionSpec as P

FEAT = ("xh", "z", "y")
TOK = ("xl", "core")
PLANE = ("xh", "y")
XH, Z, Y, XL, CORE = 2, 16, 4, 2, 2
bf16, f32 = jnp.bfloat16, jnp.float32


def pair_number(source, target_layer, layers):
    return sum((layers - before for before in range(source))) + target_layer - source


def swap(x, axis):
    return lax.ppermute(x, axis, [(0, 1), (1, 0)])


def gather_z(home):
    layers, rows, width = home.shape
    return lax.all_to_all(jnp.broadcast_to(home[None], (Z, layers, rows, width)), "z", 0, 0)


def gather_plane(along_z):
    _, layers, rows, width = along_z.shape
    block = along_z.transpose(1, 0, 2, 3).reshape(1, layers, Z * rows, width)
    return lax.all_to_all(
        jnp.broadcast_to(block, (XH * Y,) + block.shape[1:]), PLANE, 0, 0
    )


def scatter_tokens(sent):
    planes, layers, rows, width = sent.shape
    got = lax.all_to_all(sent, PLANE, 0, 0)
    summed = jnp.sum(got.astype(f32), axis=0).astype(bf16)
    blocks = summed.reshape(layers, Z, rows // Z, width).transpose(1, 0, 2, 3)
    got = lax.all_to_all(blocks, "z", 0, 0)
    return jnp.sum(got.astype(f32), axis=0)


def rows_of(ref, layer):
    block = ref[:, layer]
    return block.reshape(block.shape[0] * block.shape[1], block.shape[2])


def encode_kernel(x_ref, weight_ref, out_ref):
    for l in range(out_ref.shape[0]):
        out_ref[l] = jnp.dot(rows_of(x_ref, l), weight_ref[l], preferred_element_type=f32)


def decode_kernel(mine_ref, theirs_ref, bias_ref, mask_ref, weight_ref, act_ref, out_ref):
    layers = act_ref.shape[0]
    for l in range(layers):
        pre_acts = mine_ref[l].astype(f32) + theirs_ref[l].astype(f32) + bias_ref[l : l + 1]
        act_ref[l] = jnp.where(mask_ref[l] != 0, pre_acts, 0.0).astype(bf16)
    for u in range(layers):
        totals = None
        for s in range(u + 1):
            product = jnp.dot(
                act_ref[s], weight_ref[pair_number(s, u, layers)], preferred_element_type=f32
            )
            totals = product if totals is None else totals + product
        out_ref[:, u] = totals.astype(bf16).reshape(
            out_ref.shape[0], out_ref.shape[2], out_ref.shape[3]
        )


def grad_kernel(errors_ref, weight_ref, out_ref):
    layers = out_ref.shape[0]
    for s in range(layers):
        grad_act = None
        for u in range(s, layers):
            product = lax.dot_general(
                rows_of(errors_ref, u),
                weight_ref[pair_number(s, u, layers)],
                (((1,), (1,)), ((), ())),
                preferred_element_type=f32,
            )
            grad_act = product if grad_act is None else grad_act + product
        out_ref[s] = grad_act


def decoder_grad_kernel(act_ref, errors_ref, out_ref, bias_ref):
    layers = act_ref.shape[0]
    for u in range(layers):
        errors = rows_of(errors_ref, u)
        bias_ref[u : u + 1] = jnp.sum(errors.astype(f32), axis=0, keepdims=True)
        for s in range(u + 1):
            out_ref[pair_number(s, u, layers)] = lax.dot_general(
                act_ref[s], errors, (((0,), (0,)), ((), ())), preferred_element_type=f32
            ).astype(bf16)


def encoder_grad_kernel(mine_ref, theirs_ref, mask_ref, x_ref, out_ref, bias_ref):
    for l in range(out_ref.shape[0]):
        grad_act = mine_ref[l].astype(f32) + theirs_ref[l].astype(f32)
        grad_pre = jnp.where(mask_ref[l] != 0, grad_act, 0.0).astype(bf16)
        bias_ref[l : l + 1] = jnp.sum(grad_pre.astype(f32), axis=0, keepdims=True)
        out_ref[l] = lax.dot_general(
            rows_of(x_ref, l), grad_pre, (((0,), (0,)), ((), ())), preferred_element_type=f32
        ).astype(bf16)


def call(kernel, args, outs, flops):
    size = sum(a.size * a.dtype.itemsize for a in args)
    return pl.pallas_call(
        kernel,
        out_shape=[jax.ShapeDtypeStruct(shape, kind) for shape, kind in outs],
        in_specs=[pl.BlockSpec(memory_space=pltpu.VMEM) for _ in args],
        out_specs=[pl.BlockSpec(memory_space=pltpu.VMEM) for _ in outs],
        compiler_params=pltpu.CompilerParams(vmem_limit_bytes=24 << 20),
        cost_estimate=pl.CostEstimate(flops=flops, bytes_accessed=2 * size, transcendentals=0),
    )(*args)


def body(
    layer_inputs, targets, winners, encoder_weight, encoder_bias, decoder_weight, decoder_bias
):
    layers = layer_inputs.shape[0]
    width_here = encoder_weight.shape[2]
    picks = winners.shape[2]
    tokens = winners.shape[1]
    model = encoder_weight.shape[1]

    along_z = gather_z(layer_inputs)

    order = winners.reshape(layers, XH, Z, Y, 2, picks).transpose(0, 1, 3, 2, 4, 5)
    order = order.reshape(layers, tokens, picks)
    feature_ids = lax.axis_index(FEAT) * width_here + jnp.arange(width_here, dtype=jnp.int32)
    chosen = jnp.zeros((layers, tokens, width_here), jnp.bool_)
    for offset in range(0, picks, 8):
        matches = order[:, :, offset : offset + 8, None] == feature_ids
        chosen = jnp.logical_or(chosen, jnp.any(matches, axis=2))
    along_z, chosen = lax.optimization_barrier((along_z, chosen.astype(bf16)))
    gathered = gather_plane(along_z)

    planes, rows = XH * Y, tokens // (XH * Y)
    narrow = (layers, tokens, width_here)
    work = 2 * tokens * width_here * model
    (partial_pre,) = call(
        encode_kernel, (gathered, encoder_weight), [(narrow, f32)], layers * work
    )
    mine = (partial_pre + swap(partial_pre, "core")).astype(bf16)
    activation, sent = call(
        decode_kernel,
        (mine, swap(mine, "xl"), encoder_bias, chosen, decoder_weight),
        [(narrow, bf16), ((planes, layers, rows, model), bf16)],
        decoder_weight.shape[0] * work,
    )
    summed = scatter_tokens(sent) + decoder_bias[:, None, :]
    recon = summed.astype(bf16)
    errors_home = (summed - targets.astype(f32)).astype(bf16)
    errors_got = gather_plane(gather_z(errors_home))
    (partial_grad,) = call(
        grad_kernel,
        (errors_got, decoder_weight),
        [(narrow, f32)],
        decoder_weight.shape[0] * work,
    )
    both, errors_got = lax.optimization_barrier((swap(partial_grad, "core"), errors_got))
    mine = (partial_grad + both).astype(bf16)
    decoder_grad, decoder_bias_grad = call(
        decoder_grad_kernel,
        (activation, errors_got),
        [(decoder_weight.shape, bf16), ((layers, model), f32)],
        decoder_weight.shape[0] * work,
    )
    encoder_grad, encoder_bias_grad = call(
        encoder_grad_kernel,
        (mine, swap(mine, "xl"), chosen, gathered),
        [((layers, model, width_here), bf16), ((layers, width_here), f32)],
        layers * work,
    )
    return (recon, encoder_grad, encoder_bias_grad, decoder_grad, decoder_bias_grad)


def solution(mesh):
    fine = Mesh(mesh.devices.reshape(XH, Z, Y, XL, CORE), FEAT + TOK)
    in_specs = (
        P(None, FEAT, TOK),
        P(None, FEAT, TOK),
        P(),
        P(None, TOK, FEAT),
        P(None, FEAT),
        P(None, FEAT, TOK),
        P(None, TOK),
    )
    out_specs = (
        P(None, FEAT, TOK),
        P(None, TOK, FEAT),
        P(None, FEAT),
        P(None, FEAT, TOK),
        P(None, TOK),
    )
    return jax.shard_map(body, mesh=fine, in_specs=in_specs, out_specs=out_specs, check_vma=False)
```

time: 191 us -> 193 us (1.010)
  blocking collectives: 84.8 us -> 110 us
  waiting for transfers between devices: 28.7 us -> 13 us
  matrix products: 8.04 us -> 0 us
  starting transfers between devices: 45.4 us -> 38.4 us
  Pallas kernels: 0 us -> 5.84 us
  local copies, waits for them, and re-layouts: 7.31 us -> 10.4 us
    all_to_all x1 -> x2, blocking collectives: 21.3 us -> 43.5 us  [gather_plane(): lax.all_to_all(jnp.broadcast_to(block, (XH * Y,) + block.shape[1:]), PLAN...]
    all_to_all x1, waiting for transfers between devices: 12.5 us -> 0.71 us  [gather_z(): lax.all_to_all(jnp.broadcast_to(home[None], (Z, layers, rows, width)), 'z...]
    dot_general x24 -> x0, matrix products: 8.04 us -> none  [the longest x3 1.93 us: body(): jnp.dot(x[l], encoder_weight[l], preferred_element_type=f32)]
    all_to_all x1 -> x0, starting transfers between devices: 6.65 us -> none  [gather_plane(): lax.all_to_all(jnp.broadcast_to(block, (XH * Y,) + block.shape[1:]), PLAN...]
    pallas_call x0 -> x5, Pallas kernels: none -> 5.84 us  [call(): pl.pallas_call(kernel, out_shape=[jax.ShapeDtypeStruct(shape, kind) for s...]
    all_to_all x1 -> x0, waiting for transfers between devices: 4.84 us -> none  [gather_plane(): lax.all_to_all(jnp.broadcast_to(block, (XH * Y,) + block.shape[1:]), PLAN...]
    all_to_all x1, blocking collectives: 20.9 us -> 22.9 us  [scatter_tokens(): got = lax.all_to_all(blocks, 'z', 0, 0)]
  transfers between devices with their start and end apart: 6 -> 5, of which waited for: 6 -> 5; matrix products, arithmetic and copies ran while one was open for 7% -> 6% of each run, Pallas kernels for 0% -> 1%
where the time goes in v4:
time: 193 us; the launch traced here: 192 us
  blocking collectives  110 us (57%)
  starting transfers between devices  38.4 us (20%)
  other arithmetic  13.8 us (7%)
  waiting for transfers between devices  13 us (7%)
  local copies, waits for them, and re-layouts  10.4 us (5%)
  Pallas kernels  5.84 us (3%)
    all_to_all x2, blocking collectives, gather_plane(): lax.all_to_all(jnp.broadcast_to(block, (XH * Y,) + block.shape[1:]), PLAN...  43.5 us
    all_to_all x1, blocking collectives, scatter_tokens(): got = lax.all_to_all(sent, PLANE, 0, 0)  24.1 us
    all_to_all x1, blocking collectives, scatter_tokens(): got = lax.all_to_all(blocks, 'z', 0, 0)  22.9 us
    ppermute x4, starting transfers between devices, swap(): return lax.ppermute(x, axis, [(0, 1), (1, 0)])  22.6 us
    all_to_all x1, blocking collectives, gather_z(): lax.all_to_all(jnp.broadcast_to(home[None], (Z, layers, rows, width)), 'z...  19.1 us
    all_to_all x1, starting transfers between devices, gather_z(): lax.all_to_all(jnp.broadcast_to(home[None], (Z, layers, rows, width)), 'z...  15.7 us
    ppermute x4, waiting for transfers between devices, swap(): return lax.ppermute(x, axis, [(0, 1), (1, 0)])  12.3 us
    reduce_or x1, other arithmetic, body(): chosen = jnp.logical_or(chosen, jnp.any(matches, axis=2))  9.5 us
  transfers between devices with their start and end apart: 5, of which 5 were waited for; matrix products, arithmetic and copies ran while one was open for 6% of the time, Pallas kernels for 1%

profile of v4, /device:TPU:1, one launch (start us, length us, event | category | flops | bytes accessed | tf_op | source)
XLA Modules:
  0.0 191.8 jit_solution(14964493449558247616)
XLA Ops:
  0.6 1.5 broadcast_in_dim.12
  2.1 15.7 %all-to-all-start = ((bf16[16,3,2,1024]{3,2,1,0:T(2,128)(2,1)}), bf16[16,3,2,1024]{3,2,1,0:T(2,128)(2,1)S(1)}, u32[]{:S(2)}, u32[]{:S(2)}) async-start(bf16[16,3,2,1024]{3,2,1,0:T(2,128)(2,1)} %broadcast_in_dim.12), calls=%async_computation | async-start | bytes 393216 | tf_op jit(solution)/shard_map/all_to_all | solution.py:25
  17.9 1.1 copy.21
  19.2 0.8 fusion
  20.0 9.5 %compare_reduce_fusion.6 = (pred[3,256,128]{2,1,0:T(8,128)(4,1)S(1)}, pred[3,256,128]{2,1,0:T(8,128)(4,1)S(1)}, pred[3,256,128]{2,1,0:T(8,128)(4,1)S(1)}, pred[3...) fusion(s32[3,256,8]{2,1,0:T(8,128)S(1)} %get-tuple-element.40, ...), kind=kLoop, calls=%fused_computation.6 | loop fusion | flops 11796480 | bytes 983552 | tf_op jit(solution)/shard_map/reduce_or | solution.py:137
  29.5 0.2 or_convert_fusion.mask_ref
  29.7 0.7 all-to-all-done
  30.9 23.8 %all_to_all.30.x_ref = bf16[8,3,32,1024]{3,2,1,0:T(8,128)(2,1)S(1)} all-to-all(bf16[8,3,32,1024]{3,2,1,0:T(8,128)(2,1)S(1)} %broadcast_in_dim.14), channel_id=1, replica_groups=mesh['xh'=2,'z'=16,'y'=4,'xl'=2,'core'=2] {'xh','y'}, dimensions={0} | all-to-all | bytes 3145728 | tf_op jit(solution)/shard_map/all_to_all | solution.py:31
  54.6 0.6 shard_map.110
  55.2 8.5 %collective-permute-start = (f32[3,256,128]{2,1,0:T(8,128)S(1)}, f32[3,256,128]{2,1,0:T(8,128)S(1)}, u32[]{:S(2)}, u32[]{:S(2)}) collective-permute-start(f32[3,256,128]{2,1,0:T(8,128)S(1)} %shard_map.110), channel_id=1, source_target_pairs={{0,1},{1,0},{2,3},{3,2},{4,5},{5,4},{6,7},{7,6},{8,9},{9,8},{10,11... | collective-permute-start | bytes 1179656 | tf_op jit(solution)/shard_map/ppermute | solution.py:20
  63.7 1.3 collective-permute-done
  65.0 2.3 %collective-permute-start.1 = (bf16[3,256,128]{2,1,0:T(8,128)(2,1)S(1)}, bf16[3,256,128]{2,1,0:T(8,128)(2,1)S(1)}, u32[]{:S(2)}, u32[]{:S(2)}) collective-permute-start(bf16[3,256,128]{2,1,0:T(8,128)(2,1)S(1)} %add_convert_fusion.1.mine_ref), channel_id=1, source_target_pairs={{0,2},{2,0},{1,3},{3,1},{4,6},{6,4},{5,7},{7,5},{8,10},{10,8},{9,1... | collective-permute-start | bytes 589832 | tf_op jit(solution)/shard_map/ppermute | solution.py:20
  67.3 5.7 %collective-permute-done.1.theirs_ref = bf16[3,256,128]{2,1,0:T(8,128)(2,1)S(1)} collective-permute-done((bf16[3,256,128]{2,1,0:T(8,128)(2,1)S(1)}, bf16[3,256,128]{2,1,0:T(8,128)(2,1)S(1)}, u32[]{:S(2)}, u32[]{:S(2)}) %collective-permute-start.1) | collective-permute-done | bytes 196640 | tf_op jit(solution)/shard_map/ppermute | solution.py:20
  73.0 1.0 shard_map.111
  74.0 24.1 %all_to_all.31 = bf16[8,3,32,1024]{3,2,1,0:T(8,128)(2,1)} all-to-all(bf16[8,3,32,1024]{3,2,1,0:T(8,128)(2,1)S(1)} %get-tuple-element.17), channel_id=1, replica_groups=mesh['xh'=2,'z'=16,'y'=4,'xl'=2,'core'=2] {'xh','y'}, dimensions={0} | all-to-all | bytes 3145728 | tf_op jit(solution)/shard_map/all_to_all | solution.py:38
  98.1 2.4 %reduce_sum.21 = bf16[3,32,1024]{2,1,0:T(8,128)(2,1)} reduce(bf16[8,3,32,1024]{3,2,1,0:T(8,128)(2,1)} %all_to_all.31, bf16[]{:T(256)} %constant.26.clone.1), dimensions={0}, to_apply=%region_8.0 | reduce | flops 688128 | bytes 1769474 | tf_op jit(solution)/shard_map/reduce_sum | solution.py:39
  100.5 1.7 reshape.40
  102.2 1.1 copy.24
  103.3 22.9 %all_to_all.32 = bf16[16,3,2,1024]{3,2,1,0:T(2,128)(2,1)S(1)} all-to-all(bf16[16,3,2,1024]{3,2,1,0:T(2,128)(2,1)S(1)} %copy.24), channel_id=1, replica_groups=mesh['xh'=2,'z'=16,'y'=4,'xl'=2,'core'=2] {'z'}, dimensions={0} | all-to-all | bytes 393216 | tf_op jit(solution)/shard_map/all_to_all | solution.py:41
  126.4 1.3 subtract_convert_fusion
  127.8 19.1 %all_to_all.33 = bf16[16,3,2,1024]{3,2,1,0:T(2,128)(2,1)S(1)} all-to-all(bf16[16,3,2,1024]{3,2,1,0:T(2,128)(2,1)S(1)} %broadcast_in_dim.15), channel_id=1, replica_groups=mesh['xh'=2,'z'=16,'y'=4,'xl'=2,'core'=2] {'z'}, dimensions={0} | all-to-all | bytes 393216 | tf_op jit(solution)/shard_map/all_to_all | solution.py:25
  146.9 0.8 copy.25
  147.7 1.7 broadcast_in_dim.16
  149.4 1.1 broadcast_in_dim.17
  150.5 19.8 %all_to_all.34.errors_ref = bf16[8,3,32,1024]{3,2,1,0:T(8,128)(2,1)S(1)} all-to-all(bf16[8,3,32,1024]{3,2,1,0:T(8,128)(2,1)S(1)} %broadcast_in_dim.17), channel_id=1, replica_groups=mesh['xh'=2,'z'=16,'y'=4,'xl'=2,'core'=2] {'xh','y'}, dimensions={0} | all-to-all | bytes 3145728 | tf_op jit(solution)/shard_map/all_to_all | solution.py:31
  170.3 1.0 shard_map.112
  171.2 9.6 %collective-permute-start.2 = (f32[3,256,128]{2,1,0:T(8,128)S(1)}, f32[3,256,128]{2,1,0:T(8,128)S(1)}, u32[]{:S(2)}, u32[]{:S(2)}) collective-permute-start(f32[3,256,128]{2,1,0:T(8,128)S(1)} %shard_map.112), channel_id=1, source_target_pairs={{0,1},{1,0},{2,3},{3,2},{4,5},{5,4},{6,7},{7,6},{8,9},{9,8},{10,11... | collective-permute-start | bytes 1179656 | tf_op jit(solution)/shard_map/ppermute | solution.py:20
  180.9 1.3 collective-permute-done.2
  182.3 2.2 %collective-permute-start.3 = (bf16[3,256,128]{2,1,0:T(8,128)(2,1)S(1)}, bf16[3,256,128]{2,1,0:T(8,128)(2,1)S(1)}, u32[]{:S(2)}, u32[]{:S(2)}) collective-permute-start(bf16[3,256,128]{2,1,0:T(8,128)(2,1)S(1)} %add_convert_fusion.mine_ref), channel_id=1, source_target_pairs={{0,2},{2,0},{1,3},{3,1},{4,6},{6,4},{5,7},{7,5},{8,10},{10,8},{9,1... | collective-permute-start | bytes 589832 | tf_op jit(solution)/shard_map/ppermute | solution.py:20
  184.5 1.8 shard_map.114
  186.3 4.0 %collective-permute-done.3.theirs_ref = bf16[3,256,128]{2,1,0:T(8,128)(2,1)S(1)} collective-permute-done((bf16[3,256,128]{2,1,0:T(8,128)(2,1)S(1)}, bf16[3,256,128]{2,1,0:T(8,128)(2,1)S(1)}, u32[]{:S(2)}, u32[]{:S(2)}) %collective-permute-start.3) | collective-permute-done | bytes 196640 | tf_op jit(solution)/shard_map/ppermute | solution.py:20
  190.3 1.5 shard_map.113
  (17 shorter events, 1.0 us)
Async XLA Ops:
  2.1 28.3 %all-to-all-start = ((bf16[16,3,2,1024]{3,2,1,0:T(2,128)(2,1)}), bf16[16,3,2,1024]{3,2,1,0:T(2,128)(2,1)S(1)}, u32[]{:S(2)}, u32[]{:S(2)}) async-start(bf16[16,3,2,1024]{3,2,1,0:T(2,128)(2,1)} %broadcast_in_dim.12), calls=%async_computation | async-start | bytes 393216 | tf_op jit(solution)/shard_map/all_to_all | solution.py:25
  30.8 23.8 %copy-start.1 = (bf16[3,1024,128]{2,1,0:T(8,128)(2,1)S(1)}, bf16[3,1024,128]{2,1,0:T(8,128)(2,1)}, u32[]{:S(2)}) copy-start(bf16[3,1024,128]{2,1,0:T(8,128)(2,1)} %weight_ref.3) | copy-start | bytes 2359300
  54.6 18.4 %copy-start = (bf16[6,128,1024]{2,1,0:T(8,128)(2,1)S(1)}, bf16[6,128,1024]{2,1,0:T(8,128)(2,1)}, u32[]{:S(2)}) copy-start(bf16[6,128,1024]{2,1,0:T(8,128)(2,1)} %weight_ref.5) | copy-start | bytes 4718596
  54.6 18.4 %copy-start.2 = (f32[3,128]{1,0:T(4,128)S(1)}, f32[3,128]{1,0:T(4,128)}, u32[]{:S(2)}) copy-start(f32[3,128]{1,0:T(4,128)} %bias_ref.1) | copy-start | bytes 4612
  55.2 9.8 %collective-permute-start = (f32[3,256,128]{2,1,0:T(8,128)S(1)}, f32[3,256,128]{2,1,0:T(8,128)S(1)}, u32[]{:S(2)}, u32[]{:S(2)}) collective-permute-start(f32[3,256,128]{2,1,0:T(8,128)S(1)} %shard_map.110), channel_id=1, source_target_pairs={{0,1},{1,0},{2,3},{3,2},{4,5},{5,4},{6,7},{7,6},{8,9},{9,8},{10,11... | collective-permute-start | bytes 1179656 | tf_op jit(solution)/shard_map/ppermute | solution.py:20
  65.0 8.0 %collective-permute-start.1 = (bf16[3,256,128]{2,1,0:T(8,128)(2,1)S(1)}, bf16[3,256,128]{2,1,0:T(8,128)(2,1)S(1)}, u32[]{:S(2)}, u32[]{:S(2)}) collective-permute-start(bf16[3,256,128]{2,1,0:T(8,128)(2,1)S(1)} %add_convert_fusion.1.mine_ref), channel_id=1, source_target_pairs={{0,2},{2,0},{1,3},{3,1},{4,6},{6,4},{5,7},{7,5},{8,10},{10,8},{9,1... | collective-permute-start | bytes 589832 | tf_op jit(solution)/shard_map/ppermute | solution.py:20
  98.1 28.2 %copy-start.3 = (f32[3,1024]{1,0:T(4,128)S(1)}, f32[3,1024]{1,0:T(4,128)}, u32[]{:S(2)}) copy-start(f32[3,1024]{1,0:T(4,128)} %param.13) | copy-start | bytes 36868
  171.2 11.0 %collective-permute-start.2 = (f32[3,256,128]{2,1,0:T(8,128)S(1)}, f32[3,256,128]{2,1,0:T(8,128)S(1)}, u32[]{:S(2)}, u32[]{:S(2)}) collective-permute-start(f32[3,256,128]{2,1,0:T(8,128)S(1)} %shard_map.112), channel_id=1, source_target_pairs={{0,1},{1,0},{2,3},{3,2},{4,5},{5,4},{6,7},{7,6},{8,9},{9,8},{10,11... | collective-permute-start | bytes 1179656 | tf_op jit(solution)/shard_map/ppermute | solution.py:20
  182.3 8.0 %collective-permute-start.3 = (bf16[3,256,128]{2,1,0:T(8,128)(2,1)S(1)}, bf16[3,256,128]{2,1,0:T(8,128)(2,1)S(1)}, u32[]{:S(2)}, u32[]{:S(2)}) collective-permute-start(bf16[3,256,128]{2,1,0:T(8,128)(2,1)S(1)} %add_convert_fusion.mine_ref), channel_id=1, source_target_pairs={{0,2},{2,0},{1,3},{3,1},{4,6},{6,4},{5,7},{7,5},{8,10},{10,8},{9,1... | collective-permute-start | bytes 589832 | tf_op jit(solution)/shard_map/ppermute | solution.py:20

commit v5 on v4

--- a/solution.py
+++ b/solution.py
@@ -9,6 +9,7 @@
 TOK = ("xl", "core")
 PLANE = ("xh", "y")
 XH, Z, Y, XL, CORE = 2, 16, 4, 2, 2
+VMEM_BYTES = 8 << 20
 bf16, f32 = jnp.bfloat16, jnp.float32
 
 
@@ -21,25 +22,53 @@
 
 
 def gather_z(home):
-    layers, rows, width = home.shape
-    return lax.all_to_all(jnp.broadcast_to(home[None], (Z, layers, rows, width)), "z", 0, 0)
+    return lax.all_to_all(jnp.broadcast_to(home[None], (Z,) + home.shape), "z", 0, 0)
+
+
+def spread_kernel(along_z_ref, out_ref, rows_ref):
+    columns, layers, rows, _ = along_z_ref.shape
+    for l in range(layers):
+        for z in range(columns):
+            rows_ref[z * rows : (z + 1) * rows] = along_z_ref[z, l].astype(f32)
+        block = rows_ref[...].astype(bf16)
+        for p in range(out_ref.shape[0]):
+            out_ref[p, l] = block
 
 
 def gather_plane(along_z):
-    _, layers, rows, width = along_z.shape
-    block = along_z.transpose(1, 0, 2, 3).reshape(1, layers, Z * rows, width)
-    return lax.all_to_all(
-        jnp.broadcast_to(block, (XH * Y,) + block.shape[1:]), PLANE, 0, 0
-    )
-
-
-def scatter_tokens(sent):
-    planes, layers, rows, width = sent.shape
-    got = lax.all_to_all(sent, PLANE, 0, 0)
-    summed = jnp.sum(got.astype(f32), axis=0).astype(bf16)
-    blocks = summed.reshape(layers, Z, rows // Z, width).transpose(1, 0, 2, 3)
-    got = lax.all_to_all(blocks, "z", 0, 0)
-    return jnp.sum(got.astype(f32), axis=0)
+    columns, layers, rows, width = along_z.shape
+    (block,) = call(
+        spread_kernel,
+        (along_z,),
+        [((XH * Y, layers, columns * rows, width), bf16)],
+        along_z.size,
+        [pltpu.VMEM((columns * rows, width), f32)],
+    )
+    return lax.all_to_all(block, PLANE, 0, 0)
+
+
+def plane_sum_kernel(got_ref, out_ref, rows_ref):
+    columns, layers, rows, _ = out_ref.shape
+    for l in range(layers):
+        total = got_ref[0, l].astype(f32)
+        for p in range(1, got_ref.shape[0]):
+            total = total + got_ref[p, l].astype(f32)
+        rows_ref[...] = total
+        for z in range(columns):
+            out_ref[z, l] = rows_ref[z * rows : (z + 1) * rows].astype(bf16)
+
+
+def errors_kernel(got_ref, bias_ref, targets_ref, recon_ref, out_ref):
+    columns, layers = got_ref.shape[:2]
+    for l in range(layers):
+        total = got_ref[0, l].astype(f32)
+        for z in range(1, columns):
+            total = total + got_ref[z, l].astype(f32)
+        total = total + bias_ref[l : l + 1]
+        recon_ref[l] = total.astype(bf16)
+        errors = (total - targets_ref[l].astype(f32)).astype(bf16)
+        for z in range(columns):
+            out_ref[z, l] = errors
 
 
 def rows_of(ref, layer):
@@ -105,14 +134,15 @@
         ).astype(bf16)
 
 
-def call(kernel, args, outs, flops):
+def call(kernel, args, outs, flops, scratch=()):
     size = sum(a.size * a.dtype.itemsize for a in args)
     return pl.pallas_call(
         kernel,
         out_shape=[jax.ShapeDtypeStruct(shape, kind) for shape, kind in outs],
         in_specs=[pl.BlockSpec(memory_space=pltpu.VMEM) for _ in args],
         out_specs=[pl.BlockSpec(memory_space=pltpu.VMEM) for _ in outs],
-        compiler_params=pltpu.CompilerParams(vmem_limit_bytes=24 << 20),
+        scratch_shapes=list(scratch),
+        compiler_params=pltpu.CompilerParams(vmem_limit_bytes=VMEM_BYTES),
         cost_estimate=pl.CostEstimate(flops=flops, bytes_accessed=2 * size, transcendentals=0),
     )(*args)
 
@@ -135,8 +165,7 @@
     for offset in range(0, picks, 8):
         matches = order[:, :, offset : offset + 8, None] == feature_ids
         chosen = jnp.logical_or(chosen, jnp.any(matches, axis=2))
-    along_z, chosen = lax.optimization_barrier((along_z, chosen.astype(bf16)))
-    gathered = gather_plane(along_z)
+    gathered, chosen = lax.optimization_barrier((gather_plane(along_z), chosen.astype(bf16)))
 
     planes, rows = XH * Y, tokens // (XH * Y)
     narrow = (layers, tokens, width_here)
@@ -151,10 +180,21 @@
         [(narrow, bf16), ((planes, layers, rows, model), bf16)],
         decoder_weight.shape[0] * work,
     )
-    summed = scatter_tokens(sent) + decoder_bias[:, None, :]
-    recon = summed.astype(bf16)
-    errors_home = (summed - targets.astype(f32)).astype(bf16)
-    errors_got = gather_plane(gather_z(errors_home))
+    columns = (Z, layers, rows // Z, model)
+    (blocks,) = call(
+        plane_sum_kernel,
+        (lax.all_to_all(sent, PLANE, 0, 0),),
+        [(columns, bf16)],
+        sent.size,
+        [pltpu.VMEM((rows, model), f32)],
+    )
+    recon, errors_home = call(
+        errors_kernel,
+        (lax.all_to_all(blocks, "z", 0, 0), decoder_bias, targets),
+        [(targets.shape, bf16), (columns, bf16)],
+        blocks.size,
+    )
+    errors_got = gather_plane(lax.all_to_all(errors_home, "z", 0, 0))
     (partial_grad,) = call(
         grad_kernel,
         (errors_got, decoder_weight),

time: 193 us -> 183 us (0.948)
  blocking collectives: 110 us -> 84.8 us
  waiting for transfers between devices: 13 us -> 26.1 us
  starting transfers between devices: 38.4 us -> 45.4 us
  local copies, waits for them, and re-layouts: 10.4 us -> 5.68 us
  other arithmetic: 13.8 us -> 10.9 us
  Pallas kernels: 5.84 us -> 8.45 us
    all_to_all x5 -> x4, blocking collectives: 110 us -> 84.8 us  [the longest x1 24.4 us: body(): lax.all_to_all(sent, PLANE, 0, 0)]
    all_to_all x1 -> x2, waiting for transfers between devices: 0.71 us -> 14 us  [the longest x1 9.47 us: gather_z(): lax.all_to_all(jnp.broadcast_to(home[None], (Z,) + home.shape), 'z', 0, 0)]
    all_to_all x1 -> x2, starting transfers between devices: 15.7 us -> 22.4 us  [the longest x1 15.7 us: gather_z(): lax.all_to_all(jnp.broadcast_to(home[None], (Z,) + home.shape), 'z', 0, 0)]
    broadcast_in_dim x6 -> x1, local copies, waits for them, and re-layouts: 4.64 us -> 1.49 us  [gather_z(): jnp.broadcast_to(home[None], (Z,) + home.shape)]
    pallas_call x5 -> x9, Pallas kernels: 5.84 us -> 8.45 us  [call(): pl.pallas_call(kernel, out_shape=[jax.ShapeDtypeStruct(shape, kind) for s...]
    reduce_sum x2 -> x0, other arithmetic: 2.59 us -> none  [the longest x1 2.42 us: scatter_tokens(): summed = jnp.sum(got.astype(f32), axis=0).astype(bf16)]
    transpose x3 -> x0, local copies, waits for them, and re-layouts: 2.01 us -> none  [the longest x1 1.06 us: scatter_tokens(): blocks = summed.reshape(layers, Z, rows // Z, width).transpose(1, 0, 2, 3)]
  transfers between devices with their start and end apart: 5 -> 6, of which waited for: 5 -> 6; matrix products, arithmetic and copies ran while one was open for 6% -> 8% of each run, Pallas kernels for 1% -> 1%
where the time goes in v5:
time: 183 us; the launch traced here: 182 us
  blocking collectives  84.8 us (46%)
  starting transfers between devices  45.4 us (25%)
  waiting for transfers between devices  26.1 us (14%)
  other arithmetic  10.9 us (6%)
  Pallas kernels  8.45 us (5%)
  local copies, waits for them, and re-layouts  5.68 us (3%)
    all_to_all x1, blocking collectives, body(): lax.all_to_all(sent, PLANE, 0, 0)  24.4 us
    ppermute x4, starting transfers between devices, swap(): return lax.ppermute(x, axis, [(0, 1), (1, 0)])  23 us
    all_to_all x1, blocking collectives, gather_plane(): return lax.all_to_all(block, PLANE, 0, 0)  21.3 us
    all_to_all x1, blocking collectives, body(): lax.all_to_all(blocks, 'z', 0, 0)  20.9 us
    all_to_all x1, blocking collectives, body(): errors_got = gather_plane(lax.all_to_all(errors_home, 'z', 0, 0))  18.2 us
    all_to_all x1, starting transfers between devices, gather_z(): lax.all_to_all(jnp.broadcast_to(home[None], (Z,) + home.shape), 'z', 0, 0)  15.7 us
    ppermute x4, waiting for transfers between devices, swap(): return lax.ppermute(x, axis, [(0, 1), (1, 0)])  12 us
    reduce_or x1, other arithmetic, body(): chosen = jnp.logical_or(chosen, jnp.any(matches, axis=2))  10.5 us
  transfers between devices with their start and end apart: 6, of which 6 were waited for; matrix products, arithmetic and copies ran while one was open for 8% of the time, Pallas kernels for 1%

profile of v5, /device:TPU:1, one launch (start us, length us, event | category | flops | bytes accessed | tf_op | source)
XLA Modules:
  0.0 182.0 jit_solution(4100407936461263907)
XLA Ops:
  0.6 1.5 broadcast_in_dim.2
  2.1 15.7 %all-to-all-start = ((bf16[16,3,2,1024]{3,2,1,0:T(2,128)(2,1)}), bf16[16,3,2,1024]{3,2,1,0:T(2,128)(2,1)S(1)}, u32[]{:S(2)}, u32[]{:S(2)}) async-start(bf16[16,3,2,1024]{3,2,1,0:T(2,128)(2,1)} %broadcast_in_dim.2), calls=%async_computation | async-start | bytes 393216 | tf_op jit(solution)/shard_map/all_to_all | solution.py:25
  17.9 1.1 copy.14
  19.0 0.2 copy.15
  19.2 1.8 fusion
  21.0 9.5 %all-to-all-done.along_z_ref = bf16[16,3,2,1024]{3,2,1,0:T(2,128)(2,1)S(1)} async-done(((bf16[16,3,2,1024]{3,2,1,0:T(2,128)(2,1)}), bf16[16,3,2,1024]{3,2,1,0:T(2,128)(2,1)S(1)}, u32[]{:S(2)}, u32[]{:S(2)}) %all-to-all-start) | async-done | bytes 196640 | tf_op jit(solution)/shard_map/all_to_all | solution.py:25
  30.4 1.4 shard_map.110
  31.8 6.7 %all-to-all-start.1 = ((bf16[8,3,32,1024]{3,2,1,0:T(8,128)(2,1)}), bf16[8,3,32,1024]{3,2,1,0:T(8,128)(2,1)S(1)}, u32[]{:S(2)}, u32[]{:S(2)}) async-start(bf16[8,3,32,1024]{3,2,1,0:T(8,128)(2,1)} %shard_map.110), calls=%async_computation.1 | async-start | bytes 3145728 | tf_op jit(solution)/shard_map/all_to_all | solution.py:47
  38.4 10.5 %compare_reduce_fusion.6 = (pred[3,256,128]{2,1,0:T(8,128)(4,1)S(1)}, pred[3,256,128]{2,1,0:T(8,128)(4,1)S(1)}, pred[3,256,128]{2,1,0:T(8,128)(4,1)S(1)}, pred[3...) fusion(s32[3,256,8]{2,1,0:T(8,128)} %get-tuple-element.44, ...), kind=kLoop, calls=%fused_computation.6 | loop fusion | flops 11796480 | bytes 983552 | tf_op jit(solution)/shard_map/reduce_or | solution.py:167
  49.0 0.2 or_convert_fusion.mask_ref
  49.2 4.6 %all-to-all-done.1.x_ref = bf16[8,3,32,1024]{3,2,1,0:T(8,128)(2,1)S(1)} async-done(((bf16[8,3,32,1024]{3,2,1,0:T(8,128)(2,1)}), bf16[8,3,32,1024]{3,2,1,0:T(8,128)(2,1)S(1)}, u32[]{:S(2)}, u32[]{:S(2)}) %all-to-all-start.1) | async-done | bytes 1572896 | tf_op jit(solution)/shard_map/all_to_all | solution.py:47
  53.8 1.1 copy-done.1
  55.0 0.6 shard_map.111
  55.5 8.5 %collective-permute-start = (f32[3,256,128]{2,1,0:T(8,128)S(1)}, f32[3,256,128]{2,1,0:T(8,128)S(1)}, u32[]{:S(2)}, u32[]{:S(2)}) collective-permute-start(f32[3,256,128]{2,1,0:T(8,128)S(1)} %shard_map.111), channel_id=1, source_target_pairs={{0,1},{1,0},{2,3},{3,2},{4,5},{5,4},{6,7},{7,6},{8,9},{9,8},{10,11... | collective-permute-start | bytes 1179656 | tf_op jit(solution)/shard_map/ppermute | solution.py:21
  64.1 1.3 collective-permute-done
  65.4 2.6 %collective-permute-start.1 = (bf16[3,256,128]{2,1,0:T(8,128)(2,1)S(1)}, bf16[3,256,128]{2,1,0:T(8,128)(2,1)S(1)}, u32[]{:S(2)}, u32[]{:S(2)}) collective-permute-start(bf16[3,256,128]{2,1,0:T(8,128)(2,1)S(1)} %add_convert_fusion.1.mine_ref), channel_id=1, source_target_pairs={{0,2},{2,0},{1,3},{3,1},{4,6},{6,4},{5,7},{7,5},{8,10},{10,8},{9,1... | collective-permute-start | bytes 589832 | tf_op jit(solution)/shard_map/ppermute | solution.py:21
  68.0 5.4 %collective-permute-done.1.theirs_ref = bf16[3,256,128]{2,1,0:T(8,128)(2,1)S(1)} collective-permute-done((bf16[3,256,128]{2,1,0:T(8,128)(2,1)S(1)}, bf16[3,256,128]{2,1,0:T(8,128)(2,1)S(1)}, u32[]{:S(2)}, u32[]{:S(2)}) %collective-permute-start.1) | collective-permute-done | bytes 196640 | tf_op jit(solution)/shard_map/ppermute | solution.py:21
  73.5 1.0 shard_map.112
  74.4 24.4 %all_to_all.30.got_ref = bf16[8,3,32,1024]{3,2,1,0:T(8,128)(2,1)S(1)} all-to-all(bf16[8,3,32,1024]{3,2,1,0:T(8,128)(2,1)S(1)} %get-tuple-element.19), channel_id=1, replica_groups=mesh['xh'=2,'z'=16,'y'=4,'xl'=2,'core'=2] {'xh','y'}, dimensions={0} | all-to-all | bytes 3145728 | tf_op jit(solution)/shard_map/all_to_all | solution.py:186
  98.8 0.3 shard_map.113
  99.2 20.9 %all_to_all.31.got_ref = bf16[16,3,2,1024]{3,2,1,0:T(2,128)(2,1)S(1)} all-to-all(bf16[16,3,2,1024]{3,2,1,0:T(2,128)(2,1)S(1)} %shard_map.113), channel_id=1, replica_groups=mesh['xh'=2,'z'=16,'y'=4,'xl'=2,'core'=2] {'z'}, dimensions={0} | all-to-all | bytes 393216 | tf_op jit(solution)/shard_map/all_to_all | solution.py:193
  120.1 0.7 shard_map.114
  120.8 18.2 %all_to_all.32.along_z_ref = bf16[16,3,2,1024]{3,2,1,0:T(2,128)(2,1)S(1)} all-to-all(bf16[16,3,2,1024]{3,2,1,0:T(2,128)(2,1)S(1)} %get-tuple-element.21), channel_id=1, replica_groups=mesh['xh'=2,'z'=16,'y'=4,'xl'=2,'core'=2] {'z'}, dimensions={0} | all-to-all | bytes 393216 | tf_op jit(solution)/shard_map/all_to_all | solution.py:197
  139.0 0.2 shard_map.115
  139.2 21.3 %all_to_all.33.errors_ref = bf16[8,3,32,1024]{3,2,1,0:T(8,128)(2,1)S(1)} all-to-all(bf16[8,3,32,1024]{3,2,1,0:T(8,128)(2,1)S(1)} %shard_map.115), channel_id=1, replica_groups=mesh['xh'=2,'z'=16,'y'=4,'xl'=2,'core'=2] {'xh','y'}, dimensions={0} | all-to-all | bytes 3145728 | tf_op jit(solution)/shard_map/all_to_all | solution.py:47
  160.5 1.0 shard_map.116
  161.5 9.6 %collective-permute-start.2 = (f32[3,256,128]{2,1,0:T(8,128)S(1)}, f32[3,256,128]{2,1,0:T(8,128)S(1)}, u32[]{:S(2)}, u32[]{:S(2)}) collective-permute-start(f32[3,256,128]{2,1,0:T(8,128)S(1)} %shard_map.116), channel_id=1, source_target_pairs={{0,1},{1,0},{2,3},{3,2},{4,5},{5,4},{6,7},{7,6},{8,9},{9,8},{10,11... | collective-permute-start | bytes 1179656 | tf_op jit(solution)/shard_map/ppermute | solution.py:21
  171.1 1.3 collective-permute-done.2
  172.5 2.2 %collective-permute-start.3 = (bf16[3,256,128]{2,1,0:T(8,128)(2,1)S(1)}, bf16[3,256,128]{2,1,0:T(8,128)(2,1)S(1)}, u32[]{:S(2)}, u32[]{:S(2)}) collective-permute-start(bf16[3,256,128]{2,1,0:T(8,128)(2,1)S(1)} %add_convert_fusion.mine_ref), channel_id=1, source_target_pairs={{0,2},{2,0},{1,3},{3,1},{4,6},{6,4},{5,7},{7,5},{8,10},{10,8},{9,1... | collective-permute-start | bytes 589832 | tf_op jit(solution)/shard_map/ppermute | solution.py:21
  174.7 1.8 shard_map.118
  176.5 4.0 %collective-permute-done.3.theirs_ref = bf16[3,256,128]{2,1,0:T(8,128)(2,1)S(1)} collective-permute-done((bf16[3,256,128]{2,1,0:T(8,128)(2,1)S(1)}, bf16[3,256,128]{2,1,0:T(8,128)(2,1)S(1)}, u32[]{:S(2)}, u32[]{:S(2)}) %collective-permute-start.3) | collective-permute-done | bytes 196640 | tf_op jit(solution)/shard_map/ppermute | solution.py:21
  180.5 1.5 shard_map.117
  (12 shorter events, 0.1 us)
Async XLA Ops:
  2.1 28.3 %all-to-all-start = ((bf16[16,3,2,1024]{3,2,1,0:T(2,128)(2,1)}), bf16[16,3,2,1024]{3,2,1,0:T(2,128)(2,1)S(1)}, u32[]{:S(2)}, u32[]{:S(2)}) async-start(bf16[16,3,2,1024]{3,2,1,0:T(2,128)(2,1)} %broadcast_in_dim.2), calls=%async_computation | async-start | bytes 393216 | tf_op jit(solution)/shard_map/all_to_all | solution.py:25
  31.8 22.0 %all-to-all-start.1 = ((bf16[8,3,32,1024]{3,2,1,0:T(8,128)(2,1)}), bf16[8,3,32,1024]{3,2,1,0:T(8,128)(2,1)S(1)}, u32[]{:S(2)}, u32[]{:S(2)}) async-start(bf16[8,3,32,1024]{3,2,1,0:T(8,128)(2,1)} %shard_map.110), calls=%async_computation.1 | async-start | bytes 3145728 | tf_op jit(solution)/shard_map/all_to_all | solution.py:47
  49.2 24.2 %copy-start = (bf16[6,128,1024]{2,1,0:T(8,128)(2,1)S(1)}, bf16[6,128,1024]{2,1,0:T(8,128)(2,1)}, u32[]{:S(2)}) copy-start(bf16[6,128,1024]{2,1,0:T(8,128)(2,1)} %weight_ref.5) | copy-start | bytes 4718596
  53.8 1.1 copy-start.1
  55.0 18.5 %copy-start.4 = (f32[3,128]{1,0:T(4,128)S(1)}, f32[3,128]{1,0:T(4,128)}, u32[]{:S(2)}) copy-start(f32[3,128]{1,0:T(4,128)} %bias_ref.2) | copy-start | bytes 4612
  55.5 9.9 %collective-permute-start = (f32[3,256,128]{2,1,0:T(8,128)S(1)}, f32[3,256,128]{2,1,0:T(8,128)S(1)}, u32[]{:S(2)}, u32[]{:S(2)}) collective-permute-start(f32[3,256,128]{2,1,0:T(8,128)S(1)} %shard_map.111), channel_id=1, source_target_pairs={{0,1},{1,0},{2,3},{3,2},{4,5},{5,4},{6,7},{7,6},{8,9},{9,8},{10,11... | collective-permute-start | bytes 1179656 | tf_op jit(solution)/shard_map/ppermute | solution.py:21
  65.4 8.0 %collective-permute-start.1 = (bf16[3,256,128]{2,1,0:T(8,128)(2,1)S(1)}, bf16[3,256,128]{2,1,0:T(8,128)(2,1)S(1)}, u32[]{:S(2)}, u32[]{:S(2)}) collective-permute-start(bf16[3,256,128]{2,1,0:T(8,128)(2,1)S(1)} %add_convert_fusion.1.mine_ref), channel_id=1, source_target_pairs={{0,2},{2,0},{1,3},{3,1},{4,6},{6,4},{5,7},{7,5},{8,10},{10,8},{9,1... | collective-permute-start | bytes 589832 | tf_op jit(solution)/shard_map/ppermute | solution.py:21
  98.8 21.3 %copy-start.2 = (f32[3,1024]{1,0:T(4,128)S(1)}, f32[3,1024]{1,0:T(4,128)}, u32[]{:S(2)}) copy-start(f32[3,1024]{1,0:T(4,128)} %bias_ref.3) | copy-start | bytes 36868
  98.8 21.3 %copy-start.3 = (bf16[3,2,1024]{2,1,0:T(2,128)(2,1)S(1)}, bf16[3,2,1024]{2,1,0:T(2,128)(2,1)}, u32[]{:S(2)}) copy-start(bf16[3,2,1024]{2,1,0:T(2,128)(2,1)} %targets_ref.1) | copy-start | bytes 36868
  161.5 11.0 %collective-permute-start.2 = (f32[3,256,128]{2,1,0:T(8,128)S(1)}, f32[3,256,128]{2,1,0:T(8,128)S(1)}, u32[]{:S(2)}, u32[]{:S(2)}) collective-permute-start(f32[3,256,128]{2,1,0:T(8,128)S(1)} %shard_map.116), channel_id=1, source_target_pairs={{0,1},{1,0},{2,3},{3,2},{4,5},{5,4},{6,7},{7,6},{8,9},{9,8},{10,11... | collective-permute-start | bytes 1179656 | tf_op jit(solution)/shard_map/ppermute | solution.py:21
  172.5 8.0 %collective-permute-start.3 = (bf16[3,256,128]{2,1,0:T(8,128)(2,1)S(1)}, bf16[3,256,128]{2,1,0:T(8,128)(2,1)S(1)}, u32[]{:S(2)}, u32[]{:S(2)}) collective-permute-start(bf16[3,256,128]{2,1,0:T(8,128)(2,1)S(1)} %add_convert_fusion.mine_ref), channel_id=1, source_target_pairs={{0,2},{2,0},{1,3},{3,1},{4,6},{6,4},{5,7},{7,5},{8,10},{10,8},{9,1... | collective-permute-start | bytes 589832 | tf_op jit(solution)/shard_map/ppermute | solution.py:21

commit v6 on v5

--- a/solution.py
+++ b/solution.py
@@ -21,8 +21,14 @@
     return lax.ppermute(x, axis, [(0, 1), (1, 0)])
 
 
+def copies_kernel(home_ref, out_ref):
+    for z in range(out_ref.shape[0]):
+        out_ref[z] = home_ref[...]
+
+
 def gather_z(home):
-    return lax.all_to_all(jnp.broadcast_to(home[None], (Z,) + home.shape), "z", 0, 0)
+    (copies,) = call(copies_kernel, (home,), [((Z,) + home.shape, bf16)], home.size)
+    return lax.all_to_all(copies, "z", 0, 0)
 
 
 def spread_kernel(along_z_ref, out_ref, rows_ref):
@@ -74,6 +80,20 @@
 def rows_of(ref, layer):
     block = ref[:, layer]
     return block.reshape(block.shape[0] * block.shape[1], block.shape[2])
+
+
+def mask_kernel(winners_ref, out_ref, marks_ref):
+    layers, picks, tokens = winners_ref.shape
+    features = out_ref.shape[2]
+    half = features // 2
+    for l in range(layers):
+        for h in range(0, features, half):
+            ids = h + lax.broadcasted_iota(jnp.int32, (half, tokens), 0)
+            marks = jnp.zeros((half, tokens), f32)
+            for k in range(picks):
+                marks = jnp.where(winners_ref[l, k : k + 1, :] == ids, 1.0, marks)
+            marks_ref[h : h + half] = marks
+        out_ref[l] = marks_ref[...].T.astype(bf16)
 
 
 def encode_kernel(x_ref, weight_ref, out_ref):
@@ -113,8 +133,10 @@
         out_ref[s] = grad_act
 
 
-def decoder_grad_kernel(act_ref, errors_ref, out_ref, bias_ref):
+def decoder_grad_kernel(act_ref, errors_ref, x_ref, out_ref, bias_ref, turned_ref):
     layers = act_ref.shape[0]
+    for l in range(layers):
+        turned_ref[l] = rows_of(x_ref, l).T
     for u in range(layers):
         errors = rows_of(errors_ref, u)
         bias_ref[u : u + 1] = jnp.sum(errors.astype(f32), axis=0, keepdims=True)
@@ -124,13 +146,13 @@
             ).astype(bf16)
 
 
-def encoder_grad_kernel(mine_ref, theirs_ref, mask_ref, x_ref, out_ref, bias_ref):
+def encoder_grad_kernel(mine_ref, theirs_ref, mask_ref, turned_ref, out_ref, bias_ref):
     for l in range(out_ref.shape[0]):
         grad_act = mine_ref[l].astype(f32) + theirs_ref[l].astype(f32)
         grad_pre = jnp.where(mask_ref[l] != 0, grad_act, 0.0).astype(bf16)
         bias_ref[l : l + 1] = jnp.sum(grad_pre.astype(f32), axis=0, keepdims=True)
-        out_ref[l] = lax.dot_general(
-            rows_of(x_ref, l), grad_pre, (((0,), (0,)), ((), ())), preferred_element_type=f32
+        out_ref[l] = jnp.dot(
+            turned_ref[l], grad_pre, preferred_element_type=f32
         ).astype(bf16)
 
 
@@ -158,14 +180,17 @@
 
     along_z = gather_z(layer_inputs)
 
-    order = winners.reshape(layers, XH, Z, Y, 2, picks).transpose(0, 1, 3, 2, 4, 5)
-    order = order.reshape(layers, tokens, picks)
-    feature_ids = lax.axis_index(FEAT) * width_here + jnp.arange(width_here, dtype=jnp.int32)
-    chosen = jnp.zeros((layers, tokens, width_here), jnp.bool_)
-    for offset in range(0, picks, 8):
-        matches = order[:, :, offset : offset + 8, None] == feature_ids
-        chosen = jnp.logical_or(chosen, jnp.any(matches, axis=2))
-    gathered, chosen = lax.optimization_barrier((gather_plane(along_z), chosen.astype(bf16)))
+    order = winners.reshape(layers, XH, Z, Y, 2, picks).transpose(0, 5, 1, 3, 2, 4)
+    order = order.reshape(layers, picks, tokens) - lax.axis_index(FEAT) * width_here
+    (chosen,) = call(
+        mask_kernel,
+        (order,),
+        [((layers, tokens, width_here), bf16)],
+        layers * picks * tokens * width_here,
+        [pltpu.VMEM((width_here, tokens), f32)],
+    )
+    along_z, chosen = lax.optimization_barrier((along_z, chosen))
+    gathered = gather_plane(along_z)
 
     planes, rows = XH * Y, tokens // (XH * Y)
     narrow = (layers, tokens, width_here)
@@ -203,15 +228,15 @@
     )
     both, errors_got = lax.optimization_barrier((swap(partial_grad, "core"), errors_got))
     mine = (partial_grad + both).astype(bf16)
-    decoder_grad, decoder_bias_grad = call(
+    decoder_grad, decoder_bias_grad, turned = call(
         decoder_grad_kernel,
-        (activation, errors_got),
-        [(decoder_weight.shape, bf16), ((layers, model), f32)],
+        (activation, errors_got, gathered),
+        [(decoder_weight.shape, bf16), ((layers, model), f32), ((layers, model, tokens), bf16)],
         decoder_weight.shape[0] * work,
     )
     encoder_grad, encoder_bias_grad = call(
         encoder_grad_kernel,
-        (mine, swap(mine, "xl"), chosen, gathered),
+        (mine, swap(mine, "xl"), chosen, turned),
         [((layers, model, width_here), bf16), ((layers, width_here), f32)],
         layers * work,
     )

time: 183 us -> 180 us (0.984)
  blocking collectives: 84.8 us -> 107 us
  other arithmetic: 10.9 us -> 0.12 us
  starting transfers between devices: 45.4 us -> 38.5 us
  waiting for transfers between devices: 26.1 us -> 21.1 us
  local copies, waits for them, and re-layouts: 5.68 us -> 2.15 us
    all_to_all x1 -> x2, blocking collectives: 21.3 us -> 43.6 us  [gather_plane(): return lax.all_to_all(block, PLANE, 0, 0)]
    reduce_or x1 -> x0, other arithmetic: 10.5 us -> none  [body(): chosen = jnp.logical_or(chosen, jnp.any(matches, axis=2))]
    all_to_all x2 -> x1, starting transfers between devices: 22.4 us -> 15.7 us  [gather_z(): return lax.all_to_all(copies, 'z', 0, 0)]
    all_to_all x2 -> x1, waiting for transfers between devices: 14 us -> 8.96 us  [gather_z(): return lax.all_to_all(copies, 'z', 0, 0)]
    pallas_call x9 -> x11, Pallas kernels: 8.45 us -> 10 us  [call(): pl.pallas_call(kernel, out_shape=[jax.ShapeDtypeStruct(shape, kind) for s...]
  transfers between devices with their start and end apart: 6 -> 5, of which waited for: 6 -> 5; matrix products, arithmetic and copies ran while one was open for 8% -> 1% of each run, Pallas kernels for 1% -> 2%
where the time goes in v6:
time: 180 us
  blocking collectives  107 us (59%)
  starting transfers between devices  38.5 us (21%)
  waiting for transfers between devices  21.1 us (12%)
  Pallas kernels  10 us (6%)
  local copies, waits for them, and re-layouts  2.15 us (1%)
    all_to_all x2, blocking collectives, gather_plane(): return lax.all_to_all(block, PLANE, 0, 0)  43.6 us
    all_to_all x1, blocking collectives, body(): lax.all_to_all(sent, PLANE, 0, 0)  23.2 us
    ppermute x4, starting transfers between devices, swap(): return lax.ppermute(x, axis, [(0, 1), (1, 0)])  22.8 us
    all_to_all x1, blocking collectives, body(): lax.all_to_all(blocks, 'z', 0, 0)  21 us
    all_to_all x1, blocking collectives, body(): errors_got = gather_plane(lax.all_to_all(errors_home, 'z', 0, 0))  19.1 us
    all_to_all x1, starting transfers between devices, gather_z(): return lax.all_to_all(copies, 'z', 0, 0)  15.7 us
    ppermute x4, waiting for transfers between devices, swap(): return lax.ppermute(x, axis, [(0, 1), (1, 0)])  12.1 us
    pallas_call x11, Pallas kernels, call(): pl.pallas_call(kernel, out_shape=[jax.ShapeDtypeStruct(shape, kind) for s...  10 us
  transfers between devices with their start and end apart: 5, of which 5 were waited for; matrix products, arithmetic and copies ran while one was open for 1% of the time, Pallas kernels for 2%

profile of v6, /device:TPU:1, one launch (start us, length us, event | category | flops | bytes accessed | tf_op | source)
XLA Modules:
  0.0 179.6 jit_solution(9742495902091093329)
XLA Ops:
  0.6 0.7 copy-done.4
  1.3 0.7 shard_map.110
  2.0 15.7 %all-to-all-start = ((bf16[16,3,2,1024]{3,2,1,0:T(2,128)(2,1)}), bf16[16,3,2,1024]{3,2,1,0:T(2,128)(2,1)S(1)}, u32[]{:S(2)}, u32[]{:S(2)}) async-start(bf16[16,3,2,1024]{3,2,1,0:T(2,128)(2,1)} %shard_map.110), calls=%async_computation | async-start | bytes 393216 | tf_op jit(solution)/shard_map/all_to_all | solution.py:31
  17.8 1.1 copy.13
  18.9 0.2 copy.14
  19.1 0.1 copy.15.winners_ref
  19.3 2.1 %shard_map.111.mask_ref = bf16[3,256,128]{2,1,0:T(8,128)(2,1)S(1)} custom-call(s32[3,64,256]{2,1,0:T(8,128)S(1)} %copy.15.winners_ref), custom_call_target="tpu_custom_call" | custom-call | flops 6291456 | bytes 393216 | tf_op jit(solution)/shard_map/pallas_call | solution.py:161
  21.4 9.0 %all-to-all-done.along_z_ref = bf16[16,3,2,1024]{3,2,1,0:T(2,128)(2,1)S(1)} async-done(((bf16[16,3,2,1024]{3,2,1,0:T(2,128)(2,1)}), bf16[16,3,2,1024]{3,2,1,0:T(2,128)(2,1)S(1)}, u32[]{:S(2)}, u32[]{:S(2)}) %all-to-all-start) | async-done | bytes 196640 | tf_op jit(solution)/shard_map/all_to_all | solution.py:31
  30.3 0.2 shard_map.112
  30.6 0.0 copy-start.1
  30.6 23.8 %all_to_all.30.x_ref = bf16[8,3,32,1024]{3,2,1,0:T(8,128)(2,1)S(1)} all-to-all(bf16[8,3,32,1024]{3,2,1,0:T(8,128)(2,1)S(1)} %shard_map.112), channel_id=1, replica_groups=mesh['xh'=2,'z'=16,'y'=4,'xl'=2,'core'=2] {'xh','y'}, dimensions={0} | all-to-all | bytes 3145728 | tf_op jit(solution)/shard_map/all_to_all | solution.py:53
  54.3 0.6 shard_map.113
  54.9 8.5 %collective-permute-start = (f32[3,256,128]{2,1,0:T(8,128)S(1)}, f32[3,256,128]{2,1,0:T(8,128)S(1)}, u32[]{:S(2)}, u32[]{:S(2)}) collective-permute-start(f32[3,256,128]{2,1,0:T(8,128)S(1)} %shard_map.113), channel_id=1, source_target_pairs={{0,1},{1,0},{2,3},{3,2},{4,5},{5,4},{6,7},{7,6},{8,9},{9,8},{10,11... | collective-permute-start | bytes 1179656 | tf_op jit(solution)/shard_map/ppermute | solution.py:21
  63.4 1.3 collective-permute-done
  64.7 2.3 %collective-permute-start.1 = (bf16[3,256,128]{2,1,0:T(8,128)(2,1)S(1)}, bf16[3,256,128]{2,1,0:T(8,128)(2,1)S(1)}, u32[]{:S(2)}, u32[]{:S(2)}) collective-permute-start(bf16[3,256,128]{2,1,0:T(8,128)(2,1)S(1)} %add_convert_fusion.1.mine_ref), channel_id=1, source_target_pairs={{0,2},{2,0},{1,3},{3,1},{4,6},{6,4},{5,7},{7,5},{8,10},{10,8},{9,1... | collective-permute-start | bytes 589832 | tf_op jit(solution)/shard_map/ppermute | solution.py:21
  67.1 5.7 %collective-permute-done.1.theirs_ref = bf16[3,256,128]{2,1,0:T(8,128)(2,1)S(1)} collective-permute-done((bf16[3,256,128]{2,1,0:T(8,128)(2,1)S(1)}, bf16[3,256,128]{2,1,0:T(8,128)(2,1)S(1)}, u32[]{:S(2)}, u32[]{:S(2)}) %collective-permute-start.1) | collective-permute-done | bytes 196640 | tf_op jit(solution)/shard_map/ppermute | solution.py:21
  72.8 1.0 shard_map.114
  73.7 23.2 %all_to_all.31.got_ref = bf16[8,3,32,1024]{3,2,1,0:T(8,128)(2,1)S(1)} all-to-all(bf16[8,3,32,1024]{3,2,1,0:T(8,128)(2,1)S(1)} %get-tuple-element.20), channel_id=1, replica_groups=mesh['xh'=2,'z'=16,'y'=4,'xl'=2,'core'=2] {'xh','y'}, dimensions={0} | all-to-all | bytes 3145728 | tf_op jit(solution)/shard_map/all_to_all | solution.py:211
  97.0 0.3 shard_map.115
  97.3 21.0 %all_to_all.32.got_ref = bf16[16,3,2,1024]{3,2,1,0:T(2,128)(2,1)S(1)} all-to-all(bf16[16,3,2,1024]{3,2,1,0:T(2,128)(2,1)S(1)} %shard_map.115), channel_id=1, replica_groups=mesh['xh'=2,'z'=16,'y'=4,'xl'=2,'core'=2] {'z'}, dimensions={0} | all-to-all | bytes 393216 | tf_op jit(solution)/shard_map/all_to_all | solution.py:218
  118.3 0.7 shard_map.116
  118.9 19.1 %all_to_all.33.along_z_ref = bf16[16,3,2,1024]{3,2,1,0:T(2,128)(2,1)S(1)} all-to-all(bf16[16,3,2,1024]{3,2,1,0:T(2,128)(2,1)S(1)} %get-tuple-element.22), channel_id=1, replica_groups=mesh['xh'=2,'z'=16,'y'=4,'xl'=2,'core'=2] {'z'}, dimensions={0} | all-to-all | bytes 393216 | tf_op jit(solution)/shard_map/all_to_all | solution.py:222
  138.1 0.2 shard_map.117
  138.3 19.9 %all_to_all.34.errors_ref = bf16[8,3,32,1024]{3,2,1,0:T(8,128)(2,1)S(1)} all-to-all(bf16[8,3,32,1024]{3,2,1,0:T(8,128)(2,1)S(1)} %shard_map.117), channel_id=1, replica_groups=mesh['xh'=2,'z'=16,'y'=4,'xl'=2,'core'=2] {'xh','y'}, dimensions={0} | all-to-all | bytes 3145728 | tf_op jit(solution)/shard_map/all_to_all | solution.py:53
  158.2 1.0 shard_map.118
  159.1 9.6 %collective-permute-start.2 = (f32[3,256,128]{2,1,0:T(8,128)S(1)}, f32[3,256,128]{2,1,0:T(8,128)S(1)}, u32[]{:S(2)}, u32[]{:S(2)}) collective-permute-start(f32[3,256,128]{2,1,0:T(8,128)S(1)} %shard_map.118), channel_id=1, source_target_pairs={{0,1},{1,0},{2,3},{3,2},{4,5},{5,4},{6,7},{7,6},{8,9},{9,8},{10,11... | collective-permute-start | bytes 1179656 | tf_op jit(solution)/shard_map/ppermute | solution.py:21
  168.8 1.3 collective-permute-done.2
  170.1 0.1 add_convert_fusion.mine_ref
  170.2 2.4 %collective-permute-start.3 = (bf16[3,256,128]{2,1,0:T(8,128)(2,1)S(1)}, bf16[3,256,128]{2,1,0:T(8,128)(2,1)S(1)}, u32[]{:S(2)}, u32[]{:S(2)}) collective-permute-start(bf16[3,256,128]{2,1,0:T(8,128)(2,1)S(1)} %add_convert_fusion.mine_ref), channel_id=1, source_target_pairs={{0,2},{2,0},{1,3},{3,1},{4,6},{6,4},{5,7},{7,5},{8,10},{10,8},{9,1... | collective-permute-start | bytes 589832 | tf_op jit(solution)/shard_map/ppermute | solution.py:21
  172.6 1.8 %shard_map.119 = (bf16[6,128,1024]{2,1,0:T(8,128)(2,1)}, f32[3,1024]{1,0:T(4,128)}, bf16[3,1024,256]{2,1,0:T(8,128)(2,1)S(1)}) custom-call(bf16[3,256,128]{2,1,0:T(8,128)(2,1)S(1)} %get-tuple-element.24.act_ref, bf16[8,3,32,1024]{3,2,1,0:T(8,128)(2,1)S(1)} %all_to_all.34.errors_ref, bf16[8,3,32,1024]{3,2,1,0:T(8,128)(2,1)S(1)} %all_to_all.30.x_ref), custom_call_target="tpu_custom_call" | custom-call | flops 402653184 | bytes 6684672 | tf_op jit(solution)/shard_map/pallas_call | solution.py:161
  174.4 3.8 %collective-permute-done.3.theirs_ref = bf16[3,256,128]{2,1,0:T(8,128)(2,1)S(1)} collective-permute-done((bf16[3,256,128]{2,1,0:T(8,128)(2,1)S(1)}, bf16[3,256,128]{2,1,0:T(8,128)(2,1)S(1)}, u32[]{:S(2)}, u32[]{:S(2)}) %collective-permute-start.3) | collective-permute-done | bytes 196640 | tf_op jit(solution)/shard_map/ppermute | solution.py:21
  178.2 1.5 shard_map.120
  (12 shorter events, 0.1 us)
Async XLA Ops:
  0.6 0.7 copy-start.4
  2.0 28.3 %all-to-all-start = ((bf16[16,3,2,1024]{3,2,1,0:T(2,128)(2,1)}), bf16[16,3,2,1024]{3,2,1,0:T(2,128)(2,1)S(1)}, u32[]{:S(2)}, u32[]{:S(2)}) async-start(bf16[16,3,2,1024]{3,2,1,0:T(2,128)(2,1)} %shard_map.110), calls=%async_computation | async-start | bytes 393216 | tf_op jit(solution)/shard_map/all_to_all | solution.py:31
  30.6 23.8 %copy-start.1 = (bf16[3,1024,128]{2,1,0:T(8,128)(2,1)S(1)}, bf16[3,1024,128]{2,1,0:T(8,128)(2,1)}, u32[]{:S(2)}) copy-start(bf16[3,1024,128]{2,1,0:T(8,128)(2,1)} %weight_ref.3) | copy-start | bytes 2359300
  54.3 18.4 %copy-start = (bf16[6,128,1024]{2,1,0:T(8,128)(2,1)S(1)}, bf16[6,128,1024]{2,1,0:T(8,128)(2,1)}, u32[]{:S(2)}) copy-start(bf16[6,128,1024]{2,1,0:T(8,128)(2,1)} %weight_ref.5) | copy-start | bytes 4718596
  54.3 18.4 %copy-start.5 = (f32[3,128]{1,0:T(4,128)S(1)}, f32[3,128]{1,0:T(4,128)}, u32[]{:S(2)}) copy-start(f32[3,128]{1,0:T(4,128)} %bias_ref.2) | copy-start | bytes 4612
  54.9 9.8 %collective-permute-start = (f32[3,256,128]{2,1,0:T(8,128)S(1)}, f32[3,256,128]{2,1,0:T(8,128)S(1)}, u32[]{:S(2)}, u32[]{:S(2)}) collective-permute-start(f32[3,256,128]{2,1,0:T(8,128)S(1)} %shard_map.113), channel_id=1, source_target_pairs={{0,1},{1,0},{2,3},{3,2},{4,5},{5,4},{6,7},{7,6},{8,9},{9,8},{10,11... | collective-permute-start | bytes 1179656 | tf_op jit(solution)/shard_map/ppermute | solution.py:21
  64.7 8.0 %collective-permute-start.1 = (bf16[3,256,128]{2,1,0:T(8,128)(2,1)S(1)}, bf16[3,256,128]{2,1,0:T(8,128)(2,1)S(1)}, u32[]{:S(2)}, u32[]{:S(2)}) collective-permute-start(bf16[3,256,128]{2,1,0:T(8,128)(2,1)S(1)} %add_convert_fusion.1.mine_ref), channel_id=1, source_target_pairs={{0,2},{2,0},{1,3},{3,1},{4,6},{6,4},{5,7},{7,5},{8,10},{10,8},{9,1... | collective-permute-start | bytes 589832 | tf_op jit(solution)/shard_map/ppermute | solution.py:21
  97.0 21.3 %copy-start.2 = (f32[3,1024]{1,0:T(4,128)S(1)}, f32[3,1024]{1,0:T(4,128)}, u32[]{:S(2)}) copy-start(f32[3,1024]{1,0:T(4,128)} %bias_ref.3) | copy-start | bytes 36868
  97.0 21.3 %copy-start.3 = (bf16[3,2,1024]{2,1,0:T(2,128)(2,1)S(1)}, bf16[3,2,1024]{2,1,0:T(2,128)(2,1)}, u32[]{:S(2)}) copy-start(bf16[3,2,1024]{2,1,0:T(2,128)(2,1)} %targets_ref.1) | copy-start | bytes 36868
  159.1 11.0 %collective-permute-start.2 = (f32[3,256,128]{2,1,0:T(8,128)S(1)}, f32[3,256,128]{2,1,0:T(8,128)S(1)}, u32[]{:S(2)}, u32[]{:S(2)}) collective-permute-start(f32[3,256,128]{2,1,0:T(8,128)S(1)} %shard_map.118), channel_id=1, source_target_pairs={{0,1},{1,0},{2,3},{3,2},{4,5},{5,4},{6,7},{7,6},{8,9},{9,8},{10,11... | collective-permute-start | bytes 1179656 | tf_op jit(solution)/shard_map/ppermute | solution.py:21
  170.2 8.0 %collective-permute-start.3 = (bf16[3,256,128]{2,1,0:T(8,128)(2,1)S(1)}, bf16[3,256,128]{2,1,0:T(8,128)(2,1)S(1)}, u32[]{:S(2)}, u32[]{:S(2)}) collective-permute-start(bf16[3,256,128]{2,1,0:T(8,128)(2,1)S(1)} %add_convert_fusion.mine_ref), channel_id=1, source_target_pairs={{0,2},{2,0},{1,3},{3,1},{4,6},{6,4},{5,7},{7,5},{8,10},{10,8},{9,1... | collective-permute-start | bytes 589832 | tf_op jit(solution)/shard_map/ppermute | solution.py:21

commit v7 on v6

--- a/solution.py
+++ b/solution.py
@@ -7,7 +7,7 @@
 
 FEAT = ("xh", "z", "y")
 TOK = ("xl", "core")
-PLANE = ("xh", "y")
+PLANE = ("y", "xh")
 XH, Z, Y, XL, CORE = 2, 16, 4, 2, 2
 VMEM_BYTES = 8 << 20
 bf16, f32 = jnp.bfloat16, jnp.float32
@@ -180,7 +180,7 @@
 
     along_z = gather_z(layer_inputs)
 
-    order = winners.reshape(layers, XH, Z, Y, 2, picks).transpose(0, 5, 1, 3, 2, 4)
+    order = winners.reshape(layers, XH, Z, Y, 2, picks).transpose(0, 5, 3, 1, 2, 4)
     order = order.reshape(layers, picks, tokens) - lax.axis_index(FEAT) * width_here
     (chosen,) = call(
         mask_kernel,

time: 180 us -> 180 us (level)
  no operation moved by 1% of the time
where the time goes in v7:
time: 180 us; the launch traced here: 179 us
  blocking collectives  108 us (60%)
  starting transfers between devices  37.4 us (21%)
  waiting for transfers between devices  20.7 us (12%)
  Pallas kernels  10 us (6%)
  local copies, waits for them, and re-layouts  2.16 us (1%)
    all_to_all x2, blocking collectives, gather_plane(): return lax.all_to_all(block, PLANE, 0, 0)  44.2 us
    all_to_all x1, blocking collectives, body(): lax.all_to_all(sent, PLANE, 0, 0)  23.8 us
    ppermute x4, starting transfers between devices, swap(): return lax.ppermute(x, axis, [(0, 1), (1, 0)])  21.6 us
    all_to_all x1, blocking collectives, body(): lax.all_to_all(blocks, 'z', 0, 0)  21 us
    all_to_all x1, blocking collectives, body(): errors_got = gather_plane(lax.all_to_all(errors_home, 'z', 0, 0))  18.9 us
    all_to_all x1, starting transfers between devices, gather_z(): return lax.all_to_all(copies, 'z', 0, 0)  15.7 us
    ppermute x4, waiting for transfers between devices, swap(): return lax.ppermute(x, axis, [(0, 1), (1, 0)])  11.8 us
    pallas_call x11, Pallas kernels, call(): pl.pallas_call(kernel, out_shape=[jax.ShapeDtypeStruct(shape, kind) for s...  10 us
  transfers between devices with their start and end apart: 5, of which 5 were waited for; matrix products, arithmetic and copies ran while one was open for 1% of the time, Pallas kernels for 2%

profile of v7, /device:TPU:1, one launch (start us, length us, event | category | flops | bytes accessed | tf_op | source)
XLA Modules:
  0.0 179.1 jit_solution(4732384426603592207)
XLA Ops:
  0.6 0.7 copy-done.4
  1.3 0.7 shard_map.110
  2.0 15.7 %all-to-all-start = ((bf16[16,3,2,1024]{3,2,1,0:T(2,128)(2,1)}), bf16[16,3,2,1024]{3,2,1,0:T(2,128)(2,1)S(1)}, u32[]{:S(2)}, u32[]{:S(2)}) async-start(bf16[16,3,2,1024]{3,2,1,0:T(2,128)(2,1)} %shard_map.110), calls=%async_computation | async-start | bytes 393216 | tf_op jit(solution)/shard_map/all_to_all | solution.py:31
  17.8 1.1 copy.13
  18.9 0.2 copy.14
  19.1 0.1 copy.15.winners_ref
  19.3 2.1 %shard_map.111.mask_ref = bf16[3,256,128]{2,1,0:T(8,128)(2,1)S(1)} custom-call(s32[3,64,256]{2,1,0:T(8,128)S(1)} %copy.15.winners_ref), custom_call_target="tpu_custom_call" | custom-call | flops 6291456 | bytes 393216 | tf_op jit(solution)/shard_map/pallas_call | solution.py:161
  21.4 8.9 %all-to-all-done.along_z_ref = bf16[16,3,2,1024]{3,2,1,0:T(2,128)(2,1)S(1)} async-done(((bf16[16,3,2,1024]{3,2,1,0:T(2,128)(2,1)}), bf16[16,3,2,1024]{3,2,1,0:T(2,128)(2,1)S(1)}, u32[]{:S(2)}, u32[]{:S(2)}) %all-to-all-start) | async-done | bytes 196640 | tf_op jit(solution)/shard_map/all_to_all | solution.py:31
  30.3 0.2 shard_map.112
  30.6 0.0 copy-start.1
  30.6 24.3 %all_to_all.30.x_ref = bf16[8,3,32,1024]{3,2,1,0:T(8,128)(2,1)S(1)} all-to-all(bf16[8,3,32,1024]{3,2,1,0:T(8,128)(2,1)S(1)} %shard_map.112), channel_id=1, replica_groups=mesh['xh'=2,'z'=16,'y'=4,'xl'=2,'core'=2] {'y','xh'}, dimensions={0} | all-to-all | bytes 3145728 | tf_op jit(solution)/shard_map/all_to_all | solution.py:53
  54.9 0.6 shard_map.113
  55.5 7.9 %collective-permute-start = (f32[3,256,128]{2,1,0:T(8,128)S(1)}, f32[3,256,128]{2,1,0:T(8,128)S(1)}, u32[]{:S(2)}, u32[]{:S(2)}) collective-permute-start(f32[3,256,128]{2,1,0:T(8,128)S(1)} %shard_map.113), channel_id=1, source_target_pairs={{0,1},{1,0},{2,3},{3,2},{4,5},{5,4},{6,7},{7,6},{8,9},{9,8},{10,11... | collective-permute-start | bytes 1179656 | tf_op jit(solution)/shard_map/ppermute | solution.py:21
  63.4 1.3 collective-permute-done
  64.8 2.3 %collective-permute-start.1 = (bf16[3,256,128]{2,1,0:T(8,128)(2,1)S(1)}, bf16[3,256,128]{2,1,0:T(8,128)(2,1)S(1)}, u32[]{:S(2)}, u32[]{:S(2)}) collective-permute-start(bf16[3,256,128]{2,1,0:T(8,128)(2,1)S(1)} %add_convert_fusion.1.mine_ref), channel_id=1, source_target_pairs={{0,2},{2,0},{1,3},{3,1},{4,6},{6,4},{5,7},{7,5},{8,10},{10,8},{9,1... | collective-permute-start | bytes 589832 | tf_op jit(solution)/shard_map/ppermute | solution.py:21
  67.1 5.7 %collective-permute-done.1.theirs_ref = bf16[3,256,128]{2,1,0:T(8,128)(2,1)S(1)} collective-permute-done((bf16[3,256,128]{2,1,0:T(8,128)(2,1)S(1)}, bf16[3,256,128]{2,1,0:T(8,128)(2,1)S(1)}, u32[]{:S(2)}, u32[]{:S(2)}) %collective-permute-start.1) | collective-permute-done | bytes 196640 | tf_op jit(solution)/shard_map/ppermute | solution.py:21
  72.8 1.0 shard_map.114
  73.8 23.8 %all_to_all.31.got_ref = bf16[8,3,32,1024]{3,2,1,0:T(8,128)(2,1)S(1)} all-to-all(bf16[8,3,32,1024]{3,2,1,0:T(8,128)(2,1)S(1)} %get-tuple-element.20), channel_id=1, replica_groups=mesh['xh'=2,'z'=16,'y'=4,'xl'=2,'core'=2] {'y','xh'}, dimensions={0} | all-to-all | bytes 3145728 | tf_op jit(solution)/shard_map/all_to_all | solution.py:211
  97.6 0.3 shard_map.115
  98.0 21.0 %all_to_all.32.got_ref = bf16[16,3,2,1024]{3,2,1,0:T(2,128)(2,1)S(1)} all-to-all(bf16[16,3,2,1024]{3,2,1,0:T(2,128)(2,1)S(1)} %shard_map.115), channel_id=1, replica_groups=mesh['xh'=2,'z'=16,'y'=4,'xl'=2,'core'=2] {'z'}, dimensions={0} | all-to-all | bytes 393216 | tf_op jit(solution)/shard_map/all_to_all | solution.py:218
  119.0 0.7 shard_map.116
  119.6 18.9 %all_to_all.33.along_z_ref = bf16[16,3,2,1024]{3,2,1,0:T(2,128)(2,1)S(1)} all-to-all(bf16[16,3,2,1024]{3,2,1,0:T(2,128)(2,1)S(1)} %get-tuple-element.22), channel_id=1, replica_groups=mesh['xh'=2,'z'=16,'y'=4,'xl'=2,'core'=2] {'z'}, dimensions={0} | all-to-all | bytes 393216 | tf_op jit(solution)/shard_map/all_to_all | solution.py:222
  138.5 0.2 shard_map.117
  138.8 19.8 %all_to_all.34.errors_ref = bf16[8,3,32,1024]{3,2,1,0:T(8,128)(2,1)S(1)} all-to-all(bf16[8,3,32,1024]{3,2,1,0:T(8,128)(2,1)S(1)} %shard_map.117), channel_id=1, replica_groups=mesh['xh'=2,'z'=16,'y'=4,'xl'=2,'core'=2] {'y','xh'}, dimensions={0} | all-to-all | bytes 3145728 | tf_op jit(solution)/shard_map/all_to_all | solution.py:53
  158.6 1.0 shard_map.118
  159.6 8.6 %collective-permute-start.2 = (f32[3,256,128]{2,1,0:T(8,128)S(1)}, f32[3,256,128]{2,1,0:T(8,128)S(1)}, u32[]{:S(2)}, u32[]{:S(2)}) collective-permute-start(f32[3,256,128]{2,1,0:T(8,128)S(1)} %shard_map.118), channel_id=1, source_target_pairs={{0,1},{1,0},{2,3},{3,2},{4,5},{5,4},{6,7},{7,6},{8,9},{9,8},{10,11... | collective-permute-start | bytes 1179656 | tf_op jit(solution)/shard_map/ppermute | solution.py:21
  168.2 1.3 collective-permute-done.2
  169.6 0.1 add_convert_fusion.mine_ref
  169.6 2.7 %collective-permute-start.3 = (bf16[3,256,128]{2,1,0:T(8,128)(2,1)S(1)}, bf16[3,256,128]{2,1,0:T(8,128)(2,1)S(1)}, u32[]{:S(2)}, u32[]{:S(2)}) collective-permute-start(bf16[3,256,128]{2,1,0:T(8,128)(2,1)S(1)} %add_convert_fusion.mine_ref), channel_id=1, source_target_pairs={{0,2},{2,0},{1,3},{3,1},{4,6},{6,4},{5,7},{7,5},{8,10},{10,8},{9,1... | collective-permute-start | bytes 589832 | tf_op jit(solution)/shard_map/ppermute | solution.py:21
  172.4 1.8 %shard_map.119 = (bf16[6,128,1024]{2,1,0:T(8,128)(2,1)}, f32[3,1024]{1,0:T(4,128)}, bf16[3,1024,256]{2,1,0:T(8,128)(2,1)S(1)}) custom-call(bf16[3,256,128]{2,1,0:T(8,128)(2,1)S(1)} %get-tuple-element.24.act_ref, bf16[8,3,32,1024]{3,2,1,0:T(8,128)(2,1)S(1)} %all_to_all.34.errors_ref, bf16[8,3,32,1024]{3,2,1,0:T(8,128)(2,1)S(1)} %all_to_all.30.x_ref), custom_call_target="tpu_custom_call" | custom-call | flops 402653184 | bytes 6684672 | tf_op jit(solution)/shard_map/pallas_call | solution.py:161
  174.2 3.4 %collective-permute-done.3.theirs_ref = bf16[3,256,128]{2,1,0:T(8,128)(2,1)S(1)} collective-permute-done((bf16[3,256,128]{2,1,0:T(8,128)(2,1)S(1)}, bf16[3,256,128]{2,1,0:T(8,128)(2,1)S(1)}, u32[]{:S(2)}, u32[]{:S(2)}) %collective-permute-start.3) | collective-permute-done | bytes 196640 | tf_op jit(solution)/shard_map/ppermute | solution.py:21
  177.6 1.5 shard_map.120
  (12 shorter events, 0.1 us)
Async XLA Ops:
  0.6 0.7 copy-start.4
  2.0 28.3 %all-to-all-start = ((bf16[16,3,2,1024]{3,2,1,0:T(2,128)(2,1)}), bf16[16,3,2,1024]{3,2,1,0:T(2,128)(2,1)S(1)}, u32[]{:S(2)}, u32[]{:S(2)}) async-start(bf16[16,3,2,1024]{3,2,1,0:T(2,128)(2,1)} %shard_map.110), calls=%async_computation | async-start | bytes 393216 | tf_op jit(solution)/shard_map/all_to_all | solution.py:31
  30.6 24.3 %copy-start.1 = (bf16[3,1024,128]{2,1,0:T(8,128)(2,1)S(1)}, bf16[3,1024,128]{2,1,0:T(8,128)(2,1)}, u32[]{:S(2)}) copy-start(bf16[3,1024,128]{2,1,0:T(8,128)(2,1)} %weight_ref.3) | copy-start | bytes 2359300
  54.9 17.9 %copy-start = (bf16[6,128,1024]{2,1,0:T(8,128)(2,1)S(1)}, bf16[6,128,1024]{2,1,0:T(8,128)(2,1)}, u32[]{:S(2)}) copy-start(bf16[6,128,1024]{2,1,0:T(8,128)(2,1)} %weight_ref.5) | copy-start | bytes 4718596
  54.9 17.9 %copy-start.5 = (f32[3,128]{1,0:T(4,128)S(1)}, f32[3,128]{1,0:T(4,128)}, u32[]{:S(2)}) copy-start(f32[3,128]{1,0:T(4,128)} %bias_ref.2) | copy-start | bytes 4612
  55.5 9.3 %collective-permute-start = (f32[3,256,128]{2,1,0:T(8,128)S(1)}, f32[3,256,128]{2,1,0:T(8,128)S(1)}, u32[]{:S(2)}, u32[]{:S(2)}) collective-permute-start(f32[3,256,128]{2,1,0:T(8,128)S(1)} %shard_map.113), channel_id=1, source_target_pairs={{0,1},{1,0},{2,3},{3,2},{4,5},{5,4},{6,7},{7,6},{8,9},{9,8},{10,11... | collective-permute-start | bytes 1179656 | tf_op jit(solution)/shard_map/ppermute | solution.py:21
  64.8 8.0 %collective-permute-start.1 = (bf16[3,256,128]{2,1,0:T(8,128)(2,1)S(1)}, bf16[3,256,128]{2,1,0:T(8,128)(2,1)S(1)}, u32[]{:S(2)}, u32[]{:S(2)}) collective-permute-start(bf16[3,256,128]{2,1,0:T(8,128)(2,1)S(1)} %add_convert_fusion.1.mine_ref), channel_id=1, source_target_pairs={{0,2},{2,0},{1,3},{3,1},{4,6},{6,4},{5,7},{7,5},{8,10},{10,8},{9,1... | collective-permute-start | bytes 589832 | tf_op jit(solution)/shard_map/ppermute | solution.py:21
  97.6 21.3 %copy-start.2 = (f32[3,1024]{1,0:T(4,128)S(1)}, f32[3,1024]{1,0:T(4,128)}, u32[]{:S(2)}) copy-start(f32[3,1024]{1,0:T(4,128)} %bias_ref.3) | copy-start | bytes 36868
  97.6 21.3 %copy-start.3 = (bf16[3,2,1024]{2,1,0:T(2,128)(2,1)S(1)}, bf16[3,2,1024]{2,1,0:T(2,128)(2,1)}, u32[]{:S(2)}) copy-start(bf16[3,2,1024]{2,1,0:T(2,128)(2,1)} %targets_ref.1) | copy-start | bytes 36868
  159.6 10.0 %collective-permute-start.2 = (f32[3,256,128]{2,1,0:T(8,128)S(1)}, f32[3,256,128]{2,1,0:T(8,128)S(1)}, u32[]{:S(2)}, u32[]{:S(2)}) collective-permute-start(f32[3,256,128]{2,1,0:T(8,128)S(1)} %shard_map.118), channel_id=1, source_target_pairs={{0,1},{1,0},{2,3},{3,2},{4,5},{5,4},{6,7},{7,6},{8,9},{9,8},{10,11... | collective-permute-start | bytes 1179656 | tf_op jit(solution)/shard_map/ppermute | solution.py:21
  169.6 8.0 %collective-permute-start.3 = (bf16[3,256,128]{2,1,0:T(8,128)(2,1)S(1)}, bf16[3,256,128]{2,1,0:T(8,128)(2,1)S(1)}, u32[]{:S(2)}, u32[]{:S(2)}) collective-permute-start(bf16[3,256,128]{2,1,0:T(8,128)(2,1)S(1)} %add_convert_fusion.mine_ref), channel_id=1, source_target_pairs={{0,2},{2,0},{1,3},{3,1},{4,6},{6,4},{5,7},{7,5},{8,10},{10,8},{9,1... | collective-permute-start | bytes 589832 | tf_op jit(solution)/shard_map/ppermute | solution.py:21

commit v8 on v7

--- a/solution.py
+++ b/solution.py
@@ -82,30 +82,56 @@
     return block.reshape(block.shape[0] * block.shape[1], block.shape[2])
 
 
-def mask_kernel(winners_ref, out_ref, marks_ref):
+def mask_kernel(winners_ref, slot_ref, pick_ref, marks_ref):
     layers, picks, tokens = winners_ref.shape
-    features = out_ref.shape[2]
-    half = features // 2
+    features = slot_ref.shape[2]
+    half, near = features // 2, tokens // 2
     for l in range(layers):
         for h in range(0, features, half):
             ids = h + lax.broadcasted_iota(jnp.int32, (half, tokens), 0)
             marks = jnp.zeros((half, tokens), f32)
             for k in range(picks):
-                marks = jnp.where(winners_ref[l, k : k + 1, :] == ids, 1.0, marks)
+                marks = jnp.where(winners_ref[l, k : k + 1, :] == ids, float(k + 1), marks)
             marks_ref[h : h + half] = marks
-        out_ref[l] = marks_ref[...].T.astype(bf16)
-
-
-def encode_kernel(x_ref, weight_ref, out_ref):
+        slot_ref[l] = marks_ref[...].T.astype(jnp.int32)
+        here = jnp.clip(winners_ref[l], 0, features - 1).astype(f32)
+        marks_ref[:picks, :near] = here[:, :near]
+        marks_ref[picks : 2 * picks, :near] = here[:, near:]
+        pick_ref[l] = marks_ref[:, :near].T.astype(jnp.int32)
+
+
+def take(values, places):
+    return jnp.take_along_axis(values, places, axis=1, mode="promise_in_bounds")
+
+
+def pack(values, pick):
+    near, lanes = pick.shape
+    first = lax.broadcasted_iota(jnp.int32, (near, lanes), 1) < lanes // 2
+    return jnp.where(first, take(values[:near], pick), take(values[near:], pick))
+
+
+def unpack(packed, slot_ref, layer):
+    near, lanes = packed.shape
+    for part in range(2):
+        rows = slice(part * near, (part + 1) * near)
+        slot = slot_ref[layer, rows]
+        place = jnp.maximum(slot - 1, 0) + part * (lanes // 2)
+        yield rows, slot > 0, take(packed, place)
+
+
+def encode_kernel(x_ref, weight_ref, pick_ref, out_ref):
     for l in range(out_ref.shape[0]):
-        out_ref[l] = jnp.dot(rows_of(x_ref, l), weight_ref[l], preferred_element_type=f32)
-
-
-def decode_kernel(mine_ref, theirs_ref, bias_ref, mask_ref, weight_ref, act_ref, out_ref):
+        pre_acts = jnp.dot(rows_of(x_ref, l), weight_ref[l], preferred_element_type=f32)
+        out_ref[l] = pack(pre_acts, pick_ref[l])
+
+
+def decode_kernel(mine_ref, theirs_ref, bias_ref, slot_ref, weight_ref, act_ref, out_ref):
     layers = act_ref.shape[0]
     for l in range(layers):
-        pre_acts = mine_ref[l].astype(f32) + theirs_ref[l].astype(f32) + bias_ref[l : l + 1]
-        act_ref[l] = jnp.where(mask_ref[l] != 0, pre_acts, 0.0).astype(bf16)
+        packed = mine_ref[l].astype(f32) + theirs_ref[l].astype(f32)
+        for rows, chosen, values in unpack(packed, slot_ref, l):
+            pre_acts = values + bias_ref[l : l + 1]
+            act_ref[l, rows] = jnp.where(chosen, pre_acts, 0.0).astype(bf16)
     for u in range(layers):
         totals = None
         for s in range(u + 1):
@@ -118,7 +144,7 @@
         )
 
 
-def grad_kernel(errors_ref, weight_ref, out_ref):
+def grad_kernel(errors_ref, weight_ref, pick_ref, out_ref):
     layers = out_ref.shape[0]
     for s in range(layers):
         grad_act = None
@@ -130,7 +156,7 @@
                 preferred_element_type=f32,
             )
             grad_act = product if grad_act is None else grad_act + product
-        out_ref[s] = grad_act
+        out_ref[s] = pack(grad_act, pick_ref[s])
 
 
 def decoder_grad_kernel(act_ref, errors_ref, x_ref, out_ref, bias_ref, turned_ref):
@@ -146,10 +172,12 @@
             ).astype(bf16)
 
 
-def encoder_grad_kernel(mine_ref, theirs_ref, mask_ref, turned_ref, out_ref, bias_ref):
+def encoder_grad_kernel(mine_ref, theirs_ref, slot_ref, turned_ref, out_ref, bias_ref, grad_ref):
     for l in range(out_ref.shape[0]):
-        grad_act = mine_ref[l].astype(f32) + theirs_ref[l].astype(f32)
-        grad_pre = jnp.where(mask_ref[l] != 0, grad_act, 0.0).astype(bf16)
+        packed = mine_ref[l].astype(f32) + theirs_ref[l].astype(f32)
+        for rows, chosen, values in unpack(packed, slot_ref, l):
+            grad_ref[rows] = jnp.where(chosen, values, 0.0).astype(bf16)
+        grad_pre = grad_ref[...]
         bias_ref[l : l + 1] = jnp.sum(grad_pre.astype(f32), axis=0, keepdims=True)
         out_ref[l] = jnp.dot(
             turned_ref[l], grad_pre, preferred_element_type=f32
@@ -182,26 +210,30 @@
 
     order = winners.reshape(layers, XH, Z, Y, 2, picks).transpose(0, 5, 3, 1, 2, 4)
     order = order.reshape(layers, picks, tokens) - lax.axis_index(FEAT) * width_here
-    (chosen,) = call(
+    slots, picked = call(
         mask_kernel,
         (order,),
-        [((layers, tokens, width_here), bf16)],
+        [
+            ((layers, tokens, width_here), jnp.int32),
+            ((layers, tokens // 2, 2 * picks), jnp.int32),
+        ],
         layers * picks * tokens * width_here,
         [pltpu.VMEM((width_here, tokens), f32)],
     )
-    along_z, chosen = lax.optimization_barrier((along_z, chosen))
+    along_z, slots, picked = lax.optimization_barrier((along_z, slots, picked))
     gathered = gather_plane(along_z)
 
     planes, rows = XH * Y, tokens // (XH * Y)
     narrow = (layers, tokens, width_here)
+    packed = (layers, tokens // 2, 2 * picks)
     work = 2 * tokens * width_here * model
     (partial_pre,) = call(
-        encode_kernel, (gathered, encoder_weight), [(narrow, f32)], layers * work
+        encode_kernel, (gathered, encoder_weight, picked), [(packed, f32)], layers * work
     )
     mine = (partial_pre + swap(partial_pre, "core")).astype(bf16)
     activation, sent = call(
         decode_kernel,
-        (mine, swap(mine, "xl"), encoder_bias, chosen, decoder_weight),
+        (mine, swap(mine, "xl"), encoder_bias, slots, decoder_weight),
         [(narrow, bf16), ((planes, layers, rows, model), bf16)],
         decoder_weight.shape[0] * work,
     )
@@ -222,8 +254,8 @@
     errors_got = gather_plane(lax.all_to_all(errors_home, "z", 0, 0))
     (partial_grad,) = call(
         grad_kernel,
-        (errors_got, decoder_weight),
-        [(narrow, f32)],
+        (errors_got, decoder_weight, picked),
+        [(packed, f32)],
         decoder_weight.shape[0] * work,
     )
     both, errors_got = lax.optimization_barrier((swap(partial_grad, "core"), errors_got))
@@ -236,9 +268,10 @@
     )
     encoder_grad, encoder_bias_grad = call(
         encoder_grad_kernel,
-        (mine, swap(mine, "xl"), chosen, turned),
+        (mine, swap(mine, "xl"), slots, turned),
         [((layers, model, width_here), bf16), ((layers, width_here), f32)],
         layers * work,
+        [pltpu.VMEM((tokens, width_here), bf16)],
     )
     return (recon, encoder_grad, encoder_bias_grad, decoder_grad, decoder_bias_grad)
 

time: 180 us -> 175 us (0.972)
  waiting for transfers between devices: 20.7 us -> 15.9 us
    ppermute x4, waiting for transfers between devices: 11.8 us -> 7.05 us  [swap(): return lax.ppermute(x, axis, [(0, 1), (1, 0)])]
where the time goes in v8:
time: 175 us
  blocking collectives  108 us (62%)
  starting transfers between devices  37.4 us (21%)
  waiting for transfers between devices  15.9 us (9%)
  Pallas kernels  10.7 us (6%)
  local copies, waits for them, and re-layouts  2.16 us (1%)
    all_to_all x2, blocking collectives, gather_plane(): return lax.all_to_all(block, PLANE, 0, 0)  44 us
    all_to_all x1, blocking collectives, body(): lax.all_to_all(sent, PLANE, 0, 0)  23.8 us
    ppermute x4, starting transfers between devices, swap(): return lax.ppermute(x, axis, [(0, 1), (1, 0)])  21.6 us
    all_to_all x1, blocking collectives, body(): lax.all_to_all(blocks, 'z', 0, 0)  21 us
    all_to_all x1, blocking collectives, body(): errors_got = gather_plane(lax.all_to_all(errors_home, 'z', 0, 0))  19.1 us
    all_to_all x1, starting transfers between devices, gather_z(): return lax.all_to_all(copies, 'z', 0, 0)  15.7 us
    pallas_call x11, Pallas kernels, call(): pl.pallas_call(kernel, out_shape=[jax.ShapeDtypeStruct(shape, kind) for s...  10.7 us
    all_to_all x1, waiting for transfers between devices, gather_z(): return lax.all_to_all(copies, 'z', 0, 0)  8.9 us
  transfers between devices with their start and end apart: 5, of which 5 were waited for; matrix products, arithmetic and copies ran while one was open for 1% of the time, Pallas kernels for 2%

profile of v8, /device:TPU:1, one launch (start us, length us, event | category | flops | bytes accessed | tf_op | source)
XLA Modules:
  0.0 174.9 jit_solution(12511770340183465036)
XLA Ops:
  0.6 0.7 copy-done.4
  1.3 0.7 shard_map.110
  2.0 15.7 %all-to-all-start = ((bf16[16,3,2,1024]{3,2,1,0:T(2,128)(2,1)}), bf16[16,3,2,1024]{3,2,1,0:T(2,128)(2,1)S(1)}, u32[]{:S(2)}, u32[]{:S(2)}) async-start(bf16[16,3,2,1024]{3,2,1,0:T(2,128)(2,1)} %shard_map.110), calls=%async_computation | async-start | bytes 393216 | tf_op jit(solution)/shard_map/all_to_all | solution.py:31
  17.8 1.1 copy.13
  18.9 0.2 copy.14
  19.1 0.1 copy.15.winners_ref
  19.3 2.1 %shard_map.111 = (s32[3,256,128]{2,1,0:T(8,128)S(1)}, s32[3,128,128]{2,1,0:T(8,128)S(1)}) custom-call(s32[3,64,256]{2,1,0:T(8,128)S(1)} %copy.15.winners_ref), custom_call_target="tpu_custom_call" | custom-call | flops 6291456 | bytes 393216 | tf_op jit(solution)/shard_map/pallas_call | solution.py:189
  21.4 8.9 %all-to-all-done.along_z_ref = bf16[16,3,2,1024]{3,2,1,0:T(2,128)(2,1)S(1)} async-done(((bf16[16,3,2,1024]{3,2,1,0:T(2,128)(2,1)}), bf16[16,3,2,1024]{3,2,1,0:T(2,128)(2,1)S(1)}, u32[]{:S(2)}, u32[]{:S(2)}) %all-to-all-start) | async-done | bytes 196640 | tf_op jit(solution)/shard_map/all_to_all | solution.py:31
  30.3 0.2 shard_map.112
  30.6 0.0 copy-start.1
  30.6 24.3 %all_to_all.30.x_ref = bf16[8,3,32,1024]{3,2,1,0:T(8,128)(2,1)S(1)} all-to-all(bf16[8,3,32,1024]{3,2,1,0:T(8,128)(2,1)S(1)} %shard_map.112), channel_id=1, replica_groups=mesh['xh'=2,'z'=16,'y'=4,'xl'=2,'core'=2] {'y','xh'}, dimensions={0} | all-to-all | bytes 3145728 | tf_op jit(solution)/shard_map/all_to_all | solution.py:53
  54.9 0.6 shard_map.113
  55.5 7.9 %collective-permute-start = (f32[3,128,128]{2,1,0:T(8,128)S(1)}, f32[3,128,128]{2,1,0:T(8,128)S(1)}, u32[]{:S(2)}, u32[]{:S(2)}) collective-permute-start(f32[3,128,128]{2,1,0:T(8,128)S(1)} %shard_map.113), channel_id=1, source_target_pairs={{0,1},{1,0},{2,3},{3,2},{4,5},{5,4},{6,7},{7,6},{8,9},{9,8},{10,11... | collective-permute-start | bytes 589832 | tf_op jit(solution)/shard_map/ppermute | solution.py:21
  63.5 1.0 collective-permute-done
  64.6 2.3 %collective-permute-start.1 = (bf16[3,128,128]{2,1,0:T(8,128)(2,1)S(1)}, bf16[3,128,128]{2,1,0:T(8,128)(2,1)S(1)}, u32[]{:S(2)}, u32[]{:S(2)}) collective-permute-start(bf16[3,128,128]{2,1,0:T(8,128)(2,1)S(1)} %add_convert_fusion.1.mine_ref), channel_id=1, source_target_pairs={{0,2},{2,0},{1,3},{3,1},{4,6},{6,4},{5,7},{7,5},{8,10},{10,8},{9,1... | collective-permute-start | bytes 294920 | tf_op jit(solution)/shard_map/ppermute | solution.py:21
  66.9 3.6 %collective-permute-done.1.theirs_ref = bf16[3,128,128]{2,1,0:T(8,128)(2,1)S(1)} collective-permute-done((bf16[3,128,128]{2,1,0:T(8,128)(2,1)S(1)}, bf16[3,128,128]{2,1,0:T(8,128)(2,1)S(1)}, u32[]{:S(2)}, u32[]{:S(2)}) %collective-permute-start.1) | collective-permute-done | bytes 98336 | tf_op jit(solution)/shard_map/ppermute | solution.py:21
  70.5 1.1 shard_map.114
  71.6 23.8 %all_to_all.31.got_ref = bf16[8,3,32,1024]{3,2,1,0:T(8,128)(2,1)S(1)} all-to-all(bf16[8,3,32,1024]{3,2,1,0:T(8,128)(2,1)S(1)} %get-tuple-element.26), channel_id=1, replica_groups=mesh['xh'=2,'z'=16,'y'=4,'xl'=2,'core'=2] {'y','xh'}, dimensions={0} | all-to-all | bytes 3145728 | tf_op jit(solution)/shard_map/all_to_all | solution.py:243
  95.4 0.3 shard_map.115
  95.7 21.0 %all_to_all.32.got_ref = bf16[16,3,2,1024]{3,2,1,0:T(2,128)(2,1)S(1)} all-to-all(bf16[16,3,2,1024]{3,2,1,0:T(2,128)(2,1)S(1)} %shard_map.115), channel_id=1, replica_groups=mesh['xh'=2,'z'=16,'y'=4,'xl'=2,'core'=2] {'z'}, dimensions={0} | all-to-all | bytes 393216 | tf_op jit(solution)/shard_map/all_to_all | solution.py:250
  116.7 0.0 copy-done.2
  116.7 0.7 shard_map.116
  117.4 19.1 %all_to_all.33.along_z_ref = bf16[16,3,2,1024]{3,2,1,0:T(2,128)(2,1)S(1)} all-to-all(bf16[16,3,2,1024]{3,2,1,0:T(2,128)(2,1)S(1)} %get-tuple-element.28), channel_id=1, replica_groups=mesh['xh'=2,'z'=16,'y'=4,'xl'=2,'core'=2] {'z'}, dimensions={0} | all-to-all | bytes 393216 | tf_op jit(solution)/shard_map/all_to_all | solution.py:254
  136.5 0.2 shard_map.117
  136.7 19.7 %all_to_all.34.errors_ref = bf16[8,3,32,1024]{3,2,1,0:T(8,128)(2,1)S(1)} all-to-all(bf16[8,3,32,1024]{3,2,1,0:T(8,128)(2,1)S(1)} %shard_map.117), channel_id=1, replica_groups=mesh['xh'=2,'z'=16,'y'=4,'xl'=2,'core'=2] {'y','xh'}, dimensions={0} | all-to-all | bytes 3145728 | tf_op jit(solution)/shard_map/all_to_all | solution.py:53
  156.4 1.1 shard_map.118
  157.5 8.7 %collective-permute-start.2 = (f32[3,128,128]{2,1,0:T(8,128)S(1)}, f32[3,128,128]{2,1,0:T(8,128)S(1)}, u32[]{:S(2)}, u32[]{:S(2)}) collective-permute-start(f32[3,128,128]{2,1,0:T(8,128)S(1)} %shard_map.118), channel_id=1, source_target_pairs={{0,1},{1,0},{2,3},{3,2},{4,5},{5,4},{6,7},{7,6},{8,9},{9,8},{10,11... | collective-permute-start | bytes 589832 | tf_op jit(solution)/shard_map/ppermute | solution.py:21
  166.2 1.0 collective-permute-done.2
  167.3 2.7 %collective-permute-start.3 = (bf16[3,128,128]{2,1,0:T(8,128)(2,1)S(1)}, bf16[3,128,128]{2,1,0:T(8,128)(2,1)S(1)}, u32[]{:S(2)}, u32[]{:S(2)}) collective-permute-start(bf16[3,128,128]{2,1,0:T(8,128)(2,1)S(1)} %add_convert_fusion.mine_ref), channel_id=1, source_target_pairs={{0,2},{2,0},{1,3},{3,1},{4,6},{6,4},{5,7},{7,5},{8,10},{10,8},{9,1... | collective-permute-start | bytes 294920 | tf_op jit(solution)/shard_map/ppermute | solution.py:21
  170.0 1.8 %shard_map.119 = (bf16[6,128,1024]{2,1,0:T(8,128)(2,1)}, f32[3,1024]{1,0:T(4,128)}, bf16[3,1024,256]{2,1,0:T(8,128)(2,1)S(1)}) custom-call(bf16[3,256,128]{2,1,0:T(8,128)(2,1)S(1)} %get-tuple-element.30.act_ref, bf16[8,3,32,1024]{3,2,1,0:T(8,128)(2,1)S(1)} %all_to_all.34.errors_ref, bf16[8,3,32,1024]{3,2,1,0:T(8,128)(2,1)S(1)} %all_to_all.30.x_ref), custom_call_target="tpu_custom_call" | custom-call | flops 402653184 | bytes 6684672 | tf_op jit(solution)/shard_map/pallas_call | solution.py:189
  171.8 1.4 collective-permute-done.3.theirs_ref
  173.2 1.7 shard_map.120
  (12 shorter events, 0.1 us)
Async XLA Ops:
  0.6 0.7 copy-start.4
  2.0 28.3 %all-to-all-start = ((bf16[16,3,2,1024]{3,2,1,0:T(2,128)(2,1)}), bf16[16,3,2,1024]{3,2,1,0:T(2,128)(2,1)S(1)}, u32[]{:S(2)}, u32[]{:S(2)}) async-start(bf16[16,3,2,1024]{3,2,1,0:T(2,128)(2,1)} %shard_map.110), calls=%async_computation | async-start | bytes 393216 | tf_op jit(solution)/shard_map/all_to_all | solution.py:31
  30.6 24.3 %copy-start.1 = (bf16[3,1024,128]{2,1,0:T(8,128)(2,1)S(1)}, bf16[3,1024,128]{2,1,0:T(8,128)(2,1)}, u32[]{:S(2)}) copy-start(bf16[3,1024,128]{2,1,0:T(8,128)(2,1)} %weight_ref.3) | copy-start | bytes 2359300
  54.9 15.6 %copy-start = (bf16[6,128,1024]{2,1,0:T(8,128)(2,1)S(1)}, bf16[6,128,1024]{2,1,0:T(8,128)(2,1)}, u32[]{:S(2)}) copy-start(bf16[6,128,1024]{2,1,0:T(8,128)(2,1)} %weight_ref.5) | copy-start | bytes 4718596
  54.9 15.6 %copy-start.5 = (f32[3,128]{1,0:T(4,128)S(1)}, f32[3,128]{1,0:T(4,128)}, u32[]{:S(2)}) copy-start(f32[3,128]{1,0:T(4,128)} %bias_ref.2) | copy-start | bytes 4612
  55.5 9.0 %collective-permute-start = (f32[3,128,128]{2,1,0:T(8,128)S(1)}, f32[3,128,128]{2,1,0:T(8,128)S(1)}, u32[]{:S(2)}, u32[]{:S(2)}) collective-permute-start(f32[3,128,128]{2,1,0:T(8,128)S(1)} %shard_map.113), channel_id=1, source_target_pairs={{0,1},{1,0},{2,3},{3,2},{4,5},{5,4},{6,7},{7,6},{8,9},{9,8},{10,11... | collective-permute-start | bytes 589832 | tf_op jit(solution)/shard_map/ppermute | solution.py:21
  64.6 5.9 %collective-permute-start.1 = (bf16[3,128,128]{2,1,0:T(8,128)(2,1)S(1)}, bf16[3,128,128]{2,1,0:T(8,128)(2,1)S(1)}, u32[]{:S(2)}, u32[]{:S(2)}) collective-permute-start(bf16[3,128,128]{2,1,0:T(8,128)(2,1)S(1)} %add_convert_fusion.1.mine_ref), channel_id=1, source_target_pairs={{0,2},{2,0},{1,3},{3,1},{4,6},{6,4},{5,7},{7,5},{8,10},{10,8},{9,1... | collective-permute-start | bytes 294920 | tf_op jit(solution)/shard_map/ppermute | solution.py:21
  95.4 21.3 %copy-start.2 = (f32[3,1024]{1,0:T(4,128)S(1)}, f32[3,1024]{1,0:T(4,128)}, u32[]{:S(2)}) copy-start(f32[3,1024]{1,0:T(4,128)} %bias_ref.3) | copy-start | bytes 36868
  95.4 21.3 %copy-start.3 = (bf16[3,2,1024]{2,1,0:T(2,128)(2,1)S(1)}, bf16[3,2,1024]{2,1,0:T(2,128)(2,1)}, u32[]{:S(2)}) copy-start(bf16[3,2,1024]{2,1,0:T(2,128)(2,1)} %targets_ref.1) | copy-start | bytes 36868
  157.5 9.7 %collective-permute-start.2 = (f32[3,128,128]{2,1,0:T(8,128)S(1)}, f32[3,128,128]{2,1,0:T(8,128)S(1)}, u32[]{:S(2)}, u32[]{:S(2)}) collective-permute-start(f32[3,128,128]{2,1,0:T(8,128)S(1)} %shard_map.118), channel_id=1, source_target_pairs={{0,1},{1,0},{2,3},{3,2},{4,5},{5,4},{6,7},{7,6},{8,9},{9,8},{10,11... | collective-permute-start | bytes 589832 | tf_op jit(solution)/shard_map/ppermute | solution.py:21
  167.3 5.9 %collective-permute-start.3 = (bf16[3,128,128]{2,1,0:T(8,128)(2,1)S(1)}, bf16[3,128,128]{2,1,0:T(8,128)(2,1)S(1)}, u32[]{:S(2)}, u32[]{:S(2)}) collective-permute-start(bf16[3,128,128]{2,1,0:T(8,128)(2,1)S(1)} %add_convert_fusion.mine_ref), channel_id=1, source_target_pairs={{0,2},{2,0},{1,3},{3,1},{4,6},{6,4},{5,7},{7,5},{8,10},{10,8},{9,1... | collective-permute-start | bytes 294920 | tf_op jit(solution)/shard_map/ppermute | solution.py:21

commit v9 on v8

--- a/solution.py
+++ b/solution.py
@@ -21,13 +21,27 @@
     return lax.ppermute(x, axis, [(0, 1), (1, 0)])
 
 
-def copies_kernel(home_ref, out_ref):
-    for z in range(out_ref.shape[0]):
-        out_ref[z] = home_ref[...]
+def copies_kernel(home_ref, out_ref, sems):
+    copies = [
+        pltpu.make_async_copy(home_ref, out_ref.at[z], sems.at[z])
+        for z in range(out_ref.shape[0])
+    ]
+    for copy in copies:
+        copy.start()
+    for copy in copies:
+        copy.wait()
 
 
 def gather_z(home):
-    (copies,) = call(copies_kernel, (home,), [((Z,) + home.shape, bf16)], home.size)
+    (copies,) = call(
+        copies_kernel,
+        (home,),
+        [((Z,) + home.shape, bf16)],
+        home.size,
+        [pltpu.SemaphoreType.DMA((Z,))],
+        [pltpu.VMEM],
+        [pl.ANY],
+    )
     return lax.all_to_all(copies, "z", 0, 0)
 
 
@@ -172,25 +186,36 @@
             ).astype(bf16)
 
 
-def encoder_grad_kernel(mine_ref, theirs_ref, slot_ref, turned_ref, out_ref, bias_ref, grad_ref):
+def encoder_grad_kernel(
+    mine_ref, theirs_ref, slot_ref, turned_ref, out_ref, bias_ref, grad_ref, held_ref, sems
+):
+    copies = []
     for l in range(out_ref.shape[0]):
         packed = mine_ref[l].astype(f32) + theirs_ref[l].astype(f32)
         for rows, chosen, values in unpack(packed, slot_ref, l):
             grad_ref[rows] = jnp.where(chosen, values, 0.0).astype(bf16)
         grad_pre = grad_ref[...]
-        bias_ref[l : l + 1] = jnp.sum(grad_pre.astype(f32), axis=0, keepdims=True)
-        out_ref[l] = jnp.dot(
+        held_ref[l] = jnp.dot(
             turned_ref[l], grad_pre, preferred_element_type=f32
         ).astype(bf16)
-
-
-def call(kernel, args, outs, flops, scratch=()):
+        copies.append(pltpu.make_async_copy(held_ref.at[l], out_ref.at[l], sems.at[l]))
+        copies[l].start()
+        bias_ref[l : l + 1] = jnp.sum(grad_pre.astype(f32), axis=0, keepdims=True)
+    for copy in copies:
+        copy.wait()
+
+
+def call(kernel, args, outs, flops, scratch=(), spaces_in=None, spaces_out=None):
     size = sum(a.size * a.dtype.itemsize for a in args)
     return pl.pallas_call(
         kernel,
         out_shape=[jax.ShapeDtypeStruct(shape, kind) for shape, kind in outs],
-        in_specs=[pl.BlockSpec(memory_space=pltpu.VMEM) for _ in args],
-        out_specs=[pl.BlockSpec(memory_space=pltpu.VMEM) for _ in outs],
+        in_specs=[
+            pl.BlockSpec(memory_space=space) for space in spaces_in or [pltpu.VMEM] * len(args)
+        ],
+        out_specs=[
+            pl.BlockSpec(memory_space=space) for space in spaces_out or [pltpu.VMEM] * len(outs)
+        ],
         scratch_shapes=list(scratch),
         compiler_params=pltpu.CompilerParams(vmem_limit_bytes=VMEM_BYTES),
         cost_estimate=pl.CostEstimate(flops=flops, bytes_accessed=2 * size, transcendentals=0),
@@ -271,7 +296,13 @@
         (mine, swap(mine, "xl"), slots, turned),
         [((layers, model, width_here), bf16), ((layers, width_here), f32)],
         layers * work,
-        [pltpu.VMEM((tokens, width_here), bf16)],
+        [
+            pltpu.VMEM((tokens, width_here), bf16),
+            pltpu.VMEM((layers, model, width_here), bf16),
+            pltpu.SemaphoreType.DMA((layers,)),
+        ],
+        None,
+        [pl.ANY, pltpu.VMEM],
     )
     return (recon, encoder_grad, encoder_bias_grad, decoder_grad, decoder_bias_grad)
 

time: 175 us -> 176 us (level)
  no operation moved by 1% of the time
where the time goes in v9:
time: 176 us
  blocking collectives  108 us (61%)
  starting transfers between devices  37.4 us (21%)
  waiting for transfers between devices  15.9 us (9%)
  Pallas kernels  11.3 us (6%)
  local copies, waits for them, and re-layouts  2.16 us (1%)
    all_to_all x2, blocking collectives, gather_plane(): return lax.all_to_all(block, PLANE, 0, 0)  44 us
    all_to_all x1, blocking collectives, body(): lax.all_to_all(sent, PLANE, 0, 0)  23.8 us
    ppermute x4, starting transfers between devices, swap(): return lax.ppermute(x, axis, [(0, 1), (1, 0)])  21.6 us
    all_to_all x1, blocking collectives, body(): lax.all_to_all(blocks, 'z', 0, 0)  21 us
    all_to_all x1, blocking collectives, body(): errors_got = gather_plane(lax.all_to_all(errors_home, 'z', 0, 0))  19.1 us
    all_to_all x1, starting transfers between devices, gather_z(): return lax.all_to_all(copies, 'z', 0, 0)  15.8 us
    pallas_call x11, Pallas kernels, call(): pl.pallas_call(kernel, out_shape=[jax.ShapeDtypeStruct(shape, kind) for s...  11.3 us
    all_to_all x1, waiting for transfers between devices, gather_z(): return lax.all_to_all(copies, 'z', 0, 0)  8.9 us
  transfers between devices with their start and end apart: 5, of which 5 were waited for; matrix products, arithmetic and copies ran while one was open for 1% of the time, Pallas kernels for 2%

profile of v9, /device:TPU:1, one launch (start us, length us, event | category | flops | bytes accessed | tf_op | source)
XLA Modules:
  0.0 175.5 jit_solution(8709475954761318045)
XLA Ops:
  0.6 0.7 copy-done.4
  1.3 0.8 shard_map.110
  2.1 15.8 %all-to-all-start = ((bf16[16,3,2,1024]{3,2,1,0:T(2,128)(2,1)}), bf16[16,3,2,1024]{3,2,1,0:T(2,128)(2,1)S(1)}, u32[]{:S(2)}, u32[]{:S(2)}) async-start(bf16[16,3,2,1024]{3,2,1,0:T(2,128)(2,1)} %shard_map.110), calls=%async_computation | async-start | bytes 393216 | tf_op jit(solution)/shard_map/all_to_all | solution.py:45
  17.9 1.1 copy.13
  19.1 0.2 copy.14
  19.3 0.1 copy.15.winners_ref
  19.4 2.1 %shard_map.111 = (s32[3,256,128]{2,1,0:T(8,128)S(1)}, s32[3,128,128]{2,1,0:T(8,128)S(1)}) custom-call(s32[3,64,256]{2,1,0:T(8,128)S(1)} %copy.15.winners_ref), custom_call_target="tpu_custom_call" | custom-call | flops 6291456 | bytes 393216 | tf_op jit(solution)/shard_map/pallas_call | solution.py:210
  21.6 8.9 %all-to-all-done.along_z_ref = bf16[16,3,2,1024]{3,2,1,0:T(2,128)(2,1)S(1)} async-done(((bf16[16,3,2,1024]{3,2,1,0:T(2,128)(2,1)}), bf16[16,3,2,1024]{3,2,1,0:T(2,128)(2,1)S(1)}, u32[]{:S(2)}, u32[]{:S(2)}) %all-to-all-start) | async-done | bytes 196640 | tf_op jit(solution)/shard_map/all_to_all | solution.py:45
  30.5 0.2 shard_map.112
  30.7 0.0 copy-start.1
  30.7 24.3 %all_to_all.30.x_ref = bf16[8,3,32,1024]{3,2,1,0:T(8,128)(2,1)S(1)} all-to-all(bf16[8,3,32,1024]{3,2,1,0:T(8,128)(2,1)S(1)} %shard_map.112), channel_id=1, replica_groups=mesh['xh'=2,'z'=16,'y'=4,'xl'=2,'core'=2] {'y','xh'}, dimensions={0} | all-to-all | bytes 3145728 | tf_op jit(solution)/shard_map/all_to_all | solution.py:67
  55.0 0.6 shard_map.113
  55.7 7.9 %collective-permute-start = (f32[3,128,128]{2,1,0:T(8,128)S(1)}, f32[3,128,128]{2,1,0:T(8,128)S(1)}, u32[]{:S(2)}, u32[]{:S(2)}) collective-permute-start(f32[3,128,128]{2,1,0:T(8,128)S(1)} %shard_map.113), channel_id=1, source_target_pairs={{0,1},{1,0},{2,3},{3,2},{4,5},{5,4},{6,7},{7,6},{8,9},{9,8},{10,11... | collective-permute-start | bytes 589832 | tf_op jit(solution)/shard_map/ppermute | solution.py:21
  63.6 1.0 collective-permute-done
  64.7 2.3 %collective-permute-start.1 = (bf16[3,128,128]{2,1,0:T(8,128)(2,1)S(1)}, bf16[3,128,128]{2,1,0:T(8,128)(2,1)S(1)}, u32[]{:S(2)}, u32[]{:S(2)}) collective-permute-start(bf16[3,128,128]{2,1,0:T(8,128)(2,1)S(1)} %add_convert_fusion.1.mine_ref), channel_id=1, source_target_pairs={{0,2},{2,0},{1,3},{3,1},{4,6},{6,4},{5,7},{7,5},{8,10},{10,8},{9,1... | collective-permute-start | bytes 294920 | tf_op jit(solution)/shard_map/ppermute | solution.py:21
  67.0 3.6 %collective-permute-done.1.theirs_ref = bf16[3,128,128]{2,1,0:T(8,128)(2,1)S(1)} collective-permute-done((bf16[3,128,128]{2,1,0:T(8,128)(2,1)S(1)}, bf16[3,128,128]{2,1,0:T(8,128)(2,1)S(1)}, u32[]{:S(2)}, u32[]{:S(2)}) %collective-permute-start.1) | collective-permute-done | bytes 98336 | tf_op jit(solution)/shard_map/ppermute | solution.py:21
  70.6 0.0 copy-done.5
  70.6 1.1 shard_map.114
  71.7 23.8 %all_to_all.31.got_ref = bf16[8,3,32,1024]{3,2,1,0:T(8,128)(2,1)S(1)} all-to-all(bf16[8,3,32,1024]{3,2,1,0:T(8,128)(2,1)S(1)} %get-tuple-element.26), channel_id=1, replica_groups=mesh['xh'=2,'z'=16,'y'=4,'xl'=2,'core'=2] {'y','xh'}, dimensions={0} | all-to-all | bytes 3145728 | tf_op jit(solution)/shard_map/all_to_all | solution.py:268
  95.5 0.3 shard_map.115
  95.9 21.0 %all_to_all.32.got_ref = bf16[16,3,2,1024]{3,2,1,0:T(2,128)(2,1)S(1)} all-to-all(bf16[16,3,2,1024]{3,2,1,0:T(2,128)(2,1)S(1)} %shard_map.115), channel_id=1, replica_groups=mesh['xh'=2,'z'=16,'y'=4,'xl'=2,'core'=2] {'z'}, dimensions={0} | all-to-all | bytes 393216 | tf_op jit(solution)/shard_map/all_to_all | solution.py:275
  116.8 0.7 shard_map.116
  117.5 19.1 %all_to_all.33.along_z_ref = bf16[16,3,2,1024]{3,2,1,0:T(2,128)(2,1)S(1)} all-to-all(bf16[16,3,2,1024]{3,2,1,0:T(2,128)(2,1)S(1)} %get-tuple-element.28), channel_id=1, replica_groups=mesh['xh'=2,'z'=16,'y'=4,'xl'=2,'core'=2] {'z'}, dimensions={0} | all-to-all | bytes 393216 | tf_op jit(solution)/shard_map/all_to_all | solution.py:279
  136.6 0.2 shard_map.117
  136.9 19.7 %all_to_all.34.errors_ref = bf16[8,3,32,1024]{3,2,1,0:T(8,128)(2,1)S(1)} all-to-all(bf16[8,3,32,1024]{3,2,1,0:T(8,128)(2,1)S(1)} %shard_map.117), channel_id=1, replica_groups=mesh['xh'=2,'z'=16,'y'=4,'xl'=2,'core'=2] {'y','xh'}, dimensions={0} | all-to-all | bytes 3145728 | tf_op jit(solution)/shard_map/all_to_all | solution.py:67
  156.5 1.1 shard_map.118
  157.7 8.7 %collective-permute-start.2 = (f32[3,128,128]{2,1,0:T(8,128)S(1)}, f32[3,128,128]{2,1,0:T(8,128)S(1)}, u32[]{:S(2)}, u32[]{:S(2)}) collective-permute-start(f32[3,128,128]{2,1,0:T(8,128)S(1)} %shard_map.118), channel_id=1, source_target_pairs={{0,1},{1,0},{2,3},{3,2},{4,5},{5,4},{6,7},{7,6},{8,9},{9,8},{10,11... | collective-permute-start | bytes 589832 | tf_op jit(solution)/shard_map/ppermute | solution.py:21
  166.3 1.0 collective-permute-done.2
  167.4 2.7 %collective-permute-start.3 = (bf16[3,128,128]{2,1,0:T(8,128)(2,1)S(1)}, bf16[3,128,128]{2,1,0:T(8,128)(2,1)S(1)}, u32[]{:S(2)}, u32[]{:S(2)}) collective-permute-start(bf16[3,128,128]{2,1,0:T(8,128)(2,1)S(1)} %add_convert_fusion.mine_ref), channel_id=1, source_target_pairs={{0,2},{2,0},{1,3},{3,1},{4,6},{6,4},{5,7},{7,5},{8,10},{10,8},{9,1... | collective-permute-start | bytes 294920 | tf_op jit(solution)/shard_map/ppermute | solution.py:21
  170.1 1.8 %shard_map.119 = (bf16[6,128,1024]{2,1,0:T(8,128)(2,1)}, f32[3,1024]{1,0:T(4,128)}, bf16[3,1024,256]{2,1,0:T(8,128)(2,1)S(1)}) custom-call(bf16[3,256,128]{2,1,0:T(8,128)(2,1)S(1)} %get-tuple-element.30.act_ref, bf16[8,3,32,1024]{3,2,1,0:T(8,128)(2,1)S(1)} %all_to_all.34.errors_ref, bf16[8,3,32,1024]{3,2,1,0:T(8,128)(2,1)S(1)} %all_to_all.30.x_ref), custom_call_target="tpu_custom_call" | custom-call | flops 402653184 | bytes 6684672 | tf_op jit(solution)/shard_map/pallas_call | solution.py:210
  172.0 1.4 collective-permute-done.3.theirs_ref
  173.3 2.2 %shard_map.120 = (bf16[3,1024,128]{2,1,0:T(8,128)(2,1)}, f32[3,128]{1,0:T(4,128)}) custom-call(bf16[3,128,128]{2,1,0:T(8,128)(2,1)S(1)} %add_convert_fusion.mine_ref, bf16[3,128,128]{2,1,0:T(8,128)(2,1)S(1)} %collective-permute-done.3.theirs_ref, s32[3,256,128]{2,1,0:T(8,128)S(1)} %get-tuple-element.25.slot_ref, ...), custom_call_target="tpu_custom_call" | custom-call | flops 201326592 | bytes 4325376 | tf_op jit(solution)/shard_map/pallas_call | solution.py:210
  (12 shorter events, 0.1 us)
Async XLA Ops:
  0.6 0.7 copy-start.4
  2.1 28.3 %all-to-all-start = ((bf16[16,3,2,1024]{3,2,1,0:T(2,128)(2,1)}), bf16[16,3,2,1024]{3,2,1,0:T(2,128)(2,1)S(1)}, u32[]{:S(2)}, u32[]{:S(2)}) async-start(bf16[16,3,2,1024]{3,2,1,0:T(2,128)(2,1)} %shard_map.110), calls=%async_computation | async-start | bytes 393216 | tf_op jit(solution)/shard_map/all_to_all | solution.py:45
  30.7 24.3 %copy-start.1 = (bf16[3,1024,128]{2,1,0:T(8,128)(2,1)S(1)}, bf16[3,1024,128]{2,1,0:T(8,128)(2,1)}, u32[]{:S(2)}) copy-start(bf16[3,1024,128]{2,1,0:T(8,128)(2,1)} %weight_ref.3) | copy-start | bytes 2359300
  55.0 15.6 %copy-start = (bf16[6,128,1024]{2,1,0:T(8,128)(2,1)S(1)}, bf16[6,128,1024]{2,1,0:T(8,128)(2,1)}, u32[]{:S(2)}) copy-start(bf16[6,128,1024]{2,1,0:T(8,128)(2,1)} %weight_ref.5) | copy-start | bytes 4718596
  55.0 15.6 %copy-start.5 = (f32[3,128]{1,0:T(4,128)S(1)}, f32[3,128]{1,0:T(4,128)}, u32[]{:S(2)}) copy-start(f32[3,128]{1,0:T(4,128)} %bias_ref.2) | copy-start | bytes 4612
  55.7 9.0 %collective-permute-start = (f32[3,128,128]{2,1,0:T(8,128)S(1)}, f32[3,128,128]{2,1,0:T(8,128)S(1)}, u32[]{:S(2)}, u32[]{:S(2)}) collective-permute-start(f32[3,128,128]{2,1,0:T(8,128)S(1)} %shard_map.113), channel_id=1, source_target_pairs={{0,1},{1,0},{2,3},{3,2},{4,5},{5,4},{6,7},{7,6},{8,9},{9,8},{10,11... | collective-permute-start | bytes 589832 | tf_op jit(solution)/shard_map/ppermute | solution.py:21
  64.7 5.9 %collective-permute-start.1 = (bf16[3,128,128]{2,1,0:T(8,128)(2,1)S(1)}, bf16[3,128,128]{2,1,0:T(8,128)(2,1)S(1)}, u32[]{:S(2)}, u32[]{:S(2)}) collective-permute-start(bf16[3,128,128]{2,1,0:T(8,128)(2,1)S(1)} %add_convert_fusion.1.mine_ref), channel_id=1, source_target_pairs={{0,2},{2,0},{1,3},{3,1},{4,6},{6,4},{5,7},{7,5},{8,10},{10,8},{9,1... | collective-permute-start | bytes 294920 | tf_op jit(solution)/shard_map/ppermute | solution.py:21
  95.5 21.3 %copy-start.2 = (f32[3,1024]{1,0:T(4,128)S(1)}, f32[3,1024]{1,0:T(4,128)}, u32[]{:S(2)}) copy-start(f32[3,1024]{1,0:T(4,128)} %bias_ref.3) | copy-start | bytes 36868
  95.5 21.3 %copy-start.3 = (bf16[3,2,1024]{2,1,0:T(2,128)(2,1)S(1)}, bf16[3,2,1024]{2,1,0:T(2,128)(2,1)}, u32[]{:S(2)}) copy-start(bf16[3,2,1024]{2,1,0:T(2,128)(2,1)} %targets_ref.1) | copy-start | bytes 36868
  157.7 9.7 %collective-permute-start.2 = (f32[3,128,128]{2,1,0:T(8,128)S(1)}, f32[3,128,128]{2,1,0:T(8,128)S(1)}, u32[]{:S(2)}, u32[]{:S(2)}) collective-permute-start(f32[3,128,128]{2,1,0:T(8,128)S(1)} %shard_map.118), channel_id=1, source_target_pairs={{0,1},{1,0},{2,3},{3,2},{4,5},{5,4},{6,7},{7,6},{8,9},{9,8},{10,11... | collective-permute-start | bytes 589832 | tf_op jit(solution)/shard_map/ppermute | solution.py:21
  167.4 5.9 %collective-permute-start.3 = (bf16[3,128,128]{2,1,0:T(8,128)(2,1)S(1)}, bf16[3,128,128]{2,1,0:T(8,128)(2,1)S(1)}, u32[]{:S(2)}, u32[]{:S(2)}) collective-permute-start(bf16[3,128,128]{2,1,0:T(8,128)(2,1)S(1)} %add_convert_fusion.mine_ref), channel_id=1, source_target_pairs={{0,2},{2,0},{1,3},{3,1},{4,6},{6,4},{5,7},{7,5},{8,10},{10,8},{9,1... | collective-permute-start | bytes 294920 | tf_op jit(solution)/shard_map/ppermute | solution.py:21

commit v10 on v8

--- a/solution.py
+++ b/solution.py
@@ -5,10 +5,12 @@
 from jax.experimental.pallas import tpu as pltpu
 from jax.sharding import Mesh, PartitionSpec as P
 
-FEAT = ("xh", "z", "y")
+FEAT = ("xh", "zh", "zl", "y")
+COLUMN = ("zl", "zh")
 TOK = ("xl", "core")
 PLANE = ("y", "xh")
-XH, Z, Y, XL, CORE = 2, 16, 4, 2, 2
+XH, ZH, ZL, Y, XL, CORE = 2, 4, 4, 4, 2, 2
+Z = ZH * ZL
 VMEM_BYTES = 8 << 20
 bf16, f32 = jnp.bfloat16, jnp.float32
 
@@ -28,7 +30,7 @@
 
 def gather_z(home):
     (copies,) = call(copies_kernel, (home,), [((Z,) + home.shape, bf16)], home.size)
-    return lax.all_to_all(copies, "z", 0, 0)
+    return lax.all_to_all(copies, COLUMN, 0, 0)
 
 
 def spread_kernel(along_z_ref, out_ref, rows_ref):
@@ -208,7 +210,7 @@
 
     along_z = gather_z(layer_inputs)
 
-    order = winners.reshape(layers, XH, Z, Y, 2, picks).transpose(0, 5, 3, 1, 2, 4)
+    order = winners.reshape(layers, XH, ZH, ZL, Y, 2, picks).transpose(0, 6, 4, 1, 3, 2, 5)
     order = order.reshape(layers, picks, tokens) - lax.axis_index(FEAT) * width_here
     slots, picked = call(
         mask_kernel,
@@ -247,11 +249,11 @@
     )
     recon, errors_home = call(
         errors_kernel,
-        (lax.all_to_all(blocks, "z", 0, 0), decoder_bias, targets),
+        (lax.all_to_all(blocks, COLUMN, 0, 0), decoder_bias, targets),
         [(targets.shape, bf16), (columns, bf16)],
         blocks.size,
     )
-    errors_got = gather_plane(lax.all_to_all(errors_home, "z", 0, 0))
+    errors_got = gather_plane(lax.all_to_all(errors_home, COLUMN, 0, 0))
     (partial_grad,) = call(
         grad_kernel,
         (errors_got, decoder_weight, picked),
@@ -277,7 +279,7 @@
 
 
 def solution(mesh):
-    fine = Mesh(mesh.devices.reshape(XH, Z, Y, XL, CORE), FEAT + TOK)
+    fine = Mesh(mesh.devices.reshape(XH, ZH, ZL, Y, XL, CORE), FEAT + TOK)
     in_specs = (
         P(None, FEAT, TOK),
         P(None, FEAT, TOK),

time: 175 us -> 177 us (1.011)
  blocking collectives: 108 us -> 111 us
  starting transfers between devices: 37.4 us -> 34.9 us
    ppermute x4, starting transfers between devices: 21.6 us -> 19.1 us  [swap(): return lax.ppermute(x, axis, [(0, 1), (1, 0)])]
    all_to_all x2, blocking collectives: 44 us -> 46.4 us  [gather_plane(): return lax.all_to_all(block, PLANE, 0, 0)]
where the time goes in v10:
time: 177 us; the launch traced here: 176 us
  blocking collectives  111 us (63%)
  starting transfers between devices  34.9 us (20%)
  waiting for transfers between devices  17.1 us (10%)
  Pallas kernels  10.7 us (6%)
  local copies, waits for them, and re-layouts  2.16 us (1%)
    all_to_all x2, blocking collectives, gather_plane(): return lax.all_to_all(block, PLANE, 0, 0)  46.4 us
    all_to_all x1, blocking collectives, body(): lax.all_to_all(sent, PLANE, 0, 0)  23.7 us
    all_to_all x1, blocking collectives, body(): lax.all_to_all(blocks, COLUMN, 0, 0)  20.5 us
    all_to_all x1, blocking collectives, body(): errors_got = gather_plane(lax.all_to_all(errors_home, COLUMN, 0, 0))  19.9 us
    ppermute x4, starting transfers between devices, swap(): return lax.ppermute(x, axis, [(0, 1), (1, 0)])  19.1 us
    all_to_all x1, starting transfers between devices, gather_z(): return lax.all_to_all(copies, COLUMN, 0, 0)  15.7 us
    pallas_call x11, Pallas kernels, call(): pl.pallas_call(kernel, out_shape=[jax.ShapeDtypeStruct(shape, kind) for s...  10.7 us
    all_to_all x1, waiting for transfers between devices, gather_z(): return lax.all_to_all(copies, COLUMN, 0, 0)  9.48 us
  transfers between devices with their start and end apart: 5, of which 5 were waited for; matrix products, arithmetic and copies ran while one was open for 1% of the time, Pallas kernels for 2%

profile of v10, /device:TPU:1, one launch (start us, length us, event | category | flops | bytes accessed | tf_op | source)
XLA Modules:
  0.0 176.2 jit_solution(5405197053654513404)
XLA Ops:
  0.6 0.7 copy-done.4
  1.3 0.7 shard_map.110
  2.0 15.7 %all-to-all-start = ((bf16[16,3,2,1024]{3,2,1,0:T(2,128)(2,1)}), bf16[16,3,2,1024]{3,2,1,0:T(2,128)(2,1)S(1)}, u32[]{:S(2)}, u32[]{:S(2)}) async-start(bf16[16,3,2,1024]{3,2,1,0:T(2,128)(2,1)} %shard_map.110), calls=%async_computation | async-start | bytes 393216 | tf_op jit(solution)/shard_map/all_to_all | solution.py:33
  17.8 1.1 copy.13
  18.9 0.2 copy.14
  19.1 0.1 copy.15.winners_ref
  19.3 2.1 %shard_map.111 = (s32[3,256,128]{2,1,0:T(8,128)S(1)}, s32[3,128,128]{2,1,0:T(8,128)S(1)}) custom-call(s32[3,64,256]{2,1,0:T(8,128)S(1)} %copy.15.winners_ref), custom_call_target="tpu_custom_call" | custom-call | flops 6291456 | bytes 393216 | tf_op jit(solution)/shard_map/pallas_call | solution.py:191
  21.4 9.5 %all-to-all-done.along_z_ref = bf16[16,3,2,1024]{3,2,1,0:T(2,128)(2,1)S(1)} async-done(((bf16[16,3,2,1024]{3,2,1,0:T(2,128)(2,1)}), bf16[16,3,2,1024]{3,2,1,0:T(2,128)(2,1)S(1)}, u32[]{:S(2)}, u32[]{:S(2)}) %all-to-all-start) | async-done | bytes 196640 | tf_op jit(solution)/shard_map/all_to_all | solution.py:33
  30.9 0.2 shard_map.112
  31.2 0.0 copy-start.1
  31.2 24.9 %all_to_all.30.x_ref = bf16[8,3,32,1024]{3,2,1,0:T(8,128)(2,1)S(1)} all-to-all(bf16[8,3,32,1024]{3,2,1,0:T(8,128)(2,1)S(1)} %shard_map.112), channel_id=1, replica_groups=mesh['xh'=2,'zh'=4,'zl'=4,'y'=4,'xl'=2,'core'=2] {'y','xh'}, dimensions={0} | all-to-all | bytes 3145728 | tf_op jit(solution)/shard_map/all_to_all | solution.py:55
  56.0 0.6 shard_map.113
  56.7 7.4 %collective-permute-start = (f32[3,128,128]{2,1,0:T(8,128)S(1)}, f32[3,128,128]{2,1,0:T(8,128)S(1)}, u32[]{:S(2)}, u32[]{:S(2)}) collective-permute-start(f32[3,128,128]{2,1,0:T(8,128)S(1)} %shard_map.113), channel_id=1, source_target_pairs={{0,1},{1,0},{2,3},{3,2},{4,5},{5,4},{6,7},{7,6},{8,9},{9,8},{10,11... | collective-permute-start | bytes 589832 | tf_op jit(solution)/shard_map/ppermute | solution.py:23
  64.1 1.0 collective-permute-done
  65.2 2.2 %collective-permute-start.1 = (bf16[3,128,128]{2,1,0:T(8,128)(2,1)S(1)}, bf16[3,128,128]{2,1,0:T(8,128)(2,1)S(1)}, u32[]{:S(2)}, u32[]{:S(2)}) collective-permute-start(bf16[3,128,128]{2,1,0:T(8,128)(2,1)S(1)} %add_convert_fusion.1.mine_ref), channel_id=1, source_target_pairs={{0,2},{2,0},{1,3},{3,1},{4,6},{6,4},{5,7},{7,5},{8,10},{10,8},{9,1... | collective-permute-start | bytes 294920 | tf_op jit(solution)/shard_map/ppermute | solution.py:23
  67.4 3.7 %collective-permute-done.1.theirs_ref = bf16[3,128,128]{2,1,0:T(8,128)(2,1)S(1)} collective-permute-done((bf16[3,128,128]{2,1,0:T(8,128)(2,1)S(1)}, bf16[3,128,128]{2,1,0:T(8,128)(2,1)S(1)}, u32[]{:S(2)}, u32[]{:S(2)}) %collective-permute-start.1) | collective-permute-done | bytes 98336 | tf_op jit(solution)/shard_map/ppermute | solution.py:23
  71.1 0.0 copy-done
  71.1 1.1 shard_map.114
  72.2 23.7 %all_to_all.31.got_ref = bf16[8,3,32,1024]{3,2,1,0:T(8,128)(2,1)S(1)} all-to-all(bf16[8,3,32,1024]{3,2,1,0:T(8,128)(2,1)S(1)} %get-tuple-element.26), channel_id=1, replica_groups=mesh['xh'=2,'zh'=4,'zl'=4,'y'=4,'xl'=2,'core'=2] {'y','xh'}, dimensions={0} | all-to-all | bytes 3145728 | tf_op jit(solution)/shard_map/all_to_all | solution.py:245
  95.9 0.3 shard_map.115
  96.2 20.5 %all_to_all.32.got_ref = bf16[16,3,2,1024]{3,2,1,0:T(2,128)(2,1)S(1)} all-to-all(bf16[16,3,2,1024]{3,2,1,0:T(2,128)(2,1)S(1)} %shard_map.115), channel_id=1, replica_groups=mesh['xh'=2,'zh'=4,'zl'=4,'y'=4,'xl'=2,'core'=2] {'zl','zh'}, dimensions={0} | all-to-all | bytes 393216 | tf_op jit(solution)/shard_map/all_to_all | solution.py:252
  116.7 0.7 shard_map.116
  117.4 19.9 %all_to_all.33.along_z_ref = bf16[16,3,2,1024]{3,2,1,0:T(2,128)(2,1)S(1)} all-to-all(bf16[16,3,2,1024]{3,2,1,0:T(2,128)(2,1)S(1)} %get-tuple-element.28), channel_id=1, replica_groups=mesh['xh'=2,'zh'=4,'zl'=4,'y'=4,'xl'=2,'core'=2] {'zl','zh'}, dimensions={0} | all-to-all | bytes 393216 | tf_op jit(solution)/shard_map/all_to_all | solution.py:256
  137.3 0.2 shard_map.117
  137.5 21.6 %all_to_all.34.errors_ref = bf16[8,3,32,1024]{3,2,1,0:T(8,128)(2,1)S(1)} all-to-all(bf16[8,3,32,1024]{3,2,1,0:T(8,128)(2,1)S(1)} %shard_map.117), channel_id=1, replica_groups=mesh['xh'=2,'zh'=4,'zl'=4,'y'=4,'xl'=2,'core'=2] {'y','xh'}, dimensions={0} | all-to-all | bytes 3145728 | tf_op jit(solution)/shard_map/all_to_all | solution.py:55
  159.1 1.1 shard_map.118
  160.2 7.3 %collective-permute-start.2 = (f32[3,128,128]{2,1,0:T(8,128)S(1)}, f32[3,128,128]{2,1,0:T(8,128)S(1)}, u32[]{:S(2)}, u32[]{:S(2)}) collective-permute-start(f32[3,128,128]{2,1,0:T(8,128)S(1)} %shard_map.118), channel_id=1, source_target_pairs={{0,1},{1,0},{2,3},{3,2},{4,5},{5,4},{6,7},{7,6},{8,9},{9,8},{10,11... | collective-permute-start | bytes 589832 | tf_op jit(solution)/shard_map/ppermute | solution.py:23
  167.5 1.0 collective-permute-done.2
  168.6 2.2 %collective-permute-start.3 = (bf16[3,128,128]{2,1,0:T(8,128)(2,1)S(1)}, bf16[3,128,128]{2,1,0:T(8,128)(2,1)S(1)}, u32[]{:S(2)}, u32[]{:S(2)}) collective-permute-start(bf16[3,128,128]{2,1,0:T(8,128)(2,1)S(1)} %add_convert_fusion.mine_ref), channel_id=1, source_target_pairs={{0,2},{2,0},{1,3},{3,1},{4,6},{6,4},{5,7},{7,5},{8,10},{10,8},{9,1... | collective-permute-start | bytes 294920 | tf_op jit(solution)/shard_map/ppermute | solution.py:23
  170.8 1.8 %shard_map.119 = (bf16[6,128,1024]{2,1,0:T(8,128)(2,1)}, f32[3,1024]{1,0:T(4,128)}, bf16[3,1024,256]{2,1,0:T(8,128)(2,1)S(1)}) custom-call(bf16[3,256,128]{2,1,0:T(8,128)(2,1)S(1)} %get-tuple-element.30.act_ref, bf16[8,3,32,1024]{3,2,1,0:T(8,128)(2,1)S(1)} %all_to_all.34.errors_ref, bf16[8,3,32,1024]{3,2,1,0:T(8,128)(2,1)S(1)} %all_to_all.30.x_ref), custom_call_target="tpu_custom_call" | custom-call | flops 402653184 | bytes 6684672 | tf_op jit(solution)/shard_map/pallas_call | solution.py:191
  172.6 1.9 %collective-permute-done.3.theirs_ref = bf16[3,128,128]{2,1,0:T(8,128)(2,1)S(1)} collective-permute-done((bf16[3,128,128]{2,1,0:T(8,128)(2,1)S(1)}, bf16[3,128,128]{2,1,0:T(8,128)(2,1)S(1)}, u32[]{:S(2)}, u32[]{:S(2)}) %collective-permute-start.3) | collective-permute-done | bytes 98336 | tf_op jit(solution)/shard_map/ppermute | solution.py:23
  174.5 1.7 shard_map.120
  (12 shorter events, 0.1 us)
Async XLA Ops:
  0.6 0.7 copy-start.4
  2.0 28.9 %all-to-all-start = ((bf16[16,3,2,1024]{3,2,1,0:T(2,128)(2,1)}), bf16[16,3,2,1024]{3,2,1,0:T(2,128)(2,1)S(1)}, u32[]{:S(2)}, u32[]{:S(2)}) async-start(bf16[16,3,2,1024]{3,2,1,0:T(2,128)(2,1)} %shard_map.110), calls=%async_computation | async-start | bytes 393216 | tf_op jit(solution)/shard_map/all_to_all | solution.py:33
  31.2 24.9 %copy-start.1 = (bf16[3,1024,128]{2,1,0:T(8,128)(2,1)S(1)}, bf16[3,1024,128]{2,1,0:T(8,128)(2,1)}, u32[]{:S(2)}) copy-start(bf16[3,1024,128]{2,1,0:T(8,128)(2,1)} %weight_ref.3) | copy-start | bytes 2359300
  56.0 15.0 %copy-start = (bf16[6,128,1024]{2,1,0:T(8,128)(2,1)S(1)}, bf16[6,128,1024]{2,1,0:T(8,128)(2,1)}, u32[]{:S(2)}) copy-start(bf16[6,128,1024]{2,1,0:T(8,128)(2,1)} %weight_ref.5) | copy-start | bytes 4718596
  56.0 15.0 %copy-start.5 = (f32[3,128]{1,0:T(4,128)S(1)}, f32[3,128]{1,0:T(4,128)}, u32[]{:S(2)}) copy-start(f32[3,128]{1,0:T(4,128)} %bias_ref.2) | copy-start | bytes 4612
  56.7 8.5 %collective-permute-start = (f32[3,128,128]{2,1,0:T(8,128)S(1)}, f32[3,128,128]{2,1,0:T(8,128)S(1)}, u32[]{:S(2)}, u32[]{:S(2)}) collective-permute-start(f32[3,128,128]{2,1,0:T(8,128)S(1)} %shard_map.113), channel_id=1, source_target_pairs={{0,1},{1,0},{2,3},{3,2},{4,5},{5,4},{6,7},{7,6},{8,9},{9,8},{10,11... | collective-permute-start | bytes 589832 | tf_op jit(solution)/shard_map/ppermute | solution.py:23
  65.2 5.9 %collective-permute-start.1 = (bf16[3,128,128]{2,1,0:T(8,128)(2,1)S(1)}, bf16[3,128,128]{2,1,0:T(8,128)(2,1)S(1)}, u32[]{:S(2)}, u32[]{:S(2)}) collective-permute-start(bf16[3,128,128]{2,1,0:T(8,128)(2,1)S(1)} %add_convert_fusion.1.mine_ref), channel_id=1, source_target_pairs={{0,2},{2,0},{1,3},{3,1},{4,6},{6,4},{5,7},{7,5},{8,10},{10,8},{9,1... | collective-permute-start | bytes 294920 | tf_op jit(solution)/shard_map/ppermute | solution.py:23
  95.9 20.8 %copy-start.2 = (f32[3,1024]{1,0:T(4,128)S(1)}, f32[3,1024]{1,0:T(4,128)}, u32[]{:S(2)}) copy-start(f32[3,1024]{1,0:T(4,128)} %bias_ref.3) | copy-start | bytes 36868
  95.9 20.8 %copy-start.3 = (bf16[3,2,1024]{2,1,0:T(2,128)(2,1)S(1)}, bf16[3,2,1024]{2,1,0:T(2,128)(2,1)}, u32[]{:S(2)}) copy-start(bf16[3,2,1024]{2,1,0:T(2,128)(2,1)} %targets_ref.1) | copy-start | bytes 36868
  160.2 8.4 %collective-permute-start.2 = (f32[3,128,128]{2,1,0:T(8,128)S(1)}, f32[3,128,128]{2,1,0:T(8,128)S(1)}, u32[]{:S(2)}, u32[]{:S(2)}) collective-permute-start(f32[3,128,128]{2,1,0:T(8,128)S(1)} %shard_map.118), channel_id=1, source_target_pairs={{0,1},{1,0},{2,3},{3,2},{4,5},{5,4},{6,7},{7,6},{8,9},{9,8},{10,11... | collective-permute-start | bytes 589832 | tf_op jit(solution)/shard_map/ppermute | solution.py:23
  168.6 5.9 %collective-permute-start.3 = (bf16[3,128,128]{2,1,0:T(8,128)(2,1)S(1)}, bf16[3,128,128]{2,1,0:T(8,128)(2,1)S(1)}, u32[]{:S(2)}, u32[]{:S(2)}) collective-permute-start(bf16[3,128,128]{2,1,0:T(8,128)(2,1)S(1)} %add_convert_fusion.mine_ref), channel_id=1, source_target_pairs={{0,2},{2,0},{1,3},{3,1},{4,6},{6,4},{5,7},{7,5},{8,10},{10,8},{9,1... | collective-permute-start | bytes 294920 | tf_op jit(solution)/shard_map/ppermute | solution.py:23
